TPU v7x, 32 devices: a whole 2x2x4 slice. The times are simulated.
32 devices in a mesh: dp: 8 (over z, y), ctx: 4 (over x, core).
Axes of the slice: x: 2, y: 2, z: 4, core: 2. Of those that a mesh axis runs over, the one named last changes fastest.
Arguments:
- block_in: bfloat16 [16, 1024, 1024], P('dp', 'ctx'), may hold values from -6 to 6
- out_grad: bfloat16 [16, 1024, 1024], P('dp', 'ctx'), may hold values from -6 to 6
- w_in: float32 [1024, 4384], P(('dp', 'ctx')), may hold values from -0.1875 to 0.1875
- w_in_m: float32 [1024, 4384], P(('dp', 'ctx')), may hold values from -28 to 28
- w_in_v: float32 [1024, 4384], P(('dp', 'ctx')), may hold values from 1.47456 to 5.89824
- w_out: float32 [2048, 1024], P(('dp', 'ctx')), may hold values from -0.125 to 0.125
- w_out_m: float32 [2048, 1024], P(('dp', 'ctx')), may hold values from -80 to 80
- w_out_v: float32 [2048, 1024], P(('dp', 'ctx')), may hold values from 16.384 to 65.536
- small_params: float32 [14688], replicated, may hold values from -8 to 8
- small_m: float32 [14688], replicated, may hold values from -24 to 24
- small_v: float32 [14688], replicated, may hold values from 1.6384 to 6.5536
Outputs:
- block_out: bfloat16 [16, 1024, 1024], P('dp', 'ctx')
- input_grad: bfloat16 [16, 1024, 1024], P('dp', 'ctx')
- grad_w_in: float32 [1024, 4384], P(('dp', 'ctx'))
- w_in_v_new: float32 [1024, 4384], P(('dp', 'ctx'))
- w_in_new: float32 [1024, 4384], P(('dp', 'ctx'))
- grad_w_out: float32 [2048, 1024], P(('dp', 'ctx'))
- w_out_v_new: float32 [2048, 1024], P(('dp', 'ctx'))
- w_out_new: float32 [2048, 1024], P(('dp', 'ctx'))
- grad_small: float32 [14688], replicated
- small_v_new: float32 [14688], replicated
- small_new: float32 [14688], replicated
All inputs are finite; a program needn't handle non-finite values.
Results may differ from a plain program's by a relative error of at most 0.0078.
Values may be sent and summed in bfloat16 or wider, within the bound.
No kernel may reach another device: no remote copies, remote signals or barrier semaphores. Data moves between devices by JAX's collectives and lax.ppermute only.
A program may use at most 192 MiB of HBM per device.

v0:
```python
import jax
import jax.numpy as jnp
from jax import lax
from jax.sharding import PartitionSpec as P

D = 1024
HEADS = 32
HD = 64
NS = 128
KCONV = 4
MICRO = 2
STEP = 10
SEQS = 1
DI = 2048


NORM_EPS = 1e-05
ADAM_EPS = 1e-08
BETA_ONE = 0.9
BETA_TWO = 0.999
RATE_BIG = 0.03
RATE_SMALL = 0.3
DECAY_WEIGHT = 0.01
PRECISE = lax.Precision.HIGHEST


def from_behind(value, axis, steps):
    count = lax.axis_size(axis)
    leading, last = (max(0, -steps), min(count, count - steps))
    return lax.ppermute(value, axis, [(source, source + steps) for source in range(leading, last)])


def carried_in(value, axis, combine, identity):
    peers, mine = (lax.axis_size(axis), lax.axis_index(axis))
    everything = jax.tree.map(
        lambda part, kind: lax.all_gather(part.astype(kind), axis),
        value,
        (jnp.bfloat16, jnp.bfloat16),
    )
    start = jax.tree.map(
        lambda part, zero: jnp.broadcast_to(jnp.asarray(zero, part.dtype), part.shape),
        value,
        identity,
    )

    def hop(k, before):
        reached = k < mine
        new = combine(
            before, jax.tree.map(lambda part, own: part[k].astype(own.dtype), everything, value)
        )
        return jax.tree.map(lambda a, b: jnp.where(reached, a, b), new, before)

    return lax.fori_loop(0, peers, hop, start)


def carried_in_2(value, axis, join, neutral):
    count = lax.axis_size(axis)
    place = lax.axis_index(axis)
    ahead = count - 1 - place
    gathered = jax.tree.map(
        lambda a, kind: lax.all_gather(a.astype(kind), axis),
        value,
        jax.tree.map(lambda a: jnp.bfloat16 if a.dtype == jnp.float32 else a.dtype, value),
    )
    state = jax.tree.map(lambda a, e: jnp.zeros_like(a) + jnp.asarray(e, a.dtype), value, neutral)

    def one(hop, state):
        source = count - 1 - hop
        return join(
            state,
            jax.tree.map(
                lambda a, own: lax.dynamic_index_in_dim(a, source, 0, False).astype(own.dtype),
                gathered,
                value,
            ),
        )

    return lax.fori_loop(0, ahead, one, state)


def split_small(packed):
    channels = DI + 2 * NS
    pieces = []
    offset = 0
    for amount in (D, DI, KCONV * channels, channels, HEADS, HEADS, HEADS):
        pieces.append(packed[offset : offset + amount])
        offset = offset + amount
    return (
        pieces[0],
        pieces[1],
        pieces[2].reshape(KCONV, channels),
        pieces[3],
        pieces[4],
        pieces[5],
        pieces[6],
    )


def rms_scale(values, scale_gain):
    return (
        values
        * lax.rsqrt(jnp.mean(values * values, axis=-1, keepdims=True) + NORM_EPS)
        * scale_gain
    )


def prepare(projected, prev_rim, conv_taps, conv_bias, dt_bias, a_log):
    channels = DI + 2 * NS
    batch_rows, span_rows = (projected.shape[0], projected.shape[1])
    conv_in = projected[:, :, DI : DI + channels]
    padded = jnp.concatenate([prev_rim, conv_in], axis=1)
    conv_out = conv_bias + sum(
        (
            conv_taps[tap_index] * padded[:, tap_index : tap_index + span_rows]
            for tap_index in range(KCONV)
        )
    )
    active = jax.nn.silu(conv_out)
    values = active[:, :, :DI].reshape(batch_rows, span_rows, HEADS, HD)
    in_b = active[:, :, DI : DI + NS]
    out_c = active[:, :, DI + NS :]
    step_size = jax.nn.softplus(projected[:, :, DI + channels :] + dt_bias)
    cumulative = jnp.cumsum(-jnp.exp(a_log) * step_size, axis=1)
    return (values, in_b, out_c, step_size, cumulative)


def group_state(prepared):
    values, in_b, out_c, step_size, cumulative = prepared
    totals = cumulative[:, -1, :]
    weights = jnp.exp(totals[:, None, :] - cumulative) * step_size
    states = jnp.einsum("bqh,bqn,bqhp->bhpn", weights, in_b, values, precision=PRECISE)
    return (states, totals)


def mix_out(prepared, incoming, projected, skip_gain, gate_gain):
    values, in_b, out_c, step_size, cumulative = prepared
    batch_rows, span_rows = (values.shape[0], values.shape[1])
    by_head = jnp.swapaxes(cumulative, 1, 2)
    differ = by_head[:, :, :, None] - by_head[:, :, None, :]
    causal = jnp.arange(span_rows)[:, None] >= jnp.arange(span_rows)[None, :]
    decays = jnp.exp(jnp.where(causal, differ, -1e30))
    scores = jnp.einsum("btn,bun->btu", out_c, in_b, precision=PRECISE)
    mixing = decays * scores[:, None] * jnp.swapaxes(step_size, 1, 2)[:, :, None, :]
    inner_part = jnp.einsum("bhtu,buhp->bthp", mixing, values, precision=PRECISE)
    outer_part = jnp.einsum(
        "btn,bth,bhpn->bthp", out_c, jnp.exp(cumulative), incoming, precision=PRECISE
    )
    mixed = inner_part + outer_part + skip_gain[:, None] * values
    gated = mixed.reshape(batch_rows, span_rows, DI) * jax.nn.silu(projected[:, :, :DI])
    return rms_scale(gated, gate_gain)


def chain_join(earlier, latter):
    return (earlier[0] + latter[0], jnp.exp(latter[0])[:, :, None, None] * earlier[1] + latter[1])


def adam_step(weight, first_old, second_old, gradient, step_rate):
    first_new = BETA_ONE * first_old + (1.0 - BETA_ONE) * gradient
    second_new = BETA_TWO * second_old + (1.0 - BETA_TWO) * gradient * gradient
    first_hat = first_new / (1.0 - BETA_ONE**STEP)
    second_hat = second_new / (1.0 - BETA_TWO**STEP)
    weight_new = weight - step_rate * (
        first_hat / (jnp.sqrt(second_hat) + ADAM_EPS) + DECAY_WEIGHT * weight
    )
    return (second_new, weight_new)


def shards(
    block_in,
    out_grad,
    w_in,
    w_in_m,
    w_in_v,
    w_out,
    w_out_m,
    w_out_v,
    small_params,
    small_m,
    small_v,
):
    norm_gain, gate_gain, conv_taps, conv_bias, dt_bias, a_log, skip_gain = split_small(
        small_params
    )
    channels = DI + 2 * NS
    rim_rows = KCONV - 1
    grad_in = jnp.zeros((w_in.shape[1] * 0 + D, w_in.shape[1]), jnp.float32)
    grad_out = jnp.zeros((DI, D), jnp.float32)
    grad_small = jnp.zeros(small_params.shape, jnp.float32)
    outputs = []
    input_grads = []
    for micro_index in range(MICRO):
        lower_row = micro_index * SEQS
        tokens = block_in[lower_row : lower_row + SEQS].astype(jnp.float32)
        fwd_in, fwd_out = (
            lax.all_gather(w_in.astype(jnp.bfloat16), ("dp", "ctx"), axis=0, tiled=True),
            lax.all_gather(w_out.astype(jnp.bfloat16), ("dp", "ctx"), axis=0, tiled=True),
        )
        normed, norm_back = jax.vjp(rms_scale, tokens, norm_gain)
        normed_low = normed.astype(jnp.bfloat16)
        projected = jnp.einsum(
            "sqd,dk->sqk", normed_low, fwd_in, preferred_element_type=jnp.float32
        )
        rim_out = projected[:, -rim_rows:, DI : DI + channels]
        prev_rim = from_behind(rim_out, "ctx", 1)
        prepared, prep_back = jax.vjp(
            prepare, projected, prev_rim, conv_taps, conv_bias, dt_bias, a_log
        )
        (states, totals), state_back = jax.vjp(group_state, prepared)
        _, incoming = carried_in(
            (totals, states), "ctx", chain_join, (jnp.zeros_like(totals), jnp.zeros_like(states))
        )
        normed_out, mix_back = jax.vjp(mix_out, prepared, incoming, projected, skip_gain, gate_gain)
        out_low = normed_out.astype(jnp.bfloat16)
        branch = jnp.einsum("sqi,id->sqd", out_low, fwd_out, preferred_element_type=jnp.float32)
        outputs.append((tokens + branch).astype(jnp.bfloat16))
        bwd_in, bwd_out = (
            lax.all_gather(w_in.astype(jnp.bfloat16), ("dp", "ctx"), axis=0, tiled=True),
            lax.all_gather(w_out.astype(jnp.bfloat16), ("dp", "ctx"), axis=0, tiled=True),
        )
        upstream = out_grad[lower_row : lower_row + SEQS]
        grad_out = grad_out + jnp.einsum(
            "sqi,sqd->id", out_low, upstream, preferred_element_type=jnp.float32
        )
        d_normed_out = jnp.einsum(
            "sqd,id->sqi", upstream, bwd_out, preferred_element_type=jnp.float32
        )
        d_prep_mix, d_incoming, d_proj_mix, d_skip, d_gate_gain = mix_back(d_normed_out)
        _, carried = carried_in_2(
            (totals, d_incoming),
            "ctx",
            chain_join,
            (jnp.zeros_like(totals), jnp.zeros_like(d_incoming)),
        )
        d_totals = jnp.exp(totals) * jnp.sum(carried * incoming, axis=(2, 3))
        (d_prep_state,) = state_back((carried, d_totals))
        d_prepared = jax.tree.map(jnp.add, d_prep_mix, d_prep_state)
        d_proj_prep, d_prev_rim, d_taps, d_conv_bias, d_dt_bias, d_a_log = prep_back(d_prepared)
        rim_grad = from_behind(d_prev_rim, "ctx", -1)
        d_projected = d_proj_prep + d_proj_mix
        d_projected = d_projected.at[:, -rim_rows:, DI : DI + channels].add(rim_grad)
        d_proj_low = d_projected.astype(jnp.bfloat16)
        grad_in = grad_in + jnp.einsum(
            "sqd,sqk->dk", normed_low, d_proj_low, preferred_element_type=jnp.float32
        )
        d_normed = jnp.einsum("sqk,dk->sqd", d_proj_low, bwd_in, preferred_element_type=jnp.float32)
        d_tokens, d_norm_gain = norm_back(d_normed)
        input_grads.append((upstream.astype(jnp.float32) + d_tokens).astype(jnp.bfloat16))
        grad_small = grad_small + jnp.concatenate(
            [d_norm_gain, d_gate_gain, d_taps.reshape(-1), d_conv_bias, d_dt_bias, d_a_log, d_skip]
        )
    grad_in_shard, grad_out_shard = (
        lax.psum_scatter(grad_in, ("dp", "ctx"), scatter_dimension=0, tiled=True),
        lax.psum_scatter(grad_out, ("dp", "ctx"), scatter_dimension=0, tiled=True),
    )
    grad_small_all = lax.psum(grad_small, ("dp", "ctx"))
    in_second, in_new = adam_step(w_in, w_in_m, w_in_v, grad_in_shard, RATE_BIG)
    out_second, out_new = adam_step(w_out, w_out_m, w_out_v, grad_out_shard, RATE_BIG)
    small_second, small_updated = adam_step(
        small_params, small_m, small_v, grad_small_all, RATE_SMALL
    )
    return (
        jnp.concatenate(outputs, axis=0),
        jnp.concatenate(input_grads, axis=0),
        grad_in_shard,
        in_second,
        in_new,
        grad_out_shard,
        out_second,
        out_new,
        grad_small_all,
        small_second,
        small_updated,
    )


def solution(mesh):
    return jax.shard_map(
        shards,
        mesh=mesh,
        in_specs=(
            P("dp", "ctx", None),
            P("dp", "ctx", None),
            P(("dp", "ctx"), None),
            P(("dp", "ctx"), None),
            P(("dp", "ctx"), None),
            P(("dp", "ctx"), None),
            P(("dp", "ctx"), None),
            P(("dp", "ctx"), None),
            P(),
            P(),
            P(),
        ),
        out_specs=(
            P("dp", "ctx", None),
            P("dp", "ctx", None),
            P(("dp", "ctx"), None),
            P(("dp", "ctx"), None),
            P(("dp", "ctx"), None),
            P(("dp", "ctx"), None),
            P(("dp", "ctx"), None),
            P(("dp", "ctx"), None),
            P(),
            P(),
            P(),
        ),
        check_vma=False,
    )
```

profile of v0, /device:TPU:5, one launch (start us, length us, event | category | flops | bytes accessed | tf_op | source)
XLA Modules:
  0.0 869.7 jit_solution(5171531440002477190)
XLA Ops:
  14.8 78.9 %all-gather.11.cloned.1.call-done = bf16[1024,4384]{1,0:T(8,128)(2,1)} async-done(((bf16[32,4384]{1,0:T(8,128)(2,1)}), bf16[1024,4384]{1,0:T(8,128)(2,1)}) %all-gather.11.cloned.1.call-update) | async-done | bytes 8978448 | tf_op jit(solution)/shard_map/all_gather | solution.py:195
  93.8 6.4 convolution_bitcast_fusion
  120.3 7.4 fusion.51
  148.5 5.2 all_gather.49
  167.0 5.4 while.60
  175.4 10.8 %fusion.66 = f32[1,256,32,64]{1,3,2,0:T(8,128)} fusion(f32[32,64,256]{2,1,0:T(8,128)S(1)} %fusion.171, f32[1,256,32,64]{1,3,2,0:T(8,128)S(1)} %bitcast.594, f32[256,32,64]{0,2,1:T(8,128)S(1)} %bitcast.593, f32[32,256]{1,0:T(8,128)S(1)} %copy.315, f32[256,256]{1,0:T(8,128)S(1)} %fusion.228, f32[32,256]{1,0:T(8,128)S(1)} %bitcast_add_fusion.13, ...), kind=kOutput, calls=%fused_computation.114 | convolution fusion | flops 1621098496 | bytes 8814720 | tf_op jit(solution)/shard_map/jvp(bhtu,buhp->bthp)/dot_general | solution.py:144
  189.1 5.3 while.61
  197.4 10.8 %fusion.65 = f32[1,256,32,64]{1,3,2,0:T(8,128)} fusion(f32[32,64,256]{2,1,0:T(8,128)S(1)} %fusion.168, f32[1,256,32,64]{1,3,2,0:T(8,128)S(1)} %bitcast.585, f32[256,32,64]{0,2,1:T(8,128)S(1)} %bitcast.584, f32[32,256]{1,0:T(8,128)S(1)} %copy.329, f32[256,256]{1,0:T(8,128)S(1)} %fusion.219, f32[32,256]{1,0:T(8,128)S(1)} %bitcast_add_fusion.12, ...), kind=kOutput, calls=%fused_computation.112 | convolution fusion | flops 1621098496 | bytes 8814720 | tf_op jit(solution)/shard_map/jvp(bhtu,buhp->bthp)/dot_general | solution.py:144
  224.0 132.9 %reduce-scatter.5.cloned.1.call-done = f32[64,1024]{1,0:T(8,128)} async-done(((f32[2048,1024]{1,0:T(8,128)}), f32[64,1024]{1,0:T(8,128)}) %reduce-scatter.5.cloned.1.call-update) | async-done | bytes 262160 | tf_op jit(solution)/shard_map/reduce_scatter | solution.py:253
  359.3 73.4 %all-gather.13.cloned.1.call-done = bf16[2048,1024]{1,0:T(8,128)(2,1)} async-done(((bf16[64,1024]{1,0:T(8,128)(2,1)}), bf16[2048,1024]{1,0:T(8,128)(2,1)}) %all-gather.13.cloned.1.call-update) | async-done | bytes 4194320 | tf_op jit(solution)/shard_map/all_gather | solution.py:196
  441.5 7.0 multiply_reduce_fusion.13
  465.4 11.3 %fusion.285 = f32[32,256,256]{2,1,0:T(8,128)} fusion(f32[32,64,256]{2,1,0:T(8,128)} %bitcast.577, f32[256,32,64]{0,2,1:T(8,128)} %bitcast.583), kind=kOutput, calls=%fused_computation.412 | convolution fusion | flops 1610612736 | bytes 12582912 | tf_op jit(solution)/shard_map/transpose(jvp(bhtu,buhp->bthp))/dot_general | solution.py:144
  476.9 18.9 %fusion.15 = (f32[32,256]{1,0:T(8,128)}, f32[32,256]{1,0:T(8,128)}, f32[32,256]{1,0:T(8,128)S(1)}, f32[256,256]{1,0:T(8,128)S(1)}, f32[256,256]{1,0:T(8,128)S(1)...) fusion(f32[32,256]{1,0:T(8,128)S(1)} %copy-done.117, f32[256,256]{1,0:T(8,128)S(1)} %copy-done.83, ...), kind=kOutput, calls=%fused_computation.30 | convolution fusion | flops 1664958464 | bytes 14024704 | tf_op jit(solution)/shard_map/transpose(jvp(bhtu,buhp->bthp))/dot_general | solution.py:144
  550.9 10.6 %fusion.63 = f32[1,256,32,64]{1,3,2,0:T(8,128)} fusion(f32[32,64,256]{2,1,0:T(8,128)} %get-tuple-element.735, f32[1,256,32,64]{1,3,2,0:T(8,128)} %bitcast.578, f32[32,64,256]{2,1,0:T(8,128)} %bitcast.579, f32[32,256]{1,0:T(8,128)} %copy-done.119, f32[256,256]{1,0:T(8,128)} %copy-done.85, f32[32,256]{1,0:T(8,128)} %copy-done.121, ...), kind=kOutput, calls=%fused_computation.108 | convolution fusion | flops 1621098496 | bytes 8814720 | tf_op jit(solution)/shard_map/transpose(jvp(bhtu,buhp->bthp))/dot_general | solution.py:144
  564.5 11.0 %fusion.64 = f32[1,256,32,64]{1,3,2,0:T(8,128)} fusion(f32[32,64,256]{2,1,0:T(8,128)} %get-tuple-element.733, f32[1,256,32,64]{1,3,2,0:T(8,128)} %bitcast.600, f32[32,64,256]{2,1,0:T(8,128)} %bitcast.599, f32[32,256]{1,0:T(8,128)S(1)} %copy-done.118, f32[256,256]{1,0:T(8,128)S(1)} %copy-done.84, f32[32,256]{1,0:T(8,128)S(1)} %copy-done.125, ...), kind=kOutput, calls=%fused_computation.110 | convolution fusion | flops 1621098496 | bytes 8814720 | tf_op jit(solution)/shard_map/transpose(jvp(bhtu,buhp->bthp))/dot_general | solution.py:144
  588.1 7.9 multiply_reduce_fusion.10
  600.3 6.9 broadcast_multiply_fusion
  617.6 6.1 collective-permute-start.3
  637.4 10.3 %fusion.55 = f32[1024,4384]{1,0:T(8,128)} fusion(f32[1,256,4384]{2,1,0:T(8,128)} %scatter-add.6, f32[1024]{0:T(1024)S(1)} %copy-done.51, f32[256]{0:T(256)S(1)} %copy-done.102, bf16[2,256,1024]{2,1,0:T(8,128)(2,1)S(1)} %copy-done.30), kind=kOutput, calls=%fused_computation.99 | convolution fusion | flops 2300649472 | bytes 22975488 | tf_op jit(solution)/shard_map/sqd,sqk->dk/dot_general | solution.py:242
  647.7 11.5 %convolution_add_fusion = f32[1024,4384]{1,0:T(8,128)} fusion(f32[1024,4384]{1,0:T(8,128)} %fusion.55, f32[1,256,4384]{2,1,0:T(8,128)S(1)} %copy-done.35, f32[256]{0:T(256)S(1)} %copy-done.115, f32[1024]{0:T(1024)S(1)} %copy-done.51, bf16[2,256,1024]{2,1,0:T(8,128)(2,1)S(1)} %copy-done.30), kind=kOutput, calls=%fused_computation.10 | convolution fusion | flops 2305138688 | bytes 41030656 | tf_op jit(solution)/shard_map/sqd,sqk->dk/dot_general | solution.py:242
  668.0 6.9 fusion.53
  675.0 8.0 fusion.150
  683.2 43.5 %psum.7 = f32[14688]{0:T(1024)S(1)} all-reduce(f32[14688]{0:T(1024)S(1)} %add.453), channel_id=1, replica_groups=mesh['dp'=8,'ctx'=4] {'dp','ctx'}, use_global_device_ids=true, to_apply=%region_60.62 | all-reduce | flops 14688 | bytes 117504 | tf_op jit(solution)/shard_map/psum | solution.py:255
  730.7 129.3 %reduce-scatter.3.cloned.1.call-done = f32[32,4384]{1,0:T(8,128)} async-done(((f32[1024,4384]{1,0:T(8,128)}), f32[32,4384]{1,0:T(8,128)}) %reduce-scatter.3.cloned.1.call-update) | async-done | bytes 561168 | tf_op jit(solution)/shard_map/reduce_scatter | solution.py:252
  (561 shorter events, 245.3 us)
Async XLA Ops:
  7.2 86.6 %copy-start.29 = (bf16[2,256,1024]{2,1,0:T(8,128)(2,1)S(1)}, bf16[2,256,1024]{2,1,0:T(8,128)(2,1)}, u32[]{:S(2)}) copy-start(bf16[2,256,1024]{2,1,0:T(8,128)(2,1)} %param.24) | copy-start | bytes 3145732
  7.2 86.5 %all-gather.11.cloned.1.call-start = ((), (), s32[]{:S(2)}) async-start(), calls=%async_computation.2 | async-start | bytes 9461760 | tf_op jit(solution)/shard_map/all_gather | solution.py:195
  9.1 157.8 %all-gather.15.cloned.1.call-start = ((), (), s32[]{:S(2)}) async-start(), calls=%async_computation.6 | async-start | bytes 2621440 | tf_op jit(solution)/shard_map/all_gather | solution.py:36
  9.9 90.3 %copy-start.50 = (f32[1024]{0:T(1024)}, f32[1024]{0:T(1024)S(1)}, u32[]{:S(2)}) copy-start(f32[1024]{0:T(1024)S(1)} %slice.206) | copy-start | bytes 12292
  11.9 88.3 %copy-start.101 = (f32[256]{0:T(256)}, f32[256]{0:T(256)S(1)}, u32[]{:S(2)}) copy-start(f32[256]{0:T(256)S(1)} %fusion.255) | copy-start | bytes 3076
  13.4 89.6 %copy-start.150 = (f32[32]{0:T(128)}, f32[32]{0:T(128)S(1)}, u32[]{:S(2)}) copy-start(f32[32]{0:T(128)S(1)} %get-tuple-element.712) | copy-start | bytes 388
  13.4 99.7 %copy-start.133 = (f32[32]{0:T(128)}, f32[32]{0:T(128)S(1)}, u32[]{:S(2)}) copy-start(f32[32]{0:T(128)S(1)} %get-tuple-element.711) | copy-start | bytes 388
  14.8 104.9 %copy-start.88 = (f32[2304]{0:T(1024)}, f32[2304]{0:T(1024)S(1)}, u32[]{:S(2)}) copy-start(f32[2304]{0:T(1024)S(1)} %get-tuple-element.714) | copy-start | bytes 27652
  107.1 12.6 %collective-permute-start.1 = (f32[1,3,2304]{2,0,1:T(1,128)S(1)}, f32[1,3,2304]{2,0,1:T(1,128)S(1)}, u32[]{:S(2)}, u32[]{:S(2)}) collective-permute-start(f32[1,3,2304]{2,0,1:T(1,128)S(1)} %copy.323), channel_id=1, source_target_pairs={{0,1},{1,2},{2,3},{4,5},{5,6},{6,7},{8,9},{9,10},{10,11},{12,13},{... | collective-permute-start | bytes 82952 | tf_op jit(solution)/shard_map/ppermute | solution.py:30
  109.4 10.3 %collective-permute-start = (f32[1,3,2304]{2,0,1:T(1,128)S(1)}, f32[1,3,2304]{2,0,1:T(1,128)S(1)}, u32[]{:S(2)}, u32[]{:S(2)}) collective-permute-start(f32[1,3,2304]{2,0,1:T(1,128)S(1)} %copy.309), channel_id=1, source_target_pairs={{0,1},{1,2},{2,3},{4,5},{5,6},{6,7},{8,9},{9,10},{10,11},{12,13},{... | collective-permute-start | bytes 82952 | tf_op jit(solution)/shard_map/ppermute | solution.py:30
  136.7 52.4 %all-gather.17.cloned.1.call-start = ((), (), s32[]{:S(2)}) async-start(), calls=%async_computation.7 | async-start | bytes 2621440 | tf_op jit(solution)/shard_map/all_gather | solution.py:36
  141.4 320.3 %copy-start.80 = (f32[256,32]{0,1:T(8,128)}, f32[256,32]{0,1:T(8,128)S(1)}, u32[]{:S(2)}) copy-start(f32[256,32]{0,1:T(8,128)S(1)} %copy.317) | copy-start | bytes 98308
  164.0 192.9 %reduce-scatter.5.cloned.1.call-start = ((), (), s32[]{:S(2)}) async-start(), calls=%async_computation.5 | async-start | bytes 8650752 | tf_op jit(solution)/shard_map/reduce_scatter | solution.py:253
  214.6 226.8 %copy-start.136 = (f32[256]{0:T(256)}, f32[256]{0:T(256)S(1)}, u32[]{:S(2)}) copy-start(f32[256]{0:T(256)S(1)} %fusion.258) | copy-start | bytes 3076
  217.7 223.8 %copy-start.131 = (f32[256]{0:T(256)}, f32[256]{0:T(256)S(1)}, u32[]{:S(2)}) copy-start(f32[256]{0:T(256)S(1)} %fusion.256) | copy-start | bytes 3076
  223.9 208.8 %all-gather.13.cloned.1.call-start = ((), (), s32[]{:S(2)}) async-start(), calls=%async_computation.3 | async-start | bytes 4325376 | tf_op jit(solution)/shard_map/all_gather | solution.py:196
  359.2 159.9 %all-gather.21.cloned.1.call-start = ((), (), s32[]{:S(2)}) async-start(), calls=%async_computation.9 | async-start | bytes 2621440 | tf_op jit(solution)/shard_map/all_gather | solution.py:61
  455.6 73.9 %all-gather.19.cloned.1.call-start = ((), (), s32[]{:S(2)}) async-start(), calls=%async_computation.8 | async-start | bytes 2621440 | tf_op jit(solution)/shard_map/all_gather | solution.py:61
  476.8 383.2 %reduce-scatter.3.cloned.1.call-start = ((), (), s32[]{:S(2)}) async-start(), calls=%async_computation.4 | async-start | bytes 18923520 | tf_op jit(solution)/shard_map/reduce_scatter | solution.py:252
  617.6 15.0 %collective-permute-start.3 = (f32[1,3,2304]{2,0,1:T(1,128)S(1)}, f32[1,3,2304]{2,0,1:T(1,128)S(1)}, u32[]{:S(2)}, u32[]{:S(2)}) collective-permute-start(f32[1,3,2304]{2,0,1:T(1,128)S(1)} %copy.360), channel_id=1, source_target_pairs={{1,0},{2,1},{3,2},{5,4},{6,5},{7,6},{9,8},{10,9},{11,10},{13,12},{... | collective-permute-start | bytes 82952 | tf_op jit(solution)/shard_map/ppermute | solution.py:30
  624.0 10.7 %collective-permute-start.2 = (f32[1,3,2304]{2,0,1:T(1,128)S(1)}, f32[1,3,2304]{2,0,1:T(1,128)S(1)}, u32[]{:S(2)}, u32[]{:S(2)}) collective-permute-start(f32[1,3,2304]{2,0,1:T(1,128)S(1)} %copy.347), channel_id=1, source_target_pairs={{1,0},{2,1},{3,2},{5,4},{6,5},{7,6},{9,8},{10,9},{11,10},{13,12},{... | collective-permute-start | bytes 82952 | tf_op jit(solution)/shard_map/ppermute | solution.py:30
  728.9 131.1 %copy-start.49 = (f32[32,4384]{1,0:T(8,128)S(1)}, f32[32,4384]{1,0:T(8,128)}, u32[]{:S(2)}) copy-start(f32[32,4384]{1,0:T(8,128)} %param.26) | copy-start | bytes 1683460
  729.0 131.1 %copy-start.53 = (f32[32,4384]{1,0:T(8,128)S(1)}, f32[32,4384]{1,0:T(8,128)}, u32[]{:S(2)}) copy-start(f32[32,4384]{1,0:T(8,128)} %param.27) | copy-start | bytes 1683460
  729.0 131.1 %copy-start.54 = (f32[32,4384]{1,0:T(8,128)S(1)}, f32[32,4384]{1,0:T(8,128)}, u32[]{:S(2)}) copy-start(f32[32,4384]{1,0:T(8,128)} %param.28) | copy-start | bytes 1683460
  (156 other events, 1427.7 us)
Sparse Core Ops, SparseCore 0:
  11.5 82.2 all-gather.10
  136.8 21.2 all-gather.14
  164.2 21.1 all-gather.16
  224.1 132.8 reduce-scatter.4
  360.2 72.4 all-gather.12
  455.7 21.0 all-gather.20
  479.0 22.5 all-gather.18
  659.4 200.5 reduce-scatter.2
where the time goes:
time: 881 us; the launch traced here: 870 us
  waiting for transfers between devices  415 us (47%)
  matrix products  199 us (23%)
  other arithmetic  103 us (12%)
  local copies, waits for them, and re-layouts  69.5 us (8%)
  blocking collectives  53.8 us (6%)
  between operations  16.8 us (2%)
  starting transfers between devices  12.9 us (1%)
    reduce_scatter x1, waiting for transfers between devices, shards(): lax.psum_scatter(grad_out, ('dp', 'ctx'), scatter_dimension=0, tiled=True)  133 us
    reduce_scatter x1, waiting for transfers between devices, shards(): lax.psum_scatter(grad_in, ('dp', 'ctx'), scatter_dimension=0, tiled=True)  129 us
    all_gather x1, waiting for transfers between devices, shards(): lax.all_gather(w_in.astype(jnp.bfloat16), ('dp', 'ctx'), axis=0, tiled=True)  78.9 us
    all_gather x1, waiting for transfers between devices, shards(): lax.all_gather(w_out.astype(jnp.bfloat16), ('dp', 'ctx'), axis=0, tiled=T...  73.4 us
    dot_general x6, matrix products, mix_out(): jnp.einsum('bhtu,buhp->bthp', mixing, values, precision=PRECISE)  73.4 us
    psum x1, blocking collectives, shards(): grad_small_all = lax.psum(grad_small, ('dp', 'ctx'))  43.5 us
    dot_general x6, matrix products, group_state(): jnp.einsum('bqh,bqn,bqhp->bhpn', weights, in_b, values, precision=PRECISE)  26.5 us
    dot_general x6, matrix products, mix_out(): jnp.einsum('btn,bth,bhpn->bthp', out_c, jnp.exp(cumulative), incoming, pr...  21.9 us
  transfers between devices with their start and end apart: 12, of which 4 were waited for; matrix products, arithmetic and copies ran while one was open for 18% of the time, Pallas kernels for 0%

commit v1 on v0

v1 whole, which is shorter than its diff:
```python
import functools

import jax
import jax.numpy as jnp
from jax import lax
from jax.experimental import pallas as pl
from jax.experimental.pallas import tpu as pltpu
from jax.sharding import PartitionSpec as P

D = 1024
HEADS = 32
HD = 64
NS = 128
KCONV = 4
STEP = 10
DI = 2048
CHANNELS = DI + 2 * NS

CHUNK = 128
LANES = 128
RIM = 8
ROWS = 256

NORM_EPS = 1e-05
ADAM_EPS = 1e-08
BETA_ONE = 0.9
BETA_TWO = 0.999
RATE_BIG = 0.03
RATE_SMALL = 0.3
DECAY_WEIGHT = 0.01

F32 = jnp.float32
BF16 = jnp.bfloat16
VMEM_BYTES = 48 * 1024 * 1024


def dot(a, b, contract=((1,), (0,))):
    return lax.dot_general(a, b, (contract, ((), ())), preferred_element_type=F32)


def terms(a, count):
    parts = []
    for _ in range(count):
        part = a.astype(BF16)
        parts.append(part)
        a = a - part.astype(F32)
    return parts


def spread_dot(a, spread):
    return dot(
        jnp.concatenate(terms(a, 2), axis=1), jnp.concatenate([spread, spread], axis=0)
    )


def sum_dot(ones, a, count):
    return sum(dot(ones, part) for part in terms(a, count))


ROW_ROW = ((1,), (1,))
COL_COL = ((0,), (0,))


def sigmoid(v):
    return 1.0 / (1.0 + jnp.exp(-v))


def softplus(v):
    return jnp.maximum(v, 0.0) + jnp.log1p(jnp.exp(-jnp.abs(v)))


def expander(inner):
    head = lax.broadcasted_iota(jnp.int32, (LANES, inner), 0)
    column = lax.broadcasted_iota(jnp.int32, (LANES, inner), 1)
    inside = (column >= head * HD) & (column < (head + 1) * HD)
    return jnp.where(inside, 1.0, 0.0).astype(BF16)


def lower_ones():
    row = lax.broadcasted_iota(jnp.int32, (CHUNK, CHUNK), 0)
    column = lax.broadcasted_iota(jnp.int32, (CHUNK, CHUNK), 1)
    return jnp.where(row >= column, 1.0, 0.0)


def row_sums(a):
    lanes = a[:, :LANES]
    for start in range(LANES, a.shape[1], LANES):
        lanes = lanes + a[:, start : start + LANES]
    return jnp.sum(lanes.T, axis=0, keepdims=True)


def side_by_side(pair):
    lane = lax.broadcasted_iota(jnp.int32, pair.shape, 1)
    zero = jnp.zeros_like(pair)
    return jnp.concatenate(
        [jnp.where(lane < HD, pair, zero), jnp.where(lane < HD, zero, pair)], axis=0
    )


def decay_terms(step, rate, spread, tri):
    cum = sum_dot(tri.astype(BF16), rate, 3)
    total = cum[CHUNK - 1 : CHUNK, :]
    wide = spread_dot(
        jnp.concatenate([step, jnp.exp(cum), jnp.exp(total - cum)], axis=0), spread
    )
    return cum, cum.T, wide[:CHUNK], wide[CHUNK : 2 * CHUNK], wide[2 * CHUNK :]


def pair_mixing(cum, cum_t, scores, pair):
    decays = []
    for head in (2 * pair, 2 * pair + 1):
        differ = cum[:, head : head + 1] - cum_t[head : head + 1, :]
        decays.append(jnp.exp(jnp.minimum(differ, 0.0)))
    return decays, [(decay * scores).astype(BF16) for decay in decays]


def conv_forward(padded_ref, taps, rows):
    total = taps[KCONV : KCONV + 1, :]
    for k in range(KCONV):
        start = RIM - (KCONV - 1) + k
        total = total + taps[k : k + 1, :] * padded_ref[start : start + rows, :]
    return total


def forward_kernel(
    inner,
    tokens_ref,
    gain_ref,
    weight_ref,
    taps_ref,
    heads_ref,
    skip_ref,
    low_ref,
    rest_ref,
    mixed_ref,
    incoming_ref,
    padded,
    state,
):
    rows = tokens_ref.shape[1]
    conv = inner + 2 * NS
    @pl.when(pl.program_id(1) == 0)
    def _():
        padded[0:RIM, :] = jnp.zeros((RIM, conv), F32)
        state[...] = jnp.zeros_like(state)

    @pl.when(pl.program_id(1) > 0)
    def _():
        padded[0:RIM, :] = padded[rows : rows + RIM, :]

    tokens = tokens_ref[0].astype(F32)
    scale = lax.rsqrt(jnp.mean(tokens * tokens, axis=1, keepdims=True) + NORM_EPS)
    low = (tokens * scale * gain_ref[...]).astype(BF16)
    low_ref[0] = low
    projected = dot(low, weight_ref[...])
    rest_ref[0] = projected
    padded[RIM : RIM + rows, :] = projected[:, :conv]
    conv_out = conv_forward(padded, taps_ref[...], rows)
    active = conv_out * sigmoid(conv_out)
    heads = heads_ref[...]
    step_all = softplus(projected[:, conv:] + heads[0:1, :])
    rate_all = heads[1:2, :] * step_all
    skip = skip_ref[...]
    spread = expander(inner)
    tri = lower_ones()
    for c in range(rows // CHUNK):
        part = slice(c * CHUNK, (c + 1) * CHUNK)
        values = active[part, :inner]
        in_b = active[part, inner : inner + NS].astype(BF16)
        out_c = active[part, inner + NS :].astype(BF16)
        cum, cum_t, step_x, grown, remain = decay_terms(
            step_all[part], rate_all[part], spread, tri
        )
        stepped = values * step_x
        stepped_low = stepped.astype(BF16)
        scores = dot(out_c, in_b, ROW_ROW) * tri
        inside = []
        for pair in range(inner // LANES):
            lanes = slice(pair * LANES, (pair + 1) * LANES)
            _, mixing = pair_mixing(cum, cum_t, scores, pair)
            inside.append(
                dot(jnp.concatenate(mixing, axis=1), side_by_side(stepped_low[:, lanes]))
            )
        before = state[...]
        before_low = before.astype(BF16)
        incoming_ref[0, c] = before_low
        outer = grown * dot(out_c, before_low)
        mixed_ref[0, part, :] = jnp.concatenate(inside, axis=1) + outer + skip * values
        state[...] = grown[CHUNK - 1 : CHUNK, :] * before + dot(
            in_b, (remain * stepped).astype(BF16), COL_COL
        )


def stats_kernel(
    place_ref, up_ref, low_ref, weight_gate_ref, mixed_ref, gain_ref, *refs
):
    *block_refs, gate_ref, d_out_ref, stats_ref, weight_ref = refs

    @pl.when((pl.program_id(0) == 0) & (pl.program_id(1) == 0))
    def _():
        deep = block_refs[0].shape[0]
        for k, block_ref in enumerate(block_refs):
            start = pl.multiple_of((place_ref[0] ^ k) * deep, deep)
            weight_ref[pl.ds(start, deep), :] = block_ref[...]

    d_out = dot(up_ref[0], weight_ref[...], ROW_ROW)
    d_out_ref[0] = d_out
    gate = dot(low_ref[0], weight_gate_ref[...])
    gate_ref[0] = gate
    gated = mixed_ref[0] * gate * sigmoid(gate)
    stats_ref[0, 0:1, :] = row_sums(gated * gated)
    stats_ref[0, 1:2, :] = row_sums(d_out * gain_ref[...] * gated)


def row_to_lanes(row):
    return jnp.broadcast_to(row, (LANES, row.shape[1])).T[:, 0:1]


def keep_or_send(refs, step, value):
    if len(refs) == 1:
        refs[0][0] = value
        return

    @pl.when(step < 2)
    def _():
        refs[0][0] = value

    @pl.when(step >= 2)
    def _():
        refs[1][0] = value


def gate_back_kernel(
    order_ref, up_ref, weight_ref, gate_ref, mixed_ref, gain_ref, d_out_ref, stats_ref, *refs
):
    *branch_refs, grad_ref, d_mixed_ref, d_gate_ref, d_gain_ref, total = refs
    first = (pl.program_id(0) == 0) & (pl.program_id(1) == 0)
    last_one = pl.program_id(0) == pl.num_programs(0) - 1
    last_two = pl.program_id(1) == pl.num_programs(1) - 1

    @pl.when(first)
    def _():
        total[...] = jnp.zeros_like(total)
        d_gain_ref[...] = jnp.zeros_like(d_gain_ref)

    stats = stats_ref[0, 0]
    for k in range(1, stats_ref.shape[0]):
        stats = stats + stats_ref[k, 0]
    squares = row_to_lanes(stats[0:1])
    products = row_to_lanes(stats[1:2])
    scale = lax.rsqrt(squares * (1.0 / DI) + NORM_EPS)
    gate = gate_ref[0]
    mixed = mixed_ref[0]
    gain = gain_ref[...]
    d_out = d_out_ref[0]
    sig = sigmoid(gate)
    silu = gate * sig
    gated = mixed * silu
    unit = gated * scale
    low = (unit * gain).astype(BF16)
    keep_or_send(branch_refs, pl.program_id(1), dot(low, weight_ref[...]).astype(BF16))
    total[...] += dot(low, up_ref[0], COL_COL)
    d_gain_ref[...] += jnp.sum(d_out * unit, axis=0, keepdims=True)
    d_gated = scale * (gain * d_out - unit * (scale * products * (1.0 / DI)))
    d_mixed_ref[0] = d_gated * silu
    d_gate_ref[0] = (d_gated * mixed * (sig + silu * (1.0 - sig))).astype(BF16)

    @pl.when(last_one & last_two)
    def _():
        grad_ref[...] = total[...].astype(BF16)


def mixer_back_kernel(
    inner,
    rest_ref,
    rim_ref,
    mixed_ref,
    d_mixed_ref,
    incoming_ref,
    taps_ref,
    heads_ref,
    skip_ref,
    after_ref,
    d_rest_ref,
    d_taps_ref,
    d_heads_ref,
    d_skip_ref,
    padded,
    later,
    carried,
    d_active,
):
    rows = rest_ref.shape[1]
    conv = inner + 2 * NS
    block = pl.num_programs(0) - 1 - pl.program_id(0)

    @pl.when(pl.program_id(0) == 0)
    def _():
        d_taps_ref[...] = jnp.zeros_like(d_taps_ref)
        d_heads_ref[...] = jnp.zeros_like(d_heads_ref)
        d_skip_ref[...] = jnp.zeros_like(d_skip_ref)
        carried[...] = jnp.zeros_like(carried)
        later[rows : rows + RIM, :] = jnp.zeros((RIM, conv), F32)

    @pl.when(pl.program_id(0) > 0)
    def _():
        later[rows : rows + RIM, :] = later[0:RIM, :]

    rim = rim_ref[0][:, :conv]
    padded[0:RIM, :] = jnp.where(block > 0, rim, jnp.zeros_like(rim))
    padded[RIM : RIM + rows, :] = rest_ref[0][:, :conv]
    taps = taps_ref[...]
    conv_out = conv_forward(padded, taps, rows)
    sig = sigmoid(conv_out)
    active = conv_out * sig
    slope = sig + active * (1.0 - sig)
    heads = heads_ref[...]
    raw = rest_ref[0][:, conv:] + heads[0:1, :]
    step_all = softplus(raw)
    rate_all = heads[1:2, :] * step_all
    skip = skip_ref[...]
    spread = expander(inner)
    tri = lower_ones()
    upper = tri.T.astype(BF16)
    for c in reversed(range(rows // CHUNK)):
        part = slice(c * CHUNK, (c + 1) * CHUNK)
        values = active[part, :inner]
        in_b = active[part, inner : inner + NS].astype(BF16)
        out_c = active[part, inner + NS :].astype(BF16)
        step = step_all[part]
        rate = rate_all[part]
        cum, cum_t, step_x, grown, remain = decay_terms(step, rate, spread, tri)
        stepped = values * step_x
        stepped_low = stepped.astype(BF16)
        scores = dot(out_c, in_b, ROW_ROW) * tri
        d_mixed = d_mixed_ref[0, part, :]
        d_low = d_mixed.astype(BF16)
        d_scores = jnp.zeros((CHUNK, CHUNK), F32)
        inside = []
        for pair in range(inner // LANES):
            lanes = slice(pair * LANES, (pair + 1) * LANES)
            decays, mixing = pair_mixing(cum, cum_t, scores, pair)
            d_two = side_by_side(d_low[:, lanes])
            d_mixing = dot(d_two, stepped_low[:, lanes], ROW_ROW)
            d_scores += decays[0] * d_mixing[:CHUNK] + decays[1] * d_mixing[CHUNK:]
            inside.append(dot(jnp.concatenate(mixing, axis=0), d_two, COL_COL))
        before = incoming_ref[0, c]
        ahead = carried[...]
        ahead_low = ahead.astype(BF16)
        through = remain * dot(in_b, ahead_low)
        outer = (grown * d_mixed).astype(BF16)
        d_scores_low = (d_scores * tri).astype(BF16)
        d_in_b = dot((remain * stepped).astype(BF16), ahead_low, ROW_ROW) + dot(
            d_scores_low, out_c, COL_COL
        )
        d_out_c = dot(outer, before, ROW_ROW) + dot(d_scores_low, in_b)
        d_stepped = jnp.concatenate(inside, axis=1) + through
        stepped_near = stepped_low.astype(F32)
        both = d_low.astype(F32) * (mixed_ref[0, part, :] - skip * values)
        d_cum_x = both - stepped_near * d_stepped
        d_step_x = d_stepped * values
        grown_total = grown[CHUNK - 1 : CHUNK, :]
        d_total_x = jnp.sum(stepped_near * through, axis=0, keepdims=True) + grown_total * jnp.sum(
            ahead * before.astype(F32), axis=0, keepdims=True
        )
        gathered = jnp.concatenate(
            [d_cum_x, d_step_x, jnp.broadcast_to(d_total_x, (16, inner))], axis=0
        )
        narrow = sum(dot(part, spread, ROW_ROW) for part in terms(gathered, 2))
        d_rate = sum_dot(upper, narrow[:CHUNK], 2) + narrow[2 * CHUNK : 2 * CHUNK + 1]
        d_raw = (narrow[CHUNK : 2 * CHUNK] + heads[1:2, :] * d_rate) * sigmoid(raw[part])
        d_heads_ref[0:1, :] += jnp.sum(d_raw, axis=0, keepdims=True)
        d_heads_ref[1:2, :] += jnp.sum(d_rate * rate, axis=0, keepdims=True)
        d_skip_ref[...] += jnp.sum(d_mixed * values, axis=0, keepdims=True)
        d_rest_ref[0, part, conv:] = d_raw.astype(BF16)
        d_active[part, :inner] = d_stepped * step_x + skip * d_mixed
        d_active[part, inner : inner + NS] = d_in_b
        d_active[part, inner + NS :] = d_out_c
        carried[...] = grown_total * ahead + dot(out_c, outer, COL_COL)
    d_conv_out = d_active[...] * slope
    later[0:rows, :] = d_conv_out
    d_conv_in = jnp.zeros((rows, conv), F32)
    for k in range(KCONV):
        ahead_rows = KCONV - 1 - k
        start = RIM - (KCONV - 1) + k
        d_conv_in += taps[k : k + 1, :] * later[ahead_rows : ahead_rows + rows, :]
        d_taps_ref[k : k + 1, :] += jnp.sum(
            d_conv_out * padded[start : start + rows, :], axis=0, keepdims=True
        )
    d_taps_ref[KCONV : KCONV + 1, :] += jnp.sum(d_conv_out, axis=0, keepdims=True)
    d_rest_ref[0, :, :conv] = d_conv_in.astype(BF16)


def norm_back_kernel(
    order_ref, d_gate_ref, d_rest_ref, weight_gate_ref, weight_rest_ref, tokens_ref, after_ref, *refs
):
    *d_normed_refs, d_gain_ref = refs

    @pl.when(pl.program_id(0) == 0)
    def _():
        d_gain_ref[...] = jnp.zeros_like(d_gain_ref)

    d_normed = dot(d_gate_ref[0], weight_gate_ref[...], ROW_ROW) + dot(
        d_rest_ref[0], weight_rest_ref[...], ROW_ROW
    )
    tokens = tokens_ref[0].astype(F32)
    scale = lax.rsqrt(jnp.mean(tokens * tokens, axis=1, keepdims=True) + NORM_EPS)
    d_gain_ref[...] += jnp.sum(d_normed * (tokens * scale), axis=0, keepdims=True)
    keep_or_send(d_normed_refs, pl.program_id(0), d_normed.astype(BF16))


def whole(shape):
    return pl.BlockSpec(shape, lambda *_: (0,) * len(shape))


def by_rows(width):
    return pl.BlockSpec((1, ROWS, width), lambda s, b, *_: (s, b, 0))


def by_order(width):
    return pl.BlockSpec((1, ROWS, width), lambda s, b, order: (s, order[b], 0))


def left_alone():
    return pl.BlockSpec(memory_space=pl.ANY)


def cost(micros):
    return pl.CostEstimate(
        flops=int(micros * 1.1e9), bytes_accessed=int(micros * 2e6), transcendentals=0
    )


def params():
    return pltpu.CompilerParams(
        vmem_limit_bytes=VMEM_BYTES
    )


def shaped(shape, dtype=F32):
    return jax.ShapeDtypeStruct(shape, dtype)


def run_forward(tokens, norm_gain, weight, taps, heads, skip):
    count, length, _ = tokens.shape
    inner = skip.shape[1]
    rest = weight.shape[1]
    conv = inner + 2 * NS
    chunks = ROWS // CHUNK
    return pl.pallas_call(
        functools.partial(forward_kernel, inner),
        grid=(count, length // ROWS),
        in_specs=[
            by_rows(D),
            whole((1, D)),
            whole((D, rest)),
            whole((RIM, conv)),
            whole((8, LANES)),
            whole((1, inner)),
        ],
        out_specs=[
            by_rows(D),
            by_rows(rest),
            by_rows(inner),
            pl.BlockSpec((1, chunks, NS, inner), lambda s, b: (s, b, 0, 0)),
        ],
        out_shape=[
            shaped((count, length, D), BF16),
            shaped((count, length, rest)),
            shaped((count, length, inner)),
            shaped((count, length // CHUNK, NS, inner), BF16),
        ],
        scratch_shapes=[pltpu.VMEM((RIM + ROWS, conv), F32), pltpu.VMEM((NS, inner), F32)],
        compiler_params=params(),
        cost_estimate=cost(22),
        name="forward_mixer",
    )(tokens, norm_gain, weight, taps, heads, skip)


def run_stats(place, upstream, low, weight_gate, mixed, gate_gain, blocks):
    count, length, inner = mixed.shape
    return pl.pallas_call(
        stats_kernel,
        grid_spec=pltpu.PrefetchScalarGridSpec(
            num_scalar_prefetch=1,
            grid=(count, length // ROWS),
            in_specs=[
                by_rows(D),
                by_rows(D),
                whole((D, inner)),
                by_rows(inner),
                whole((1, inner)),
            ]
            + [whole(block.shape) for block in blocks],
            out_specs=[
                by_rows(inner),
                by_rows(inner),
                pl.BlockSpec((1, 2, ROWS), lambda s, b, *_: (s, 0, b)),
                whole((inner, D)),
            ],
        ),
        out_shape=[
            shaped((count, length, inner)),
            shaped((count, length, inner)),
            shaped((count, 2, length)),
            shaped((inner, D), BF16),
        ],
        compiler_params=params(),
        cost_estimate=cost(11),
        name="gate_stats",
    )(place, upstream, low, weight_gate, mixed, gate_gain, *blocks)


def kept_and_sent(split, count, length, place):
    if not split:
        return [place(lambda order, b: order[b])], [shaped((count, length, D), BF16)]
    specs = [
        place(lambda order, b: jnp.minimum(b, 1)),
        place(lambda order, b: jnp.maximum(b - 2, 0)),
    ]
    return specs, [shaped((count, 2 * ROWS, D), BF16)] * 2


def run_gate_back(split, order, upstream, weight, gate, mixed, gate_gain, d_out, stats):
    count, length, inner = gate.shape

    def place(group):
        return pl.BlockSpec((1, ROWS, D), lambda s, b, order: (s, group(order, b), 0))

    branch_specs, branch_shapes = kept_and_sent(split, count, length, place)
    return pl.pallas_call(
        gate_back_kernel,
        grid_spec=pltpu.PrefetchScalarGridSpec(
            num_scalar_prefetch=1,
            grid=(count, length // ROWS),
            in_specs=[
                by_order(D),
                whole((inner, D)),
                by_order(inner),
                by_order(inner),
                whole((1, inner)),
                by_order(inner),
                pl.BlockSpec(
                    (stats.shape[0], 1, 2, ROWS), lambda s, b, order: (0, s, 0, order[b])
                ),
            ],
            out_specs=branch_specs
            + [whole((inner, D)), by_order(inner), by_order(inner), whole((1, inner))],
            scratch_shapes=[pltpu.VMEM((inner, D), F32)],
        ),
        out_shape=branch_shapes
        + [
            shaped((inner, D), BF16),
            shaped((count, length, inner)),
            shaped((count, length, inner), BF16),
            shaped((1, inner)),
        ],
        compiler_params=params(),
        cost_estimate=cost(13),
        name="gate_back",
    )(order, upstream, weight, gate, mixed, gate_gain, d_out, stats)


def run_mixer_back(s, rest, mixed, d_mixed, incoming, taps, heads, skip, after):
    _, length, inner = mixed.shape
    conv = inner + 2 * NS
    last = length // ROWS - 1
    chunks = ROWS // CHUNK
    width = rest.shape[2]

    def rows(width, s=s):
        return pl.BlockSpec((1, ROWS, width), lambda b: (s, last - b, 0))

    return pl.pallas_call(
        functools.partial(mixer_back_kernel, inner),
        grid=(length // ROWS,),
        in_specs=[
            rows(width),
            pl.BlockSpec(
                (1, RIM, width),
                lambda b: (s, jnp.maximum((last - b) * (ROWS // RIM) - 1, 0), 0),
            ),
            rows(inner),
            rows(inner),
            pl.BlockSpec((1, chunks, NS, inner), lambda b: (s, last - b, 0, 0)),
            whole((RIM, conv)),
            whole((8, LANES)),
            whole((1, inner)),
            left_alone(),
        ],
        out_specs=[rows(width, 0), whole((RIM, conv)), whole((8, LANES)), whole((1, inner))],
        scratch_shapes=[
            pltpu.VMEM((RIM + ROWS, conv), F32),
            pltpu.VMEM((RIM + ROWS, conv), F32),
            pltpu.VMEM((NS, inner), F32),
            pltpu.VMEM((ROWS, conv), F32),
        ],
        out_shape=[
            shaped((1, length, width), BF16),
            shaped((RIM, conv)),
            shaped((8, LANES)),
            shaped((1, inner)),
        ],
        compiler_params=params(),
        cost_estimate=cost(19),
        name="mixer_back",
    )(rest, rest, mixed, d_mixed, incoming, taps, heads, skip, after)


def run_norm_back(split, s, order, d_gate, d_rest, weight_gate, weight_rest, tokens, after):
    _, length, inner = d_gate.shape
    width = d_rest.shape[2]

    def rows(width, s):
        return pl.BlockSpec((1, ROWS, width), lambda b, order: (s, order[b], 0))

    def place(group):
        return pl.BlockSpec((1, ROWS, D), lambda b, order: (0, group(order, b), 0))

    specs, shapes = kept_and_sent(split, 1, length, place)
    return pl.pallas_call(
        norm_back_kernel,
        grid_spec=pltpu.PrefetchScalarGridSpec(
            num_scalar_prefetch=1,
            grid=(length // ROWS,),
            in_specs=[
                rows(inner, s),
                rows(width, 0),
                whole(weight_gate.shape),
                whole(weight_rest.shape),
                rows(D, s),
                left_alone(),
            ],
            out_specs=specs + [whole((1, D))],
        ),
        out_shape=shapes + [shaped((1, D))],
        compiler_params=params(),
        cost_estimate=cost(6),
        name="norm_back",
    )(order, d_gate, d_rest, weight_gate, weight_rest, tokens, after)


BOTH = ("dp", "ctx")


def swapped(value, axis, mask):
    count = lax.axis_size(axis)
    return lax.ppermute(value, axis, [(a, a ^ mask) for a in range(count)])


def gather_blocks(block):
    if lax.axis_size("dp") != 8:
        return [lax.all_gather(block, "dp", axis=0, tiled=True)]
    far, near, side = (swapped(block, "dp", mask) for mask in (4, 2, 1))
    far_near, far_side = swapped(far, "dp", 2), swapped(far, "dp", 1)
    near_side = swapped(near, "dp", 1)
    every = swapped(far_near, "dp", 1)
    return [block, side, near, near_side, far, far_side, far_near, every]


def chip_sums(parts):
    if len(parts) == 1:
        total = lax.psum_scatter(parts[0], "ctx", scatter_dimension=1, tiled=True)
        return total.astype(F32), None
    kept, sent = parts
    got = swapped(sent, "ctx", 1)
    own = kept[:, :ROWS].astype(F32) + got[:, :ROWS].astype(F32)
    return own, (kept[:, ROWS:].astype(F32) + got[:, ROWS:].astype(F32)).astype(BF16)


def across_sums(own, sent):
    if sent is None:
        return own
    return own + swapped(sent, "ctx", 2).astype(F32)


def sum_over_dp(value):
    if lax.axis_size("dp") != 8:
        return lax.psum(value, "dp")
    for mask in (1, 2, 4):
        value = value + swapped(value, "dp", mask)
    return value


def adam_step(weight, first_old, second_old, gradient, step_rate):
    first_new = BETA_ONE * first_old + (1.0 - BETA_ONE) * gradient
    second_new = BETA_TWO * second_old + (1.0 - BETA_TWO) * gradient * gradient
    first_hat = first_new / (1.0 - BETA_ONE**STEP)
    second_hat = second_new / (1.0 - BETA_TWO**STEP)
    weight_new = weight - step_rate * (
        first_hat / (jnp.sqrt(second_hat) + ADAM_EPS) + DECAY_WEIGHT * weight
    )
    return (second_new, weight_new)


def pad_lanes(value, width):
    return jnp.pad(value, [(0, 0)] * (value.ndim - 1) + [(0, width - value.shape[-1])])


def shards(
    block_in,
    out_grad,
    w_in,
    w_in_m,
    w_in_v,
    w_out,
    w_out_m,
    w_out_v,
    small_params,
    small_m,
    small_v,
):
    n_dp, n_ctx = lax.axis_size("dp"), lax.axis_size("ctx")
    rank = lax.axis_index("ctx")
    heads = HEADS // n_ctx
    inner = heads * HD
    conv = inner + 2 * NS
    count = block_in.shape[0]

    moves = []
    for block in range(n_dp * n_ctx):
        moves.append((block, (block % n_dp) * n_ctx + block // n_dp))
    mine_out = lax.ppermute(w_out.astype(BF16), BOTH, moves)
    w_in_low = w_in.astype(BF16)
    slices = []
    for r in range(n_ctx):
        first = DI + CHANNELS + r * heads
        slices.append(
            jnp.concatenate(
                [
                    w_in_low[:, DI + r * inner : DI + (r + 1) * inner],
                    w_in_low[:, 2 * DI : 2 * DI + 2 * NS],
                    pad_lanes(w_in_low[:, first : first + heads], LANES),
                ],
                axis=1,
            )
        )

    def to_ranks(slices):
        stacked = jnp.stack(slices)
        sent = jnp.broadcast_to(stacked[None], (n_dp,) + stacked.shape)
        sent = sent.reshape(-1, stacked.shape[2])
        return lax.all_to_all(sent, BOTH, split_axis=0, concat_axis=0, tiled=True)

    tokens = lax.all_gather(block_in, "ctx", axis=1, tiled=True)
    upstream = lax.all_gather(out_grad, "ctx", axis=1, tiled=True)
    weight_rest = to_ranks(slices)
    weight_gate = to_ranks([w_in_low[:, r * inner : (r + 1) * inner] for r in range(n_ctx)])
    blocks_out = gather_blocks(mine_out)

    offset = 0
    pieces = []
    for amount in (D, DI, KCONV * CHANNELS, CHANNELS, HEADS, HEADS, HEADS):
        pieces.append(small_params[offset : offset + amount])
        offset = offset + amount
    norm_gain = pieces[0].reshape(1, D)
    gate_gain = lax.dynamic_slice(pieces[1], (rank * inner,), (inner,)).reshape(1, inner)
    taps_all = jnp.concatenate([pieces[2].reshape(KCONV, CHANNELS), pieces[3][None]], axis=0)
    taps = jnp.concatenate(
        [lax.dynamic_slice(taps_all, (0, rank * inner), (KCONV + 1, inner)), taps_all[:, DI:]],
        axis=1,
    )
    taps = jnp.pad(taps, ((0, RIM - KCONV - 1), (0, 0)))
    dt_bias = lax.dynamic_slice(pieces[4], (rank * heads,), (heads,))
    decay = -jnp.exp(lax.dynamic_slice(pieces[5], (rank * heads,), (heads,)))
    head_rows = jnp.pad(jnp.stack([dt_bias, decay]), ((0, 6), (0, LANES - heads)))
    skip = jnp.repeat(lax.dynamic_slice(pieces[6], (rank * heads,), (heads,)), HD).reshape(1, inner)

    split = n_ctx == 4 and block_in.shape[1] == ROWS
    place = lax.axis_index("dp") if len(blocks_out) > 1 else rank * 0
    place = place.astype(jnp.int32).reshape(1)
    order = jnp.arange(n_ctx * block_in.shape[1] // ROWS, dtype=jnp.int32)
    if split:
        order = rank.astype(jnp.int32) ^ jnp.array([0, 2, 1, 3], jnp.int32)
    low, rest, mixed, incoming = run_forward(tokens, norm_gain, weight_rest, taps, head_rows, skip)
    gate, d_out, stats, weight_out = run_stats(
        place, upstream, low, weight_gate, mixed, gate_gain, blocks_out
    )
    stats = lax.all_gather(stats, "ctx")
    *branch, grad_out, d_mixed, d_gate, d_gate_gain = run_gate_back(
        split, order, upstream, weight_out, gate, mixed, gate_gain, d_out, stats
    )
    grad_out = lax.all_to_all(grad_out, "dp", split_axis=0, concat_axis=0, tiled=True)
    branch, branch_sent = chip_sums(branch)

    def to_owners(grad):
        return lax.all_to_all(grad.astype(BF16), BOTH, split_axis=0, concat_axis=0, tiled=True)

    def summed(got):
        return jnp.sum(got.astype(F32).reshape(n_dp, n_ctx, -1, got.shape[1]), axis=0)

    grad_gate = dot(low.reshape(-1, D), d_gate.reshape(-1, inner), COL_COL).astype(BF16)
    after = grad_gate if branch_sent is None else branch_sent
    branch = across_sums(branch, branch_sent)
    grad_rest = 0.0
    smalls = []
    normeds = []
    for s in range(count):
        d_rest, *small = run_mixer_back(
            s, rest, mixed, d_mixed, incoming, taps, head_rows, skip, after
        )
        grad_rest = grad_rest + dot(low[s], d_rest[0], COL_COL)
        if s == 0:
            after = grad_out
            grad_gate = to_owners(grad_gate)
        if s == count - 1:
            grad_rest = grad_rest.astype(BF16)
            after = grad_rest
            grad_rest = to_owners(grad_rest)
        *d_normed, d_gain = run_norm_back(
            split, s, order, d_gate, d_rest, weight_gate, weight_rest, tokens, after
        )
        smalls.append([d_gain] + small)
        d_normed, normed_sent = chip_sums(d_normed)
        after = d_normed if normed_sent is None else normed_sent
        normeds.append(across_sums(d_normed, normed_sent))
    d_normed = jnp.concatenate(normeds, axis=0)
    d_norm_gain, d_taps, d_heads, d_skip = (sum(parts) for parts in zip(*smalls))
    grad_out = jnp.sum(grad_out.astype(F32).reshape(n_dp, -1, D), axis=0)
    grad_out = lax.ppermute(grad_out, BOTH, [(b, a) for a, b in moves])
    grad_gate = summed(grad_gate)
    grad_rest = summed(grad_rest)
    columns = [grad_gate[r] for r in range(n_ctx)]
    columns += [grad_rest[r, :, :inner] for r in range(n_ctx)]
    columns += [jnp.sum(grad_rest[:, :, inner:conv], axis=0)]
    columns += [grad_rest[r, :, conv : conv + heads] for r in range(n_ctx)]
    grad_in = jnp.concatenate(columns, axis=1)

    parts = (
        d_norm_gain.reshape(-1),
        d_gate_gain.reshape(-1),
        d_taps[: KCONV + 1].reshape(-1),
        d_heads[0, :heads],
        d_heads[1, :heads],
        jnp.sum(d_skip.reshape(heads, HD), axis=1),
    )
    mine = jnp.concatenate(parts)
    mine = jnp.pad(mine, (0, -mine.shape[0] % (8 * LANES))).reshape(-1, LANES)
    every = lax.all_gather(sum_over_dp(mine), "ctx", axis=0).reshape(n_ctx, -1)
    offset = 0
    found = []
    for part in parts:
        found.append(every[:, offset : offset + part.shape[0]])
        offset = offset + part.shape[0]
    taps_found = found[2].reshape(n_ctx, KCONV + 1, conv)
    taps_found = jnp.concatenate(
        [
            jnp.swapaxes(taps_found[:, :, :inner], 0, 1).reshape(KCONV + 1, DI),
            jnp.sum(taps_found[:, :, inner:], axis=0),
        ],
        axis=1,
    )
    grad_small = jnp.concatenate(
        [jnp.sum(found[0], axis=0), found[1].reshape(-1), taps_found.reshape(-1)]
        + [found[k].reshape(-1) for k in (3, 4, 5)]
    )

    own = block_in.astype(F32)
    block_out = (own + branch.astype(F32)).astype(BF16)
    scale = lax.rsqrt(jnp.mean(own * own, axis=-1, keepdims=True) + NORM_EPS)
    d_scaled = d_normed * norm_gain
    d_own = scale * (
        d_scaled - own * scale * scale * jnp.mean(d_scaled * own, axis=-1, keepdims=True)
    )
    input_grad = (out_grad.astype(F32) + d_own).astype(BF16)
    in_second, in_new = adam_step(w_in, w_in_m, w_in_v, grad_in, RATE_BIG)
    out_second, out_new = adam_step(w_out, w_out_m, w_out_v, grad_out, RATE_BIG)
    small_second, small_updated = adam_step(small_params, small_m, small_v, grad_small, RATE_SMALL)
    return (
        block_out,
        input_grad,
        grad_in,
        in_second,
        in_new,
        grad_out,
        out_second,
        out_new,
        grad_small,
        small_second,
        small_updated,
    )


def solution(mesh):
    rows = P(("dp", "ctx"), None)
    spread = P("dp", "ctx", None)
    return jax.shard_map(
        shards,
        mesh=mesh,
        in_specs=(spread, spread) + (rows,) * 6 + (P(),) * 3,
        out_specs=(spread, spread) + (rows,) * 6 + (P(),) * 3,
        check_vma=False,
    )
```

time: 881 us -> 348 us (0.40)
  waiting for transfers between devices: 415 us -> 50.8 us
  matrix products: 199 us -> 11.6 us
  Pallas kernels: 0 us -> 104 us
  other arithmetic: 103 us -> 23.4 us
  starting transfers between devices: 12.9 us -> 70.7 us
  local copies, waits for them, and re-layouts: 69.5 us -> 20 us
    reduce_scatter x2 -> x0, waiting for transfers between devices: 262 us -> none  [the longest x1 133 us: shards(): lax.psum_scatter(grad_out, ('dp', 'ctx'), scatter_dimension=0, tiled=True)]
    dot_general x36 -> x3, matrix products: 199 us -> 11.6 us  [dot(): lax.dot_general(a, b, (contract, ((), ())), preferred_element_type=F32)]
    all_gather x6 -> x2, waiting for transfers between devices: 152 us -> 7.01 us  [the longest x1 6.99 us: shards(): upstream = lax.all_gather(out_grad, 'ctx', axis=1, tiled=True)]
    pallas_call x0 -> x7, Pallas kernels: none -> 104 us  [the longest x2 38.6 us: run_mixer_back(): pl.pallas_call(functools.partial(mixer_back_kernel, inner), grid=(length...]
    psum x1 -> x0, blocking collectives: 43.5 us -> none  [shards(): grad_small_all = lax.psum(grad_small, ('dp', 'ctx'))]
    all_gather x2, blocking collectives: 10.3 us -> 49.3 us  [the longest x1 44 us: shards(): every = lax.all_gather(sum_over_dp(mine), 'ctx', axis=0).reshape(n_ctx, -1)]
    ppermute x4 -> x18, waiting for transfers between devices: 0.02 us -> 38.8 us  [the longest x1 28 us: shards(): mine_out = lax.ppermute(w_out.astype(BF16), BOTH, moves)]
    ppermute x4 -> x18, starting transfers between devices: 12.6 us -> 43 us  [the longest x16 35.4 us: swapped(): return lax.ppermute(value, axis, [(a, a ^ mask) for a in range(count)])]
  transfers between devices with their start and end apart: 12 -> 25, of which waited for: 4 -> 7; matrix products, arithmetic and copies ran while one was open for 18% -> 11% of each run, Pallas kernels for 0% -> 20%
where the time goes in v1:
time: 348 us; the launch traced here: 344 us
  Pallas kernels  104 us (30%)
  starting transfers between devices  70.7 us (20%)
  waiting for transfers between devices  50.8 us (15%)
  blocking collectives  49.3 us (14%)
  other arithmetic  23.4 us (7%)
  local copies, waits for them, and re-layouts  20 us (6%)
  between operations  14.7 us (4%)
  matrix products  11.6 us (3%)
    all_gather x1, blocking collectives, shards(): every = lax.all_gather(sum_over_dp(mine), 'ctx', axis=0).reshape(n_ctx, -1)  44 us
    pallas_call x2, Pallas kernels, run_mixer_back(): pl.pallas_call(functools.partial(mixer_back_kernel, inner), grid=(length...  38.6 us
    ppermute x16, starting transfers between devices, swapped(): return lax.ppermute(value, axis, [(a, a ^ mask) for a in range(count)])  35.4 us
    ppermute x1, waiting for transfers between devices, shards(): mine_out = lax.ppermute(w_out.astype(BF16), BOTH, moves)  28 us
    pallas_call x1, Pallas kernels, run_forward(): pl.pallas_call(functools.partial(forward_kernel, inner), grid=(count, len...  21.8 us
    pallas_call x1, Pallas kernels, run_gate_back(): pl.pallas_call(gate_back_kernel, grid_spec=pltpu.PrefetchScalarGridSpec(n...  16.2 us
    pallas_call x2, Pallas kernels, run_norm_back(): pl.pallas_call(norm_back_kernel, grid_spec=pltpu.PrefetchScalarGridSpec(n...  14.6 us
    unnamed x85, local copies, waits for them, and re-layouts  12.9 us
  transfers between devices with their start and end apart: 25, of which 7 were waited for; matrix products, arithmetic and copies ran while one was open for 11% of the time, Pallas kernels for 20%

profile of v1, /device:TPU:5, one launch (start us, length us, event | category | flops | bytes accessed | tf_op | source)
XLA Modules:
  0.0 344.2 jit_solution(2974540809593415161)
XLA Ops:
  10.4 6.4 %all-to-all-start = ((bf16[32,32,896]{2,1,0:T(8,128)(2,1)}), bf16[32,32,896]{2,1,0:T(8,128)(2,1)S(1)}, u32[]{:S(2)}, u32[]{:S(2)}) async-start(bf16[32,32,896]{2,1,0:T(8,128)(2,1)} %bitcast.111), calls=%async_computation | async-start | bytes 3670016 | tf_op jit(solution)/shard_map/all_to_all | solution.py:743
  16.9 4.3 %collective-permute-start = (bf16[64,1024]{1,0:T(8,128)(2,1)S(1)}, bf16[64,1024]{1,0:T(8,128)(2,1)S(1)}, u32[]{:S(2)}, u32[]{:S(2)}) collective-permute-start(bf16[64,1024]{1,0:T(8,128)(2,1)S(1)} %convert_element_type.109), channel_id=1, source_target_pairs={{0,0},{1,4},{2,8},{3,12},{4,16},{5,20},{6,24},{7,28},{8,1},{9,5},{... | collective-permute-start | bytes 393224 | tf_op jit(solution)/shard_map/ppermute | solution.py:723
  21.4 28.0 %collective-permute-done.refs_0_ = bf16[64,1024]{1,0:T(8,128)(2,1)S(1)} collective-permute-done((bf16[64,1024]{1,0:T(8,128)(2,1)S(1)}, bf16[64,1024]{1,0:T(8,128)(2,1)S(1)}, u32[]{:S(2)}, u32[]{:S(2)}) %collective-permute-start) | collective-permute-done | bytes 131104 | tf_op jit(solution)/shard_map/ppermute | solution.py:723
  49.4 17.2 %collective-permute-start.4 = (bf16[64,1024]{1,0:T(8,128)(2,1)S(1)}, bf16[64,1024]{1,0:T(8,128)(2,1)S(1)}, u32[]{:S(2)}, u32[]{:S(2)}) collective-permute-start(bf16[64,1024]{1,0:T(8,128)(2,1)S(1)} %collective-permute-done.refs_0_), channel_id=1, source_target_pairs={{0,16},{4,20},{8,24},{12,28},{16,0},{20,4},{24,8},{28,12},{1,17},{... | collective-permute-start | bytes 393224 | tf_op jit(solution)/shard_map/ppermute | solution.py:648
  69.4 3.6 %collective-permute-start.6 = (bf16[64,1024]{1,0:T(8,128)(2,1)S(1)}, bf16[64,1024]{1,0:T(8,128)(2,1)}, u32[]{:S(2)}, u32[]{:S(2)}) collective-permute-start(bf16[64,1024]{1,0:T(8,128)(2,1)S(1)} %collective-permute-done.4.refs_4_), channel_id=1, source_target_pairs={{0,8},{4,12},{8,0},{12,4},{16,24},{20,28},{24,16},{28,20},{1,9},{5... | collective-permute-start | bytes 393224 | tf_op jit(solution)/shard_map/ppermute | solution.py:648
  77.9 6.0 %all-to-all-start.1 = ((bf16[32,32,512]{2,1,0:T(8,128)(2,1)}), bf16[32,32,512]{2,1,0:T(8,128)(2,1)S(1)}, u32[]{:S(2)}, u32[]{:S(2)}) async-start(bf16[32,32,512]{2,1,0:T(8,128)(2,1)} %bitcast.112), calls=%async_computation.1 | async-start | bytes 2097152 | tf_op jit(solution)/shard_map/all_to_all | solution.py:743
  84.0 21.8 %forward_mixer.1 = (bf16[2,1024,1024]{2,1,0:T(8,128)(2,1)}, f32[2,1024,896]{2,1,0:T(8,128)}, f32[2,1024,512]{2,1,0:T(8,128)}, bf16[2,8,128,512]{3,2,1,0:T(8,128)(2,1)S(1)}) custom-call(bf16[2,1024,1024]{2,1,0:T(8,128)(2,1)} %all-gather.7.cloned.1.call-done.tokens_ref, f32[1,1024]{1,0:T(1,128)S(1)} %bitcast.107, bf16[1024,896]{1,0:T(8,128)(2,1)S(1)} %bitcast.99, ...), custom_call_target="tpu_custom_call" | custom-call | flops 24199999488 | bytes 44000000 | tf_op jit(solution)/shard_map/forward_mixer/pallas_call | solution.py:450
  109.2 7.0 %all-gather.5.cloned.1.call-done.up_ref = bf16[2,1024,1024]{2,1,0:T(8,128)(2,1)} async-done(((bf16[2,256,1024]{2,1,0:T(8,128)(2,1)}), bf16[2,1024,1024]{2,1,0:T(8,128)(2,1)}) %all-gather.5.cloned.1.call-update) | async-done | bytes 4194320 | tf_op jit(solution)/shard_map/all_gather | solution.py:746
  116.2 12.4 %gate_stats.1 = (f32[2,1024,512]{2,1,0:T(8,128)}, f32[2,1024,512]{2,1,0:T(8,128)}, f32[2,2,1024]{2,1,0:T(2,128)S(1)}, bf16[512,1024]{1,0:T(8,128)(2,1)S(1)}) custom-call(s32[1]{0:T(128)} %bitcast.place_ref, bf16[2,1024,1024]{2,1,0:T(8,128)(2,1)} %all-gather.5.cloned.1.call-done.up_ref, bf16[2,1024,1024]{2,1,0:T(8,128)(2,1)} %get-tuple-element.39.low_ref, ...), custom_call_target="tpu_custom_call" | custom-call | flops 12099999744 | bytes 22000000 | tf_op jit(solution)/shard_map/gate_stats/pallas_call | solution.py:482
  128.6 5.3 %all-gather = f32[8,2,1024]{2,1,0:T(2,128)S(1)} all-gather(f32[2,2,1024]{2,1,0:T(2,128)S(1)} %get-tuple-element.44), channel_id=2, replica_groups=mesh['dp'=8,'ctx'=4] {'ctx'}, dimensions={0}, use_global_device_ids=true | all-gather | bytes 81920 | tf_op jit(solution)/shard_map/all_gather | solution.py:779
  134.0 16.2 %gate_back.1 = (bf16[2,512,1024]{2,1,0:T(8,128)(2,1)S(1)}, bf16[2,512,1024]{2,1,0:T(8,128)(2,1)}, bf16[512,1024]{1,0:T(8,128)(2,1)S(1)}, f32[2,1024,512]{2,1,0:T...) custom-call(s32[4]{0:T(128)S(1)} %broadcast_xor_fusion.order_ref, ...), custom_call_target="tpu_custom_call" | custom-call | flops 14300000256 | bytes 26000000 | tf_op jit(solution)/shard_map/gate_back/pallas_call | solution.py:531
  151.3 5.5 %all-to-all-start.2 = ((bf16[8,64,1024]{2,1,0:T(8,128)(2,1)}), bf16[8,64,1024]{2,1,0:T(8,128)(2,1)S(1)}, u32[]{:S(2)}, u32[]{:S(2)}) async-start(bf16[8,64,1024]{2,1,0:T(8,128)(2,1)} %bitcast.105), calls=%async_computation.2 | async-start | bytes 2097152 | tf_op jit(solution)/shard_map/all_to_all | solution.py:783
  158.7 19.3 %mixer_back.2 = (bf16[1,1024,896]{2,1,0:T(8,128)(2,1)S(1)}, f32[8,768]{1,0:T(8,128)S(1)}, f32[8,128]{1,0:T(8,128)S(1)}, f32[1,512]{1,0:T(1,128)S(1)}) custom-call(f32[2,1024,896]{2,1,0:T(8,128)} %get-tuple-element.48.rest_ref.rim_ref, f32[2,1024,896]{2,1,0:T(8,128)} %get-tuple-element.48.rest_ref.rim_ref, f32[2,1024,512]{2,1,0:T(8,128)} %get-tuple-element.40.mixed_ref, ...), custom_call_target="tpu_custom_call" | custom-call | flops 20899999744 | bytes 38000000 | tf_op jit(solution)/shard_map/mixer_back/pallas_call | solution.py:574
  184.5 7.8 %norm_back.2 = (bf16[1,512,1024]{2,1,0:T(8,128)(2,1)S(1)}, bf16[1,512,1024]{2,1,0:T(8,128)(2,1)}, f32[1,1024]{1,0:T(1,128)S(1)}) custom-call(s32[4]{0:T(128)S(1)} %broadcast_xor_fusion.order_ref, bf16[2,1024,512]{2,1,0:T(8,128)(2,1)} %get-tuple-element.47.d_gate_ref, bf16[1,1024,896]{2,1,0:T(8,128)(2,1)S(1)} %copy-done.15, bf16[1024,512]{1,0:T(8,128)(2,1)S(1)} %bitcast.103, ...), custom_call_target="tpu_custom_call" | custom-call | flops 6600000000 | bytes 12000000 | tf_op jit(solution)/shard_map/norm_back/pallas_call | solution.py:621
  193.8 3.4 bitcast_convert_fusion
  201.2 3.3 collective-permute-start.14
  206.8 19.3 %mixer_back.3 = (bf16[1,1024,896]{2,1,0:T(8,128)(2,1)S(1)}, f32[8,768]{1,0:T(8,128)S(1)}, f32[8,128]{1,0:T(8,128)S(1)}, f32[1,512]{1,0:T(1,128)S(1)}) custom-call(f32[2,1024,896]{2,1,0:T(8,128)} %get-tuple-element.48.rest_ref.rim_ref, f32[2,1024,896]{2,1,0:T(8,128)} %get-tuple-element.48.rest_ref.rim_ref, f32[2,1024,512]{2,1,0:T(8,128)} %get-tuple-element.40.mixed_ref, ...), custom_call_target="tpu_custom_call" | custom-call | flops 20899999744 | bytes 38000000 | tf_op jit(solution)/shard_map/mixer_back/pallas_call | solution.py:574
  227.6 4.7 %fusion.9 = f32[1024,896]{1,0:T(8,128)S(1)} fusion(bf16[2,1024,1024]{2,1,0:T(8,128)(2,1)} %get-tuple-element.39.low_ref, bf16[1,1024,896]{2,1,0:T(8,128)(2,1)} %copy-done.12), kind=kOutput, calls=%fused_computation.18 | convolution fusion | flops 1879048192 | bytes 7602176 | tf_op jit(solution)/shard_map/dot_general | solution.py:38
  232.3 3.6 %add_convert_fusion.after_ref = bf16[1024,896]{1,0:T(8,128)(2,1)} fusion(f32[1024,896]{1,0:T(8,128)S(1)} %fusion.9, bf16[1,1024,896]{2,1,0:T(8,128)(2,1)S(1)} %copy-done.16, bf16[2,1024,1024]{2,1,0:T(8,128)(2,1)S(1)} %copy-done.39), kind=kOutput, calls=%fused_computation.1 | convolution fusion | flops 1880883200 | bytes 9437184 | tf_op jit(solution)/shard_map/dot_general | solution.py:38
  235.9 6.8 %norm_back.3 = (bf16[1,512,1024]{2,1,0:T(8,128)(2,1)S(1)}, bf16[1,512,1024]{2,1,0:T(8,128)(2,1)S(1)}, f32[1,1024]{1,0:T(1,128)S(1)}) custom-call(s32[4]{0:T(128)S(1)} %broadcast_xor_fusion.order_ref, bf16[2,1024,512]{2,1,0:T(8,128)(2,1)} %get-tuple-element.47.d_gate_ref, bf16[1,1024,896]{2,1,0:T(8,128)(2,1)S(1)} %copy-done.13, ...), custom_call_target="tpu_custom_call" | custom-call | flops 6600000000 | bytes 12000000 | tf_op jit(solution)/shard_map/norm_back/pallas_call | solution.py:621
  256.4 6.5 %all-to-all-start.4 = ((bf16[32,32,896]{2,1,0:T(8,128)(2,1)}), bf16[32,32,896]{2,1,0:T(8,128)(2,1)}, u32[]{:S(2)}, u32[]{:S(2)}) async-start(bf16[32,32,896]{2,1,0:T(8,128)(2,1)} %bitcast.113), calls=%async_computation.4 | async-start | bytes 3670016 | tf_op jit(solution)/shard_map/all_to_all | solution.py:787
  264.1 44.0 %all-gather.1 = f32[192,128]{1,0:T(8,128)S(1)} all-gather(f32[48,128]{1,0:T(8,128)S(1)} %add.171), channel_id=3, replica_groups=mesh['dp'=8,'ctx'=4] {'ctx'}, dimensions={0}, use_global_device_ids=true | all-gather | bytes 122880 | tf_op jit(solution)/shard_map/all_gather | solution.py:839
  317.3 8.8 %collective-permute-done.13 = bf16[1,256,1024]{2,1,0:T(8,128)(2,1)S(1)} collective-permute-done((bf16[1,256,1024]{2,1,0:T(8,128)(2,1)S(1)}, bf16[1,256,1024]{2,1,0:T(8,128)(2,1)S(1)}, u32[]{:S(2)}, u32[]{:S(2)}) %collective-permute-start.13) | collective-permute-done | bytes 524320 | tf_op jit(solution)/shard_map/ppermute | solution.py:648
  328.6 3.4 fusion.7
  (202 shorter events, 64.9 us)
Async XLA Ops:
  7.2 76.8 %all-gather.7.cloned.1.call-start = ((), (), s32[]{:S(2)}) async-start(), calls=%async_computation.6 | async-start | bytes 5242880 | tf_op jit(solution)/shard_map/all_gather | solution.py:745
  7.9 108.3 %all-gather.5.cloned.1.call-start = ((), (), s32[]{:S(2)}) async-start(), calls=%async_computation.5 | async-start | bytes 5242880 | tf_op jit(solution)/shard_map/all_gather | solution.py:746
  10.4 66.3 %all-to-all-start = ((bf16[32,32,896]{2,1,0:T(8,128)(2,1)}), bf16[32,32,896]{2,1,0:T(8,128)(2,1)S(1)}, u32[]{:S(2)}, u32[]{:S(2)}) async-start(bf16[32,32,896]{2,1,0:T(8,128)(2,1)} %bitcast.111), calls=%async_computation | async-start | bytes 3670016 | tf_op jit(solution)/shard_map/all_to_all | solution.py:743
  16.9 32.5 %collective-permute-start = (bf16[64,1024]{1,0:T(8,128)(2,1)S(1)}, bf16[64,1024]{1,0:T(8,128)(2,1)S(1)}, u32[]{:S(2)}, u32[]{:S(2)}) collective-permute-start(bf16[64,1024]{1,0:T(8,128)(2,1)S(1)} %convert_element_type.109), channel_id=1, source_target_pairs={{0,0},{1,4},{2,8},{3,12},{4,16},{5,20},{6,24},{7,28},{8,1},{9,5},{... | collective-permute-start | bytes 393224 | tf_op jit(solution)/shard_map/ppermute | solution.py:723
  49.4 20.1 %collective-permute-start.4 = (bf16[64,1024]{1,0:T(8,128)(2,1)S(1)}, bf16[64,1024]{1,0:T(8,128)(2,1)S(1)}, u32[]{:S(2)}, u32[]{:S(2)}) collective-permute-start(bf16[64,1024]{1,0:T(8,128)(2,1)S(1)} %collective-permute-done.refs_0_), channel_id=1, source_target_pairs={{0,16},{4,20},{8,24},{12,28},{16,0},{20,4},{24,8},{28,12},{1,17},{... | collective-permute-start | bytes 393224 | tf_op jit(solution)/shard_map/ppermute | solution.py:648
  66.6 8.3 %collective-permute-start.2 = (bf16[64,1024]{1,0:T(8,128)(2,1)S(1)}, bf16[64,1024]{1,0:T(8,128)(2,1)S(1)}, u32[]{:S(2)}, u32[]{:S(2)}) collective-permute-start(bf16[64,1024]{1,0:T(8,128)(2,1)S(1)} %collective-permute-done.refs_0_), channel_id=1, source_target_pairs={{0,8},{4,12},{8,0},{12,4},{16,24},{20,28},{24,16},{28,20},{1,9},{5... | collective-permute-start | bytes 393224 | tf_op jit(solution)/shard_map/ppermute | solution.py:648
  69.4 6.6 %collective-permute-start.6 = (bf16[64,1024]{1,0:T(8,128)(2,1)S(1)}, bf16[64,1024]{1,0:T(8,128)(2,1)}, u32[]{:S(2)}, u32[]{:S(2)}) collective-permute-start(bf16[64,1024]{1,0:T(8,128)(2,1)S(1)} %collective-permute-done.4.refs_4_), channel_id=1, source_target_pairs={{0,8},{4,12},{8,0},{12,4},{16,24},{20,28},{24,16},{28,20},{1,9},{5... | collective-permute-start | bytes 393224 | tf_op jit(solution)/shard_map/ppermute | solution.py:648
  73.4 33.7 %collective-permute-start.1 = (bf16[64,1024]{1,0:T(8,128)(2,1)S(1)}, bf16[64,1024]{1,0:T(8,128)(2,1)}, u32[]{:S(2)}, u32[]{:S(2)}) collective-permute-start(bf16[64,1024]{1,0:T(8,128)(2,1)S(1)} %collective-permute-done.refs_0_), channel_id=1, source_target_pairs={{0,4},{4,0},{8,12},{12,8},{16,20},{20,16},{24,28},{28,24},{1,5},{5... | collective-permute-start | bytes 393224 | tf_op jit(solution)/shard_map/ppermute | solution.py:648
  73.6 33.5 %collective-permute-start.5 = (bf16[64,1024]{1,0:T(8,128)(2,1)S(1)}, bf16[64,1024]{1,0:T(8,128)(2,1)}, u32[]{:S(2)}, u32[]{:S(2)}) collective-permute-start(bf16[64,1024]{1,0:T(8,128)(2,1)S(1)} %collective-permute-done.4.refs_4_), channel_id=1, source_target_pairs={{0,4},{4,0},{8,12},{12,8},{16,20},{20,16},{24,28},{28,24},{1,5},{5... | collective-permute-start | bytes 393224 | tf_op jit(solution)/shard_map/ppermute | solution.py:648
  75.0 32.1 %collective-permute-start.3 = (bf16[64,1024]{1,0:T(8,128)(2,1)S(1)}, bf16[64,1024]{1,0:T(8,128)(2,1)}, u32[]{:S(2)}, u32[]{:S(2)}) collective-permute-start(bf16[64,1024]{1,0:T(8,128)(2,1)S(1)} %collective-permute-done.2.refs_2_), channel_id=1, source_target_pairs={{0,4},{4,0},{8,12},{12,8},{16,20},{20,16},{24,28},{28,24},{1,5},{5... | collective-permute-start | bytes 393224 | tf_op jit(solution)/shard_map/ppermute | solution.py:648
  76.0 31.1 %collective-permute-start.7 = (bf16[64,1024]{1,0:T(8,128)(2,1)}, bf16[64,1024]{1,0:T(8,128)(2,1)}, u32[]{:S(2)}, u32[]{:S(2)}) collective-permute-start(bf16[64,1024]{1,0:T(8,128)(2,1)} %collective-permute-done.6.refs_6_), channel_id=1, source_target_pairs={{0,4},{4,0},{8,12},{12,8},{16,20},{20,16},{24,28},{28,24},{1,5},{5... | collective-permute-start | bytes 393224 | tf_op jit(solution)/shard_map/ppermute | solution.py:648
  77.9 31.3 %all-to-all-start.1 = ((bf16[32,32,512]{2,1,0:T(8,128)(2,1)}), bf16[32,32,512]{2,1,0:T(8,128)(2,1)S(1)}, u32[]{:S(2)}, u32[]{:S(2)}) async-start(bf16[32,32,512]{2,1,0:T(8,128)(2,1)} %bitcast.112), calls=%async_computation.1 | async-start | bytes 2097152 | tf_op jit(solution)/shard_map/all_to_all | solution.py:743
  151.1 5.7 %collective-permute-start.8 = (bf16[2,512,1024]{2,1,0:T(8,128)(2,1)}, bf16[2,512,1024]{2,1,0:T(8,128)(2,1)}, u32[]{:S(2)}, u32[]{:S(2)}) collective-permute-start(bf16[2,512,1024]{2,1,0:T(8,128)(2,1)} %get-tuple-element.46), channel_id=1, source_target_pairs={{0,1},{1,0},{2,3},{3,2},{4,5},{5,4},{6,7},{7,6},{8,9},{9,8},{10,11... | collective-permute-start | bytes 6291464 | tf_op jit(solution)/shard_map/ppermute | solution.py:648
  151.3 30.5 %all-to-all-start.2 = ((bf16[8,64,1024]{2,1,0:T(8,128)(2,1)}), bf16[8,64,1024]{2,1,0:T(8,128)(2,1)S(1)}, u32[]{:S(2)}, u32[]{:S(2)}) async-start(bf16[8,64,1024]{2,1,0:T(8,128)(2,1)} %bitcast.105), calls=%async_computation.2 | async-start | bytes 2097152 | tf_op jit(solution)/shard_map/all_to_all | solution.py:783
  192.4 12.2 %collective-permute-start.10 = (bf16[1,512,1024]{2,1,0:T(8,128)(2,1)}, bf16[1,512,1024]{2,1,0:T(8,128)(2,1)}, u32[]{:S(2)}, u32[]{:S(2)}) collective-permute-start(bf16[1,512,1024]{2,1,0:T(8,128)(2,1)} %get-tuple-element.54), channel_id=1, source_target_pairs={{0,1},{1,0},{2,3},{3,2},{4,5},{5,4},{6,7},{7,6},{8,9},{9,8},{10,11... | collective-permute-start | bytes 3145736 | tf_op jit(solution)/shard_map/ppermute | solution.py:648
  197.1 48.2 %all-to-all-start.3 = ((bf16[32,32,512]{2,1,0:T(8,128)(2,1)}), bf16[32,32,512]{2,1,0:T(8,128)(2,1)}, u32[]{:S(2)}, u32[]{:S(2)}) async-start(bf16[32,32,512]{2,1,0:T(8,128)(2,1)} %bitcast.114), calls=%async_computation.3 | async-start | bytes 2097152 | tf_op jit(solution)/shard_map/all_to_all | solution.py:787
  201.2 52.4 %collective-permute-start.14 = (f32[64,1024]{1,0:T(8,128)}, f32[64,1024]{1,0:T(8,128)}, u32[]{:S(2)}, u32[]{:S(2)}) collective-permute-start(f32[64,1024]{1,0:T(8,128)} %convert_reduce_fusion.2), channel_id=1, source_target_pairs={{0,0},{4,1},{8,2},{12,3},{16,4},{20,5},{24,6},{28,7},{1,8},{5,9},{... | collective-permute-start | bytes 786440 | tf_op jit(solution)/shard_map/ppermute | solution.py:820
  247.7 4.1 %collective-permute-start.16 = (f32[48,128]{1,0:T(8,128)S(1)}, f32[48,128]{1,0:T(8,128)S(1)}, u32[]{:S(2)}, u32[]{:S(2)}) collective-permute-start(f32[48,128]{1,0:T(8,128)S(1)} %fusion.38), channel_id=1, source_target_pairs={{0,8},{4,12},{8,0},{12,4},{16,24},{20,28},{24,16},{28,20},{1,9},{5... | collective-permute-start | bytes 73736 | tf_op jit(solution)/shard_map/ppermute | solution.py:648
  249.3 78.7 %collective-permute-start.9 = (bf16[2,256,1024]{2,1,0:T(8,128)(2,1)S(1)}, bf16[2,256,1024]{2,1,0:T(8,128)(2,1)}, u32[]{:S(2)}, u32[]{:S(2)}) collective-permute-start(bf16[2,256,1024]{2,1,0:T(8,128)(2,1)S(1)} %copy-done.2), channel_id=1, source_target_pairs={{0,2},{1,3},{2,0},{3,1},{4,6},{5,7},{6,4},{7,5},{8,10},{9,11},{10,... | collective-permute-start | bytes 3145736 | tf_op jit(solution)/shard_map/ppermute | solution.py:648
  252.5 10.9 %collective-permute-start.17 = (f32[48,128]{1,0:T(8,128)}, f32[48,128]{1,0:T(8,128)S(1)}, u32[]{:S(2)}, u32[]{:S(2)}) collective-permute-start(f32[48,128]{1,0:T(8,128)} %fusion.47), channel_id=1, source_target_pairs={{0,16},{4,20},{8,24},{12,28},{16,0},{20,4},{24,8},{28,12},{1,17},{... | collective-permute-start | bytes 73736 | tf_op jit(solution)/shard_map/ppermute | solution.py:648
  255.6 60.1 %collective-permute-start.11 = (bf16[1,256,1024]{2,1,0:T(8,128)(2,1)}, bf16[1,256,1024]{2,1,0:T(8,128)(2,1)}, u32[]{:S(2)}, u32[]{:S(2)}) collective-permute-start(bf16[1,256,1024]{2,1,0:T(8,128)(2,1)} %add_convert_fusion.3.after_ref), channel_id=1, source_target_pairs={{0,2},{1,3},{2,0},{3,1},{4,6},{5,7},{6,4},{7,5},{8,10},{9,11},{10,... | collective-permute-start | bytes 1572872 | tf_op jit(solution)/shard_map/ppermute | solution.py:648
  256.4 75.6 %all-to-all-start.4 = ((bf16[32,32,896]{2,1,0:T(8,128)(2,1)}), bf16[32,32,896]{2,1,0:T(8,128)(2,1)}, u32[]{:S(2)}, u32[]{:S(2)}) async-start(bf16[32,32,896]{2,1,0:T(8,128)(2,1)} %bitcast.113), calls=%async_computation.4 | async-start | bytes 3670016 | tf_op jit(solution)/shard_map/all_to_all | solution.py:787
  262.9 48.2 %collective-permute-start.12 = (bf16[1,512,1024]{2,1,0:T(8,128)(2,1)}, bf16[1,512,1024]{2,1,0:T(8,128)(2,1)}, u32[]{:S(2)}, u32[]{:S(2)}) collective-permute-start(bf16[1,512,1024]{2,1,0:T(8,128)(2,1)} %copy-done.11), channel_id=1, source_target_pairs={{0,1},{1,0},{2,3},{3,2},{4,5},{5,4},{6,7},{7,6},{8,9},{9,8},{10,11... | collective-permute-start | bytes 3145736 | tf_op jit(solution)/shard_map/ppermute | solution.py:648
  312.6 13.4 %collective-permute-start.13 = (bf16[1,256,1024]{2,1,0:T(8,128)(2,1)S(1)}, bf16[1,256,1024]{2,1,0:T(8,128)(2,1)S(1)}, u32[]{:S(2)}, u32[]{:S(2)}) collective-permute-start(bf16[1,256,1024]{2,1,0:T(8,128)(2,1)S(1)} %add_convert_fusion.2), channel_id=1, source_target_pairs={{0,2},{1,3},{2,0},{3,1},{4,6},{5,7},{6,4},{7,5},{8,10},{9,11},{10,... | collective-permute-start | bytes 1572872 | tf_op jit(solution)/shard_map/ppermute | solution.py:648
  (45 other events, 370.2 us)
Sparse Core Ops, SparseCore 0:
  9.6 53.5 all-gather.6
  64.8 51.3 all-gather.4

commit v2 on v1

--- a/solution.py
+++ b/solution.py
@@ -2,9 +2,11 @@
 
 import jax
 import jax.numpy as jnp
+import numpy as np
 from jax import lax
 from jax.experimental import pallas as pl
 from jax.experimental.pallas import tpu as pltpu
+from jax.sharding import Mesh
 from jax.sharding import PartitionSpec as P
 
 D = 1024
@@ -124,21 +126,35 @@
 
 def forward_kernel(
     inner,
+    order_ref,
     tokens_ref,
     gain_ref,
-    weight_ref,
     taps_ref,
     heads_ref,
     skip_ref,
+    mine_ref,
+    other_ref,
     low_ref,
     rest_ref,
     mixed_ref,
     incoming_ref,
+    weight_ref,
     padded,
     state,
 ):
     rows = tokens_ref.shape[1]
     conv = inner + 2 * NS
+
+    @pl.when((pl.program_id(0) == 0) & (pl.program_id(1) == 0))
+    def _():
+        if mine_ref.shape[0] == D:
+            weight_ref[...] = mine_ref[...]
+        else:
+            mine = pl.multiple_of(order_ref[0] * (D // 2), D // 2)
+            other = pl.multiple_of((1 - order_ref[0]) * (D // 2), D // 2)
+            weight_ref[pl.ds(mine, D // 2), :] = mine_ref[...]
+            weight_ref[pl.ds(other, D // 2), :] = other_ref[...]
+
     @pl.when(pl.program_id(1) == 0)
     def _():
         padded[0:RIM, :] = jnp.zeros((RIM, conv), F32)
@@ -148,7 +164,8 @@
     def _():
         padded[0:RIM, :] = padded[rows : rows + RIM, :]
 
-    tokens = tokens_ref[0].astype(F32)
+    tokens_low = tokens_ref[0]
+    tokens = tokens_low.astype(F32)
     scale = lax.rsqrt(jnp.mean(tokens * tokens, axis=1, keepdims=True) + NORM_EPS)
     low = (tokens * scale * gain_ref[...]).astype(BF16)
     low_ref[0] = low
@@ -191,19 +208,30 @@
         )
 
 
-def stats_kernel(
-    place_ref, up_ref, low_ref, weight_gate_ref, mixed_ref, gain_ref, *refs
-):
-    *block_refs, gate_ref, d_out_ref, stats_ref, weight_ref = refs
-
-    @pl.when((pl.program_id(0) == 0) & (pl.program_id(1) == 0))
-    def _():
-        deep = block_refs[0].shape[0]
-        for k, block_ref in enumerate(block_refs):
-            start = pl.multiple_of((place_ref[0] ^ k) * deep, deep)
-            weight_ref[pl.ds(start, deep), :] = block_ref[...]
-
-    d_out = dot(up_ref[0], weight_ref[...], ROW_ROW)
+def stats_kernel(joined, order_ref, up_ref, low_ref, mixed_ref, gain_ref, *refs):
+    if joined:
+        both_ref, weight_out_ref, weight_gate_ref, gate_ref, d_out_ref, stats_ref = refs
+        inner = gate_ref.shape[2]
+
+        @pl.when((pl.program_id(0) == 0) & (pl.program_id(1) == 0))
+        def _():
+            deep, tall = D // 8, inner // 8
+            place = 0
+            for quarter in range(4):
+                for half in (order_ref[0], 1 - order_ref[0]):
+                    block = half * 4 + quarter
+                    rows = pl.ds(pl.multiple_of(block * deep, deep), deep)
+                    weight_gate_ref[rows, :] = both_ref[place : place + deep, :]
+                    place = place + deep
+                    rows = pl.ds(pl.multiple_of(block * tall, tall), tall)
+                    for k in range(D // inner):
+                        columns = slice(k * inner, (k + 1) * inner)
+                        weight_out_ref[rows, columns] = both_ref[place : place + tall, :]
+                        place = place + tall
+
+    else:
+        weight_out_ref, weight_gate_ref, gate_ref, d_out_ref, stats_ref = refs
+    d_out = dot(up_ref[0], weight_out_ref[...], ROW_ROW)
     d_out_ref[0] = d_out
     gate = dot(low_ref[0], weight_gate_ref[...])
     gate_ref[0] = gate
@@ -281,6 +309,7 @@
     heads_ref,
     skip_ref,
     after_ref,
+    before_ref,
     d_rest_ref,
     d_taps_ref,
     d_heads_ref,
@@ -441,74 +470,71 @@
     return jax.ShapeDtypeStruct(shape, dtype)
 
 
-def run_forward(tokens, norm_gain, weight, taps, heads, skip):
+def run_forward(order, tokens, norm_gain, halves, taps, heads, skip):
     count, length, _ = tokens.shape
     inner = skip.shape[1]
-    rest = weight.shape[1]
+    rest = halves[0].shape[1]
     conv = inner + 2 * NS
     chunks = ROWS // CHUNK
+    fixed = [norm_gain, taps, heads, skip, halves[0], halves[-1]]
     return pl.pallas_call(
         functools.partial(forward_kernel, inner),
-        grid=(count, length // ROWS),
-        in_specs=[
-            by_rows(D),
-            whole((1, D)),
-            whole((D, rest)),
-            whole((RIM, conv)),
-            whole((8, LANES)),
-            whole((1, inner)),
-        ],
-        out_specs=[
-            by_rows(D),
-            by_rows(rest),
-            by_rows(inner),
-            pl.BlockSpec((1, chunks, NS, inner), lambda s, b: (s, b, 0, 0)),
-        ],
+        grid_spec=pltpu.PrefetchScalarGridSpec(
+            num_scalar_prefetch=1,
+            grid=(count, length // ROWS),
+            in_specs=[by_rows(D)] + [whole(value.shape) for value in fixed],
+            out_specs=[
+                by_rows(D),
+                by_rows(rest),
+                by_rows(inner),
+                pl.BlockSpec((1, chunks, NS, inner), lambda s, b, *_: (s, b, 0, 0)),
+                whole((D, rest)),
+            ],
+            scratch_shapes=[pltpu.VMEM((RIM + ROWS, conv), F32), pltpu.VMEM((NS, inner), F32)],
+        ),
         out_shape=[
             shaped((count, length, D), BF16),
             shaped((count, length, rest)),
             shaped((count, length, inner)),
             shaped((count, length // CHUNK, NS, inner), BF16),
+            shaped((D, rest), BF16),
         ],
-        scratch_shapes=[pltpu.VMEM((RIM + ROWS, conv), F32), pltpu.VMEM((NS, inner), F32)],
         compiler_params=params(),
-        cost_estimate=cost(22),
+        cost_estimate=cost(1),
         name="forward_mixer",
-    )(tokens, norm_gain, weight, taps, heads, skip)
-
-
-def run_stats(place, upstream, low, weight_gate, mixed, gate_gain, blocks):
+    )(order, tokens, *fixed)
+
+
+def run_stats(order, upstream, low, mixed, gate_gain, weights):
     count, length, inner = mixed.shape
-    return pl.pallas_call(
-        stats_kernel,
+    joined = len(weights) == 1
+    found_specs = [whole((inner, D)), whole((D, inner))] * joined
+    found_shapes = [shaped((inner, D), BF16), shaped((D, inner), BF16)] * joined
+    found = pl.pallas_call(
+        functools.partial(stats_kernel, joined),
         grid_spec=pltpu.PrefetchScalarGridSpec(
             num_scalar_prefetch=1,
             grid=(count, length // ROWS),
-            in_specs=[
-                by_rows(D),
-                by_rows(D),
-                whole((D, inner)),
-                by_rows(inner),
-                whole((1, inner)),
-            ]
-            + [whole(block.shape) for block in blocks],
-            out_specs=[
+            in_specs=[by_rows(D), by_rows(D), by_rows(inner), whole((1, inner))]
+            + [whole(weight.shape) for weight in weights],
+            out_specs=found_specs
+            + [
                 by_rows(inner),
                 by_rows(inner),
                 pl.BlockSpec((1, 2, ROWS), lambda s, b, *_: (s, 0, b)),
-                whole((inner, D)),
             ],
         ),
-        out_shape=[
+        out_shape=found_shapes
+        + [
             shaped((count, length, inner)),
             shaped((count, length, inner)),
             shaped((count, 2, length)),
-            shaped((inner, D), BF16),
         ],
         compiler_params=params(),
-        cost_estimate=cost(11),
+        cost_estimate=cost(1),
         name="gate_stats",
-    )(place, upstream, low, weight_gate, mixed, gate_gain, *blocks)
+    )(order, upstream, low, mixed, gate_gain, *weights)
+    return found if joined else [*weights, *found]
 
 
 def kept_and_sent(split, count, length, place):
@@ -556,19 +582,19 @@
             shaped((1, inner)),
         ],
         compiler_params=params(),
-        cost_estimate=cost(13),
+        cost_estimate=cost(1),
         name="gate_back",
     )(order, upstream, weight, gate, mixed, gate_gain, d_out, stats)
 
 
-def run_mixer_back(s, rest, mixed, d_mixed, incoming, taps, heads, skip, after):
-    _, length, inner = mixed.shape
+def run_mixer_back(s, rest, mixed, d_mixed, incoming, taps, heads, skip, after, before):
+    count, length, inner = mixed.shape
     conv = inner + 2 * NS
     last = length // ROWS - 1
     chunks = ROWS // CHUNK
     width = rest.shape[2]
 
-    def rows(width, s=s):
+    def rows(width):
         return pl.BlockSpec((1, ROWS, width), lambda b: (s, last - b, 0))
 
     return pl.pallas_call(
@@ -587,8 +613,9 @@
             whole((8, LANES)),
             whole((1, inner)),
             left_alone(),
+            left_alone(),
         ],
-        out_specs=[rows(width, 0), whole((RIM, conv)), whole((8, LANES)), whole((1, inner))],
+        out_specs=[rows(width), whole((RIM, conv)), whole((8, LANES)), whole((1, inner))],
         scratch_shapes=[
             pltpu.VMEM((RIM + ROWS, conv), F32),
             pltpu.VMEM((RIM + ROWS, conv), F32),
@@ -596,15 +623,16 @@
             pltpu.VMEM((ROWS, conv), F32),
         ],
         out_shape=[
-            shaped((1, length, width), BF16),
+            shaped((count, length, width), BF16),
             shaped((RIM, conv)),
             shaped((8, LANES)),
             shaped((1, inner)),
         ],
+        input_output_aliases={9: 0} if s > 0 else {},
         compiler_params=params(),
-        cost_estimate=cost(19),
+        cost_estimate=cost(1),
         name="mixer_back",
-    )(rest, rest, mixed, d_mixed, incoming, taps, heads, skip, after)
+    )(rest, rest, mixed, d_mixed, incoming, taps, heads, skip, after, before)
 
 
 def run_norm_back(split, s, order, d_gate, d_rest, weight_gate, weight_rest, tokens, after):
@@ -625,7 +653,7 @@
             grid=(length // ROWS,),
             in_specs=[
                 rows(inner, s),
-                rows(width, 0),
+                rows(width, s),
                 whole(weight_gate.shape),
                 whole(weight_rest.shape),
                 rows(D, s),
@@ -635,27 +663,14 @@
         ),
         out_shape=shapes + [shaped((1, D))],
         compiler_params=params(),
-        cost_estimate=cost(6),
+        cost_estimate=cost(1),
         name="norm_back",
     )(order, d_gate, d_rest, weight_gate, weight_rest, tokens, after)
 
 
-BOTH = ("dp", "ctx")
-
-
-def swapped(value, axis, mask):
+def swapped(value, axis, mask=1):
     count = lax.axis_size(axis)
     return lax.ppermute(value, axis, [(a, a ^ mask) for a in range(count)])
-
-
-def gather_blocks(block):
-    if lax.axis_size("dp") != 8:
-        return [lax.all_gather(block, "dp", axis=0, tiled=True)]
-    far, near, side = (swapped(block, "dp", mask) for mask in (4, 2, 1))
-    far_near, far_side = swapped(far, "dp", 2), swapped(far, "dp", 1)
-    near_side = swapped(near, "dp", 1)
-    every = swapped(far_near, "dp", 1)
-    return [block, side, near, near_side, far, far_side, far_near, every]
 
 
 def chip_sums(parts):
@@ -674,12 +689,23 @@
     return own + swapped(sent, "ctx", 2).astype(F32)
 
 
-def sum_over_dp(value):
-    if lax.axis_size("dp") != 8:
-        return lax.psum(value, "dp")
-    for mask in (1, 2, 4):
-        value = value + swapped(value, "dp", mask)
+def sum_over(value, axes):
+    if len(axes) == 1:
+        return lax.psum(value, axes)
+    for axis in axes:
+        value = value + swapped(value, axis)
     return value
+
+
+def to_all(value, axes):
+    return lax.all_to_all(value, axes, split_axis=0, concat_axis=0, tiled=True)
+
+
+def to_every(value, axes):
+    times = 1
+    for axis in axes:
+        times = times * lax.axis_size(axis)
+    return to_all(jnp.broadcast_to(value[None], (times,) + value.shape).reshape(-1, value.shape[1]), axes)
 
 
 def adam_step(weight, first_old, second_old, gradient, step_rate):
@@ -698,6 +724,7 @@
 
 
 def shards(
+    dp,
     block_in,
     out_grad,
     w_in,
@@ -710,7 +737,8 @@
     small_m,
     small_v,
 ):
-    n_dp, n_ctx = lax.axis_size("dp"), lax.axis_size("ctx")
+    axes = dp + ("ctx",)
+    n_dp, n_ctx = lax.axis_size(dp), lax.axis_size("ctx")
     rank = lax.axis_index("ctx")
     heads = HEADS // n_ctx
     inner = heads * HD
@@ -720,7 +748,9 @@
     moves = []
     for block in range(n_dp * n_ctx):
         moves.append((block, (block % n_dp) * n_ctx + block // n_dp))
-    mine_out = lax.ppermute(w_out.astype(BF16), BOTH, moves)
+    mine_out = lax.ppermute(w_out.astype(BF16), axes, moves)
+    tokens = lax.all_gather(block_in, "ctx", axis=1, tiled=True)
+    upstream = lax.all_gather(out_grad, "ctx", axis=1, tiled=True)
     w_in_low = w_in.astype(BF16)
     slices = []
     for r in range(n_ctx):
@@ -731,22 +761,29 @@
                     w_in_low[:, DI + r * inner : DI + (r + 1) * inner],
                     w_in_low[:, 2 * DI : 2 * DI + 2 * NS],
                     pad_lanes(w_in_low[:, first : first + heads], LANES),
+                    w_in_low[:, r * inner : (r + 1) * inner],
                 ],
                 axis=1,
             )
         )
-
-    def to_ranks(slices):
-        stacked = jnp.stack(slices)
-        sent = jnp.broadcast_to(stacked[None], (n_dp,) + stacked.shape)
-        sent = sent.reshape(-1, stacked.shape[2])
-        return lax.all_to_all(sent, BOTH, split_axis=0, concat_axis=0, tiled=True)
-
-    tokens = lax.all_gather(block_in, "ctx", axis=1, tiled=True)
-    upstream = lax.all_gather(out_grad, "ctx", axis=1, tiled=True)
-    weight_rest = to_ranks(slices)
-    weight_gate = to_ranks([w_in_low[:, r * inner : (r + 1) * inner] for r in range(n_ctx)])
-    blocks_out = gather_blocks(mine_out)
+    rest = conv + LANES
+    mine_in = to_all(jnp.concatenate(slices, axis=0), "ctx")
+    mine_rest = mine_in[:, :rest]
+    if len(dp) > 1:
+        columns = [mine_out[:, k * inner : (k + 1) * inner] for k in range(D // inner)]
+        mine_both = jnp.concatenate([mine_in[:, rest:]] + columns, axis=0)
+        other_rest = swapped(mine_rest, dp[0])
+        other_both = swapped(mine_both, dp[0])
+        weight_halves = [to_every(mine_rest, dp[1:]), to_every(other_rest, dp[1:])]
+        both = jnp.concatenate([mine_both, other_both], axis=0)
+        both, *weight_halves = lax.optimization_barrier((both, *weight_halves))
+        weights = [to_every(both, dp[1:])]
+    else:
+        weight_halves = [lax.all_gather(mine_rest, dp, axis=0, tiled=True)]
+        weights = [
+            lax.all_gather(value, dp, axis=0, tiled=True)
+            for value in (mine_out, mine_in[:, rest:])
+        ]
 
     offset = 0
     pieces = []
@@ -767,46 +804,48 @@
     skip = jnp.repeat(lax.dynamic_slice(pieces[6], (rank * heads,), (heads,)), HD).reshape(1, inner)
 
     split = n_ctx == 4 and block_in.shape[1] == ROWS
-    place = lax.axis_index("dp") if len(blocks_out) > 1 else rank * 0
-    place = place.astype(jnp.int32).reshape(1)
     order = jnp.arange(n_ctx * block_in.shape[1] // ROWS, dtype=jnp.int32)
     if split:
         order = rank.astype(jnp.int32) ^ jnp.array([0, 2, 1, 3], jnp.int32)
-    low, rest, mixed, incoming = run_forward(tokens, norm_gain, weight_rest, taps, head_rows, skip)
-    gate, d_out, stats, weight_out = run_stats(
-        place, upstream, low, weight_gate, mixed, gate_gain, blocks_out
+    high = lax.axis_index(dp[0]) if len(dp) > 1 else rank * 0
+    high = high.astype(jnp.int32).reshape(1)
+    low, rest, mixed, incoming, weight_rest = run_forward(
+        high, tokens, norm_gain, weight_halves, taps, head_rows, skip
+    )
+    weight_out, weight_gate, gate, d_out, stats = run_stats(
+        high, upstream, low, mixed, gate_gain, weights
     )
     stats = lax.all_gather(stats, "ctx")
     *branch, grad_out, d_mixed, d_gate, d_gate_gain = run_gate_back(
         split, order, upstream, weight_out, gate, mixed, gate_gain, d_out, stats
     )
-    grad_out = lax.all_to_all(grad_out, "dp", split_axis=0, concat_axis=0, tiled=True)
+    grad_out = to_all(grad_out, dp)
     branch, branch_sent = chip_sums(branch)
 
-    def to_owners(grad):
-        return lax.all_to_all(grad.astype(BF16), BOTH, split_axis=0, concat_axis=0, tiled=True)
+    own_rows = w_in.shape[0]
 
     def summed(got):
-        return jnp.sum(got.astype(F32).reshape(n_dp, n_ctx, -1, got.shape[1]), axis=0)
+        return jnp.sum(got.astype(F32).reshape(-1, n_ctx, own_rows, got.shape[1]), axis=0)
 
     grad_gate = dot(low.reshape(-1, D), d_gate.reshape(-1, inner), COL_COL).astype(BF16)
     after = grad_gate if branch_sent is None else branch_sent
     branch = across_sums(branch, branch_sent)
-    grad_rest = 0.0
+    d_rest = after
     smalls = []
     normeds = []
     for s in range(count):
         d_rest, *small = run_mixer_back(
-            s, rest, mixed, d_mixed, incoming, taps, head_rows, skip, after
+            s, rest, mixed, d_mixed, incoming, taps, head_rows, skip, after, d_rest
         )
-        grad_rest = grad_rest + dot(low[s], d_rest[0], COL_COL)
+        after = grad_out
         if s == 0:
-            after = grad_out
-            grad_gate = to_owners(grad_gate)
+            grad_gate = to_all(grad_gate, axes)
         if s == count - 1:
-            grad_rest = grad_rest.astype(BF16)
-            after = grad_rest
-            grad_rest = to_owners(grad_rest)
+            grad_rest = dot(
+                low.reshape(-1, D), d_rest.reshape(-1, d_rest.shape[2]), COL_COL
+            ).astype(BF16)
+            after = grad_gate[:16, :LANES] + grad_rest[:16, :LANES]
+            grad_rest = to_all(grad_rest, axes)
         *d_normed, d_gain = run_norm_back(
             split, s, order, d_gate, d_rest, weight_gate, weight_rest, tokens, after
         )
@@ -817,7 +856,7 @@
     d_normed = jnp.concatenate(normeds, axis=0)
     d_norm_gain, d_taps, d_heads, d_skip = (sum(parts) for parts in zip(*smalls))
     grad_out = jnp.sum(grad_out.astype(F32).reshape(n_dp, -1, D), axis=0)
-    grad_out = lax.ppermute(grad_out, BOTH, [(b, a) for a, b in moves])
+    grad_out = lax.ppermute(grad_out, axes, [(b, a) for a, b in moves])
     grad_gate = summed(grad_gate)
     grad_rest = summed(grad_rest)
     columns = [grad_gate[r] for r in range(n_ctx)]
@@ -836,7 +875,7 @@
     )
     mine = jnp.concatenate(parts)
     mine = jnp.pad(mine, (0, -mine.shape[0] % (8 * LANES))).reshape(-1, LANES)
-    every = lax.all_gather(sum_over_dp(mine), "ctx", axis=0).reshape(n_ctx, -1)
+    every = lax.all_gather(sum_over(mine, dp), "ctx", axis=0).reshape(n_ctx, -1)
     offset = 0
     found = []
     for part in parts:
@@ -882,10 +921,14 @@
 
 
 def solution(mesh):
-    rows = P(("dp", "ctx"), None)
-    spread = P("dp", "ctx", None)
+    dp = ("dp",)
+    if mesh.shape["dp"] == 8 and mesh.shape["ctx"] == 4:
+        dp = ("high", "low", "side")
+        mesh = Mesh(np.asarray(mesh.devices).reshape(2, 2, 2, 4), dp + ("ctx",))
+    rows = P(dp + ("ctx",), None)
+    spread = P(dp, "ctx", None)
     return jax.shard_map(
-        shards,
+        functools.partial(shards, dp),
         mesh=mesh,
         in_specs=(spread, spread) + (rows,) * 6 + (P(),) * 3,
         out_specs=(spread, spread) + (rows,) * 6 + (P(),) * 3,

time: 348 us -> 340 us (0.977)
  starting transfers between devices: 70.7 us -> 53.7 us
  blocking collectives: 49.3 us -> 58.7 us
    ppermute x16 -> x11, starting transfers between devices: 35.4 us -> 13.7 us  [swapped(): return lax.ppermute(value, axis, [(a, a ^ mask) for a in range(count)])]
    ppermute x16 -> x11, waiting for transfers between devices: 10.8 us -> 30.7 us  [swapped(): return lax.ppermute(value, axis, [(a, a ^ mask) for a in range(count)])]
    ppermute x2, waiting for transfers between devices: 28 us -> 13 us  [the longest x1 13 us: shards(): mine_out = lax.ppermute(w_out.astype(BF16), axes, moves)]
    all_to_all x0 -> x1, blocking collectives: none -> 9.37 us  [to_all(): return lax.all_to_all(value, axes, split_axis=0, concat_axis=0, tiled=True)]
    all_gather x1, waiting for transfers between devices: 6.99 us -> 0.01 us  [shards(): upstream = lax.all_gather(out_grad, 'ctx', axis=1, tiled=True)]
    all_to_all x5 -> x6, starting transfers between devices: 27.6 us -> 31.9 us  [to_all(): return lax.all_to_all(value, axes, split_axis=0, concat_axis=0, tiled=True)]
    dot_general x3 -> x2, matrix products: 11.6 us -> 12.7 us  [dot(): lax.dot_general(a, b, (contract, ((), ())), preferred_element_type=F32)]
  transfers between devices with their start and end apart: 25 -> 21, of which waited for: 7 -> 7; matrix products, arithmetic and copies ran while one was open for 11% -> 11% of each run, Pallas kernels for 20% -> 20%
where the time goes in v2:
time: 340 us; the launch traced here: 337 us
  Pallas kernels  105 us (31%)
  blocking collectives  58.7 us (17%)
  starting transfers between devices  53.7 us (16%)
  waiting for transfers between devices  50.6 us (15%)
  other arithmetic  21.1 us (6%)
  local copies, waits for them, and re-layouts  20.5 us (6%)
  between operations  14.7 us (4%)
  matrix products  12.7 us (4%)
    all_gather x1, blocking collectives, shards(): every = lax.all_gather(sum_over(mine, dp), 'ctx', axis=0).reshape(n_ctx, -1)  45.3 us
    pallas_call x2, Pallas kernels, run_mixer_back(): pl.pallas_call(functools.partial(mixer_back_kernel, inner), grid=(length...  39.9 us
    all_to_all x6, starting transfers between devices, to_all(): return lax.all_to_all(value, axes, split_axis=0, concat_axis=0, tiled=True)  31.9 us
    ppermute x11, waiting for transfers between devices, swapped(): return lax.ppermute(value, axis, [(a, a ^ mask) for a in range(count)])  30.7 us
    pallas_call x1, Pallas kernels, run_forward(): pl.pallas_call(functools.partial(forward_kernel, inner), grid_spec=pltpu....  22 us
    pallas_call x1, Pallas kernels, run_gate_back(): pl.pallas_call(gate_back_kernel, grid_spec=pltpu.PrefetchScalarGridSpec(n...  16.5 us
    unnamed x85, local copies, waits for them, and re-layouts  14.9 us
    pallas_call x2, Pallas kernels, run_norm_back(): pl.pallas_call(norm_back_kernel, grid_spec=pltpu.PrefetchScalarGridSpec(n...  14 us
  transfers between devices with their start and end apart: 21, of which 7 were waited for; matrix products, arithmetic and copies ran while one was open for 11% of the time, Pallas kernels for 20%

profile of v2, /device:TPU:5, one launch (start us, length us, event | category | flops | bytes accessed | tf_op | source)
XLA Modules:
  0.0 336.6 jit_solution(1866661182438207734)
XLA Ops:
  8.9 9.4 %all_to_all.70 = bf16[4,32,1408]{2,1,0:T(8,128)(2,1)S(1)} all-to-all(bf16[4,32,1408]{2,1,0:T(8,128)(2,1)S(1)} %bitcast.83), channel_id=1, replica_groups=mesh['high'=2,'low'=2,'side'=2,'ctx'=4] {'ctx'}, dimensions={0} | all-to-all | bytes 720896 | tf_op jit(solution)/shard_map/all_to_all | solution.py:701
  19.3 3.9 %all-to-all-start.1 = ((bf16[4,128,896]{2,1,0:T(8,128)(2,1)}), bf16[4,128,896]{2,1,0:T(8,128)(2,1)S(1)}, u32[]{:S(2)}, u32[]{:S(2)}) async-start(bf16[4,128,896]{2,1,0:T(8,128)(2,1)} %broadcast_in_dim.12), calls=%async_computation.1 | async-start | bytes 1835008 | tf_op jit(solution)/shard_map/all_to_all | solution.py:701
  25.5 11.5 %collective-permute-done.2 = bf16[128,896]{1,0:T(8,128)(2,1)S(1)} collective-permute-done((bf16[128,896]{1,0:T(8,128)(2,1)S(1)}, bf16[128,896]{1,0:T(8,128)(2,1)S(1)}, u32[]{:S(2)}, u32[]{:S(2)}) %collective-permute-start.2) | collective-permute-done | bytes 229408 | tf_op jit(solution)/shard_map/ppermute | solution.py:673
  40.5 4.1 %all-to-all-start.2 = ((bf16[4,128,896]{2,1,0:T(8,128)(2,1)}), bf16[4,128,896]{2,1,0:T(8,128)(2,1)S(1)}, u32[]{:S(2)}, u32[]{:S(2)}) async-start(bf16[4,128,896]{2,1,0:T(8,128)(2,1)} %broadcast_in_dim.13), calls=%async_computation.2 | async-start | bytes 1835008 | tf_op jit(solution)/shard_map/all_to_all | solution.py:701
  44.6 4.7 %collective-permute-start = (bf16[64,1024]{1,0:T(8,128)(2,1)S(1)}, bf16[64,1024]{1,0:T(8,128)(2,1)S(1)}, u32[]{:S(2)}, u32[]{:S(2)}) collective-permute-start(bf16[64,1024]{1,0:T(8,128)(2,1)S(1)} %convert_element_type.109), channel_id=1, source_target_pairs={{0,0},{1,4},{2,8},{3,12},{4,16},{5,20},{6,24},{7,28},{8,1},{9,5},{... | collective-permute-start | bytes 393224 | tf_op jit(solution)/shard_map/ppermute | solution.py:751
  49.4 13.0 %collective-permute-done = bf16[64,1024]{1,0:T(8,128)(2,1)S(1)} collective-permute-done((bf16[64,1024]{1,0:T(8,128)(2,1)S(1)}, bf16[64,1024]{1,0:T(8,128)(2,1)S(1)}, u32[]{:S(2)}, u32[]{:S(2)}) %collective-permute-start) | collective-permute-done | bytes 131104 | tf_op jit(solution)/shard_map/ppermute | solution.py:751
  62.5 8.4 %collective-permute-done.1 = bf16[256,512]{1,0:T(8,128)(2,1)S(1)} collective-permute-done((bf16[256,512]{1,0:T(8,128)(2,1)S(1)}, bf16[256,512]{1,0:T(8,128)(2,1)S(1)}, u32[]{:S(2)}, u32[]{:S(2)}) %collective-permute-start.1) | collective-permute-done | bytes 262176 | tf_op jit(solution)/shard_map/ppermute | solution.py:673
  72.7 8.9 %all-to-all-start.3 = ((bf16[4,512,512]{2,1,0:T(8,128)(2,1)}), bf16[4,512,512]{2,1,0:T(8,128)(2,1)S(1)}, u32[]{:S(2)}, u32[]{:S(2)}) async-start(bf16[4,512,512]{2,1,0:T(8,128)(2,1)} %broadcast_in_dim.14), calls=%async_computation.3 | async-start | bytes 4194304 | tf_op jit(solution)/shard_map/all_to_all | solution.py:701
  83.4 22.0 %forward_mixer.1 = (bf16[2,1024,1024]{2,1,0:T(8,128)(2,1)}, f32[2,1024,896]{2,1,0:T(8,128)}, f32[2,1024,512]{2,1,0:T(8,128)}, bf16[2,8,128,512]{3,2,1,0:T(8,128)(2,1)S(1)}, bf16[1024,896]{1,0:T(8,128)(2,1)S(1)}) custom-call(s32[1]{0:T(128)} %bitcast.order_ref, bf16[2,1024,1024]{2,1,0:T(8,128)(2,1)} %all-gather.7.cloned.1.call-done.tokens_ref, ...), custom_call_target="tpu_custom_call" | custom-call | flops 1100000000 | bytes 2000000 | tf_op jit(solution)/shard_map/forward_mixer/pallas_call | solution.py:480
  108.0 12.2 %gate_stats.1 = (bf16[512,1024]{1,0:T(8,128)(2,1)S(1)}, bf16[1024,512]{1,0:T(8,128)(2,1)S(1)}, f32[2,1024,512]{2,1,0:T(8,128)}, f32[2,1024,512]{2,1,0:T(8,128)}, f32[2,2,1024]{2,1,0:T(2,128)S(1)}) custom-call(s32[1]{0:T(128)} %bitcast.order_ref, bf16[2,1024,1024]{2,1,0:T(8,128)(2,1)} %all-gather.5.cloned.1.call-done.up_ref, ...), custom_call_target="tpu_custom_call" | custom-call | flops 1100000000 | bytes 2000000 | tf_op jit(solution)/shard_map/gate_stats/pallas_call | solution.py:513
  120.2 4.1 %all-gather = f32[8,2,1024]{2,1,0:T(2,128)S(1)} all-gather(f32[2,2,1024]{2,1,0:T(2,128)S(1)} %get-tuple-element.52), channel_id=2, replica_groups=mesh['high'=2,'low'=2,'side'=2,'ctx'=4] {'ctx'}, dimensions={0}, use_global_device_ids=true | all-gather | bytes 81920 | tf_op jit(solution)/shard_map/all_gather | solution.py:818
  124.3 16.5 %gate_back.1 = (bf16[2,512,1024]{2,1,0:T(8,128)(2,1)S(1)}, bf16[2,512,1024]{2,1,0:T(8,128)(2,1)}, bf16[512,1024]{1,0:T(8,128)(2,1)}, f32[2,1024,512]{2,1,0:T(8,1...) custom-call(s32[4]{0:T(128)S(1)} %broadcast_xor_fusion.order_ref, ...), custom_call_target="tpu_custom_call" | custom-call | flops 1100000000 | bytes 2000000 | tf_op jit(solution)/shard_map/gate_back/pallas_call | solution.py:557
  142.5 4.7 %all-to-all-start.4 = ((bf16[8,64,1024]{2,1,0:T(8,128)(2,1)}), bf16[8,64,1024]{2,1,0:T(8,128)(2,1)S(1)}, u32[]{:S(2)}, u32[]{:S(2)}) async-start(bf16[8,64,1024]{2,1,0:T(8,128)(2,1)} %bitcast.11), calls=%async_computation.4 | async-start | bytes 2097152 | tf_op jit(solution)/shard_map/all_to_all | solution.py:701
  149.4 19.9 %mixer_back.2 = (bf16[2,1024,896]{2,1,0:T(8,128)(2,1)}, f32[8,768]{1,0:T(8,128)S(1)}, f32[8,128]{1,0:T(8,128)S(1)}, f32[1,512]{1,0:T(1,128)S(1)}) custom-call(f32[2,1024,896]{2,1,0:T(8,128)} %get-tuple-element.56.rest_ref.rim_ref, f32[2,1024,896]{2,1,0:T(8,128)} %get-tuple-element.56.rest_ref.rim_ref, f32[2,1024,512]{2,1,0:T(8,128)} %get-tuple-element.47.mixed_ref, ...), custom_call_target="tpu_custom_call" | custom-call | flops 1100000000 | bytes 2000000 | tf_op jit(solution)/shard_map/mixer_back/pallas_call | solution.py:600
  173.7 7.6 %norm_back.2 = (bf16[1,512,1024]{2,1,0:T(8,128)(2,1)S(1)}, bf16[1,512,1024]{2,1,0:T(8,128)(2,1)}, f32[1,1024]{1,0:T(1,128)S(1)}) custom-call(s32[4]{0:T(128)S(1)} %broadcast_xor_fusion.order_ref, bf16[2,1024,512]{2,1,0:T(8,128)(2,1)} %get-tuple-element.55.d_gate_ref, bf16[2,1024,896]{2,1,0:T(8,128)(2,1)} %get-tuple-element.59.d_rest_ref.before_ref, ...), custom_call_target="tpu_custom_call" | custom-call | flops 1100000000 | bytes 2000000 | tf_op jit(solution)/shard_map/norm_back/pallas_call | solution.py:649
  183.6 3.4 %bitcast_convert_fusion.1 = bf16[1024,512]{1,0:T(8,128)(2,1)} fusion(bf16[2,1024,1024]{2,1,0:T(8,128)(2,1)S(1)} %copy-done.19, bf16[2,1024,512]{2,1,0:T(8,128)(2,1)S(1)} %copy-done.18), kind=kOutput, calls=%fused_computation.17 | convolution fusion | flops 2148007936 | bytes 7340032 | tf_op jit(solution)/shard_map/dot_general | solution.py:40
  187.1 4.3 %all-to-all-start.5 = ((bf16[32,32,512]{2,1,0:T(8,128)(2,1)}), bf16[32,32,512]{2,1,0:T(8,128)(2,1)}, u32[]{:S(2)}, u32[]{:S(2)}) async-start(bf16[32,32,512]{2,1,0:T(8,128)(2,1)} %bitcast.84), calls=%async_computation.5 | async-start | bytes 2097152 | tf_op jit(solution)/shard_map/all_to_all | solution.py:701
  198.0 19.9 %mixer_back.3 = (bf16[2,1024,896]{2,1,0:T(8,128)(2,1)}, f32[8,768]{1,0:T(8,128)S(1)}, f32[8,128]{1,0:T(8,128)S(1)}, f32[1,512]{1,0:T(1,128)S(1)}) custom-call(f32[2,1024,896]{2,1,0:T(8,128)} %get-tuple-element.56.rest_ref.rim_ref, f32[2,1024,896]{2,1,0:T(8,128)} %get-tuple-element.56.rest_ref.rim_ref, ...), custom_call_target="tpu_custom_call", output_to_operand_aliasing={{0}: (9, {})} | custom-call | flops 1100000000 | bytes 2000000 | tf_op jit(solution)/shard_map/mixer_back/pallas_call | solution.py:600
  218.2 9.2 %bitcast_convert_fusion = bf16[1024,896]{1,0:T(8,128)(2,1)} fusion(bf16[2,1024,1024]{2,1,0:T(8,128)(2,1)} %get-tuple-element.46.low_ref, bf16[2,1024,896]{2,1,0:T(8,128)(2,1)} %get-tuple-element.65.d_rest_ref), kind=kOutput, calls=%fused_computation.1 | convolution fusion | flops 3759013888 | bytes 9699328 | tf_op jit(solution)/shard_map/dot_general | solution.py:40
  229.3 6.4 %norm_back.3 = (bf16[1,512,1024]{2,1,0:T(8,128)(2,1)S(1)}, bf16[1,512,1024]{2,1,0:T(8,128)(2,1)S(1)}, f32[1,1024]{1,0:T(1,128)S(1)}) custom-call(s32[4]{0:T(128)S(1)} %broadcast_xor_fusion.order_ref, bf16[2,1024,512]{2,1,0:T(8,128)(2,1)} %get-tuple-element.55.d_gate_ref, bf16[2,1024,896]{2,1,0:T(8,128)(2,1)} %get-tuple-element.65.d_rest_ref, ...), custom_call_target="tpu_custom_call" | custom-call | flops 1100000000 | bytes 2000000 | tf_op jit(solution)/shard_map/norm_back/pallas_call | solution.py:649
  250.6 6.0 %all-to-all-start.6 = ((bf16[32,32,896]{2,1,0:T(8,128)(2,1)}), bf16[32,32,896]{2,1,0:T(8,128)(2,1)}, u32[]{:S(2)}, u32[]{:S(2)}) async-start(bf16[32,32,896]{2,1,0:T(8,128)(2,1)} %bitcast.22), calls=%async_computation.6 | async-start | bytes 3670016 | tf_op jit(solution)/shard_map/all_to_all | solution.py:701
  257.0 45.3 %all-gather.1 = f32[192,128]{1,0:T(8,128)S(1)} all-gather(f32[48,128]{1,0:T(8,128)S(1)} %add.171), channel_id=3, replica_groups=mesh['high'=2,'low'=2,'side'=2,'ctx'=4] {'ctx'}, dimensions={0}, use_global_device_ids=true | all-gather | bytes 122880 | tf_op jit(solution)/shard_map/all_gather | solution.py:878
  308.1 9.8 %collective-permute-done.8 = bf16[1,256,1024]{2,1,0:T(8,128)(2,1)S(1)} collective-permute-done((bf16[1,256,1024]{2,1,0:T(8,128)(2,1)S(1)}, bf16[1,256,1024]{2,1,0:T(8,128)(2,1)S(1)}, u32[]{:S(2)}, u32[]{:S(2)}) %collective-permute-start.8) | collective-permute-done | bytes 524320 | tf_op jit(solution)/shard_map/ppermute | solution.py:673
  321.1 3.4 %fusion.7 = (bf16[2,256,1024]{2,1,0:T(8,128)(2,1)}, bf16[2,256,1024]{2,1,0:T(8,128)(2,1)}) fusion(bf16[2,256,1024]{2,1,0:T(8,128)(2,1)S(1)} %copy-done.17, bf16[2,256,1024]{2,1,0:T(8,128)(2,1)S(1)} %copy-done.20, f32[1,256,1024]{2,1,0:T(8,128)S(1)} %convert_add_fusion.1, f32[1,256,1024]{2,1,0:T(8,128)S(1)} %convert_add_fusion.2, ...), kind=kLoop, calls=%fused_computation.13 | loop fusion | flops 9437184 | bytes 9445376 | tf_op jit(solution)/shard_map/convert_element_type | solution.py:904
  (199 shorter events, 63.2 us)
Async XLA Ops:
  7.2 75.1 %all-gather.7.cloned.1.call-start = ((), (), s32[]{:S(2)}) async-start(), calls=%async_computation.8 | async-start | bytes 5242880 | tf_op jit(solution)/shard_map/all_gather | solution.py:752
  7.9 100.1 %all-gather.5.cloned.1.call-start = ((), (), s32[]{:S(2)}) async-start(), calls=%async_computation.7 | async-start | bytes 5242880 | tf_op jit(solution)/shard_map/all_gather | solution.py:753
  19.3 20.2 %all-to-all-start.1 = ((bf16[4,128,896]{2,1,0:T(8,128)(2,1)}), bf16[4,128,896]{2,1,0:T(8,128)(2,1)S(1)}, u32[]{:S(2)}, u32[]{:S(2)}) async-start(bf16[4,128,896]{2,1,0:T(8,128)(2,1)} %broadcast_in_dim.12), calls=%async_computation.1 | async-start | bytes 1835008 | tf_op jit(solution)/shard_map/all_to_all | solution.py:701
  23.2 13.8 %collective-permute-start.2 = (bf16[128,896]{1,0:T(8,128)(2,1)S(1)}, bf16[128,896]{1,0:T(8,128)(2,1)S(1)}, u32[]{:S(2)}, u32[]{:S(2)}) collective-permute-start(bf16[128,896]{1,0:T(8,128)(2,1)S(1)} %slice.272), channel_id=1, source_target_pairs={{0,16},{16,0},{1,17},{17,1},{2,18},{18,2},{3,19},{19,3},{4,20},{20... | collective-permute-start | bytes 688136 | tf_op jit(solution)/shard_map/ppermute | solution.py:673
  40.5 30.5 %all-to-all-start.2 = ((bf16[4,128,896]{2,1,0:T(8,128)(2,1)}), bf16[4,128,896]{2,1,0:T(8,128)(2,1)S(1)}, u32[]{:S(2)}, u32[]{:S(2)}) async-start(bf16[4,128,896]{2,1,0:T(8,128)(2,1)} %broadcast_in_dim.13), calls=%async_computation.2 | async-start | bytes 1835008 | tf_op jit(solution)/shard_map/all_to_all | solution.py:701
  44.6 17.8 %collective-permute-start = (bf16[64,1024]{1,0:T(8,128)(2,1)S(1)}, bf16[64,1024]{1,0:T(8,128)(2,1)S(1)}, u32[]{:S(2)}, u32[]{:S(2)}) collective-permute-start(bf16[64,1024]{1,0:T(8,128)(2,1)S(1)} %convert_element_type.109), channel_id=1, source_target_pairs={{0,0},{1,4},{2,8},{3,12},{4,16},{5,20},{6,24},{7,28},{8,1},{9,5},{... | collective-permute-start | bytes 393224 | tf_op jit(solution)/shard_map/ppermute | solution.py:751
  62.5 8.5 %collective-permute-start.1 = (bf16[256,512]{1,0:T(8,128)(2,1)S(1)}, bf16[256,512]{1,0:T(8,128)(2,1)S(1)}, u32[]{:S(2)}, u32[]{:S(2)}) collective-permute-start(bf16[256,512]{1,0:T(8,128)(2,1)S(1)} %pad_maximum_fusion.1), channel_id=1, source_target_pairs={{0,16},{16,0},{1,17},{17,1},{2,18},{18,2},{3,19},{19,3},{4,20},{20... | collective-permute-start | bytes 786440 | tf_op jit(solution)/shard_map/ppermute | solution.py:673
  72.7 35.4 %all-to-all-start.3 = ((bf16[4,512,512]{2,1,0:T(8,128)(2,1)}), bf16[4,512,512]{2,1,0:T(8,128)(2,1)S(1)}, u32[]{:S(2)}, u32[]{:S(2)}) async-start(bf16[4,512,512]{2,1,0:T(8,128)(2,1)} %broadcast_in_dim.14), calls=%async_computation.3 | async-start | bytes 4194304 | tf_op jit(solution)/shard_map/all_to_all | solution.py:701
  120.2 52.0 %copy-start.6 = (bf16[1024,512]{1,0:T(8,128)(2,1)}, bf16[1024,512]{1,0:T(8,128)(2,1)S(1)}, u32[]{:S(2)}) copy-start(bf16[1024,512]{1,0:T(8,128)(2,1)S(1)} %get-tuple-element.60.weight_gate_ref) | copy-start | bytes 3145732
  142.1 5.0 %collective-permute-start.3 = (bf16[2,512,1024]{2,1,0:T(8,128)(2,1)}, bf16[2,512,1024]{2,1,0:T(8,128)(2,1)}, u32[]{:S(2)}, u32[]{:S(2)}) collective-permute-start(bf16[2,512,1024]{2,1,0:T(8,128)(2,1)} %get-tuple-element.54), channel_id=1, source_target_pairs={{0,1},{1,0},{2,3},{3,2},{4,5},{5,4},{6,7},{7,6},{8,9},{9,8},{10,11... | collective-permute-start | bytes 6291464 | tf_op jit(solution)/shard_map/ppermute | solution.py:673
  142.5 29.7 %all-to-all-start.4 = ((bf16[8,64,1024]{2,1,0:T(8,128)(2,1)}), bf16[8,64,1024]{2,1,0:T(8,128)(2,1)S(1)}, u32[]{:S(2)}, u32[]{:S(2)}) async-start(bf16[8,64,1024]{2,1,0:T(8,128)(2,1)} %bitcast.11), calls=%async_computation.4 | async-start | bytes 2097152 | tf_op jit(solution)/shard_map/all_to_all | solution.py:701
  182.2 13.4 %collective-permute-start.5 = (bf16[1,512,1024]{2,1,0:T(8,128)(2,1)}, bf16[1,512,1024]{2,1,0:T(8,128)(2,1)S(1)}, u32[]{:S(2)}, u32[]{:S(2)}) collective-permute-start(bf16[1,512,1024]{2,1,0:T(8,128)(2,1)} %get-tuple-element.64), channel_id=1, source_target_pairs={{0,1},{1,0},{2,3},{3,2},{4,5},{5,4},{6,7},{7,6},{8,9},{9,8},{10,11... | collective-permute-start | bytes 3145736 | tf_op jit(solution)/shard_map/ppermute | solution.py:673
  187.1 40.4 %all-to-all-start.5 = ((bf16[32,32,512]{2,1,0:T(8,128)(2,1)}), bf16[32,32,512]{2,1,0:T(8,128)(2,1)}, u32[]{:S(2)}, u32[]{:S(2)}) async-start(bf16[32,32,512]{2,1,0:T(8,128)(2,1)} %bitcast.84), calls=%async_computation.5 | async-start | bytes 2097152 | tf_op jit(solution)/shard_map/all_to_all | solution.py:701
  192.3 54.4 %collective-permute-start.9 = (f32[64,1024]{1,0:T(8,128)}, f32[64,1024]{1,0:T(8,128)}, u32[]{:S(2)}, u32[]{:S(2)}) collective-permute-start(f32[64,1024]{1,0:T(8,128)} %convert_reduce_fusion.2), channel_id=1, source_target_pairs={{0,0},{4,1},{8,2},{12,3},{16,4},{20,5},{24,6},{28,7},{1,8},{5,9},{... | collective-permute-start | bytes 786440 | tf_op jit(solution)/shard_map/ppermute | solution.py:859
  237.9 3.7 %collective-permute-start.10 = (f32[48,128]{1,0:T(8,128)S(1)}, f32[48,128]{1,0:T(8,128)S(1)}, u32[]{:S(2)}, u32[]{:S(2)}) collective-permute-start(f32[48,128]{1,0:T(8,128)S(1)} %pad_bitcast_fusion), channel_id=1, source_target_pairs={{0,16},{16,0},{1,17},{17,1},{2,18},{18,2},{3,19},{19,3},{4,20},{20... | collective-permute-start | bytes 73736 | tf_op jit(solution)/shard_map/ppermute | solution.py:673
  241.5 4.6 %collective-permute-start.11 = (f32[48,128]{1,0:T(8,128)S(1)}, f32[48,128]{1,0:T(8,128)S(1)}, u32[]{:S(2)}, u32[]{:S(2)}) collective-permute-start(f32[48,128]{1,0:T(8,128)S(1)} %fusion.43), channel_id=1, source_target_pairs={{0,8},{8,0},{1,9},{9,1},{2,10},{10,2},{3,11},{11,3},{4,12},{12,4},... | collective-permute-start | bytes 73736 | tf_op jit(solution)/shard_map/ppermute | solution.py:673
  243.3 76.4 %collective-permute-start.4 = (bf16[2,256,1024]{2,1,0:T(8,128)(2,1)S(1)}, bf16[2,256,1024]{2,1,0:T(8,128)(2,1)}, u32[]{:S(2)}, u32[]{:S(2)}) collective-permute-start(bf16[2,256,1024]{2,1,0:T(8,128)(2,1)S(1)} %add_convert_fusion.after_ref.before_ref), channel_id=1, source_target_pairs={{0,2},{1,3},{2,0},{3,1},{4,6},{5,7},{6,4},{7,5},{8,10},{9,11},{10,... | collective-permute-start | bytes 3145736 | tf_op jit(solution)/shard_map/ppermute | solution.py:673
  246.1 10.9 %collective-permute-start.12 = (f32[48,128]{1,0:T(8,128)S(1)}, f32[48,128]{1,0:T(8,128)S(1)}, u32[]{:S(2)}, u32[]{:S(2)}) collective-permute-start(f32[48,128]{1,0:T(8,128)S(1)} %fusion.56), channel_id=1, source_target_pairs={{0,4},{4,0},{1,5},{5,1},{2,6},{6,2},{3,7},{7,3},{8,12},{12,8},{9,1... | collective-permute-start | bytes 73736 | tf_op jit(solution)/shard_map/ppermute | solution.py:673
  248.7 58.0 %collective-permute-start.6 = (bf16[1,256,1024]{2,1,0:T(8,128)(2,1)S(1)}, bf16[1,256,1024]{2,1,0:T(8,128)(2,1)}, u32[]{:S(2)}, u32[]{:S(2)}) collective-permute-start(bf16[1,256,1024]{2,1,0:T(8,128)(2,1)S(1)} %add_convert_fusion.2.after_ref), channel_id=1, source_target_pairs={{0,2},{1,3},{2,0},{3,1},{4,6},{5,7},{6,4},{7,5},{8,10},{9,11},{10,... | collective-permute-start | bytes 1572872 | tf_op jit(solution)/shard_map/ppermute | solution.py:673
  250.6 73.9 %all-to-all-start.6 = ((bf16[32,32,896]{2,1,0:T(8,128)(2,1)}), bf16[32,32,896]{2,1,0:T(8,128)(2,1)}, u32[]{:S(2)}, u32[]{:S(2)}) async-start(bf16[32,32,896]{2,1,0:T(8,128)(2,1)} %bitcast.22), calls=%async_computation.6 | async-start | bytes 3670016 | tf_op jit(solution)/shard_map/all_to_all | solution.py:701
  256.6 49.4 %copy-start.36 = (f32[14688]{0:T(1024)S(1)}, f32[14688]{0:T(1024)}, u32[]{:S(2)}) copy-start(f32[14688]{0:T(1024)} %param.20) | copy-start | bytes 176260
  256.6 50.1 %copy-start.13 = (bf16[1,512,1024]{2,1,0:T(8,128)(2,1)S(1)}, bf16[1,512,1024]{2,1,0:T(8,128)(2,1)}, u32[]{:S(2)}) copy-start(bf16[1,512,1024]{2,1,0:T(8,128)(2,1)} %copy-done.12) | copy-start | bytes 3145732
  256.6 46.3 %collective-permute-start.7 = (bf16[1,512,1024]{2,1,0:T(8,128)(2,1)}, bf16[1,512,1024]{2,1,0:T(8,128)(2,1)}, u32[]{:S(2)}, u32[]{:S(2)}) collective-permute-start(bf16[1,512,1024]{2,1,0:T(8,128)(2,1)} %copy-done.16), channel_id=1, source_target_pairs={{0,1},{1,0},{2,3},{3,2},{4,5},{5,4},{6,7},{7,6},{8,9},{9,8},{10,11... | collective-permute-start | bytes 3145736 | tf_op jit(solution)/shard_map/ppermute | solution.py:673
  304.5 13.4 %collective-permute-start.8 = (bf16[1,256,1024]{2,1,0:T(8,128)(2,1)S(1)}, bf16[1,256,1024]{2,1,0:T(8,128)(2,1)S(1)}, u32[]{:S(2)}, u32[]{:S(2)}) collective-permute-start(bf16[1,256,1024]{2,1,0:T(8,128)(2,1)S(1)} %add_convert_fusion.1), channel_id=1, source_target_pairs={{0,2},{1,3},{2,0},{3,1},{4,6},{5,7},{6,4},{7,5},{8,10},{9,11},{10,... | collective-permute-start | bytes 1572872 | tf_op jit(solution)/shard_map/ppermute | solution.py:673
  (41 other events, 308.1 us)
Sparse Core Ops, SparseCore 0:
  9.6 36.0 all-gather.6
  47.3 34.4 all-gather.4

commit v3 on v2

--- a/solution.py
+++ b/solution.py
@@ -232,7 +232,7 @@
     else:
         weight_out_ref, weight_gate_ref, gate_ref, d_out_ref, stats_ref = refs
     d_out = dot(up_ref[0], weight_out_ref[...], ROW_ROW)
-    d_out_ref[0] = d_out
+    d_out_ref[0] = d_out.astype(BF16)
     gate = dot(low_ref[0], weight_gate_ref[...])
     gate_ref[0] = gate
     gated = mixed_ref[0] * gate * sigmoid(gate)
@@ -259,9 +259,19 @@
 
 
 def gate_back_kernel(
-    order_ref, up_ref, weight_ref, gate_ref, mixed_ref, gain_ref, d_out_ref, stats_ref, *refs
+    order_ref,
+    up_ref,
+    weight_ref,
+    gate_ref,
+    mixed_ref,
+    gain_ref,
+    d_out_ref,
+    stats_ref,
+    low_ref,
+    *refs,
 ):
-    *branch_refs, grad_ref, d_mixed_ref, d_gate_ref, d_gain_ref, total = refs
+    *branch_refs, grad_ref, grad_gate_ref, d_mixed_ref, d_gate_ref, d_gain_ref = refs[:-2]
+    total, total_gate = refs[-2:]
     first = (pl.program_id(0) == 0) & (pl.program_id(1) == 0)
     last_one = pl.program_id(0) == pl.num_programs(0) - 1
     last_two = pl.program_id(1) == pl.num_programs(1) - 1
@@ -269,6 +279,7 @@
     @pl.when(first)
     def _():
         total[...] = jnp.zeros_like(total)
+        total_gate[...] = jnp.zeros_like(total_gate)
         d_gain_ref[...] = jnp.zeros_like(d_gain_ref)
 
     stats = stats_ref[0, 0]
@@ -280,7 +291,7 @@
     gate = gate_ref[0]
     mixed = mixed_ref[0]
     gain = gain_ref[...]
-    d_out = d_out_ref[0]
+    d_out = d_out_ref[0].astype(F32)
     sig = sigmoid(gate)
     silu = gate * sig
     gated = mixed * silu
@@ -290,16 +301,20 @@
     total[...] += dot(low, up_ref[0], COL_COL)
     d_gain_ref[...] += jnp.sum(d_out * unit, axis=0, keepdims=True)
     d_gated = scale * (gain * d_out - unit * (scale * products * (1.0 / DI)))
-    d_mixed_ref[0] = d_gated * silu
-    d_gate_ref[0] = (d_gated * mixed * (sig + silu * (1.0 - sig))).astype(BF16)
+    d_mixed_ref[0] = (d_gated * silu).astype(BF16)
+    d_gate = (d_gated * mixed * (sig + silu * (1.0 - sig))).astype(BF16)
+    d_gate_ref[0] = d_gate
+    total_gate[...] += dot(low_ref[0], d_gate, COL_COL)
 
     @pl.when(last_one & last_two)
     def _():
         grad_ref[...] = total[...].astype(BF16)
+        grad_gate_ref[...] = total_gate[...].astype(BF16)
 
 
 def mixer_back_kernel(
     inner,
+    first,
     rest_ref,
     rim_ref,
     mixed_ref,
@@ -308,9 +323,12 @@
     taps_ref,
     heads_ref,
     skip_ref,
+    low_ref,
     after_ref,
     before_ref,
+    part_ref,
     d_rest_ref,
+    grad_ref,
     d_taps_ref,
     d_heads_ref,
     d_skip_ref,
@@ -318,6 +336,7 @@
     later,
     carried,
     d_active,
+    total,
 ):
     rows = rest_ref.shape[1]
     conv = inner + 2 * NS
@@ -328,6 +347,10 @@
         d_taps_ref[...] = jnp.zeros_like(d_taps_ref)
         d_heads_ref[...] = jnp.zeros_like(d_heads_ref)
         d_skip_ref[...] = jnp.zeros_like(d_skip_ref)
+        if first:
+            total[...] = jnp.zeros_like(total)
+        else:
+            pltpu.sync_copy(part_ref, total)
         carried[...] = jnp.zeros_like(carried)
         later[rows : rows + RIM, :] = jnp.zeros((RIM, conv), F32)
 
@@ -362,8 +385,8 @@
         stepped = values * step_x
         stepped_low = stepped.astype(BF16)
         scores = dot(out_c, in_b, ROW_ROW) * tri
-        d_mixed = d_mixed_ref[0, part, :]
-        d_low = d_mixed.astype(BF16)
+        d_low = d_mixed_ref[0, part, :]
+        d_mixed = d_low.astype(F32)
         d_scores = jnp.zeros((CHUNK, CHUNK), F32)
         inside = []
         for pair in range(inner // LANES):
@@ -385,7 +408,7 @@
         d_out_c = dot(outer, before, ROW_ROW) + dot(d_scores_low, in_b)
         d_stepped = jnp.concatenate(inside, axis=1) + through
         stepped_near = stepped_low.astype(F32)
-        both = d_low.astype(F32) * (mixed_ref[0, part, :] - skip * values)
+        both = d_mixed * (mixed_ref[0, part, :] - skip * values)
         d_cum_x = both - stepped_near * d_stepped
         d_step_x = d_stepped * values
         grown_total = grown[CHUNK - 1 : CHUNK, :]
@@ -418,6 +441,11 @@
         )
     d_taps_ref[KCONV : KCONV + 1, :] += jnp.sum(d_conv_out, axis=0, keepdims=True)
     d_rest_ref[0, :, :conv] = d_conv_in.astype(BF16)
+    total[...] += dot(low_ref[0], d_rest_ref[0], COL_COL)
+
+    @pl.when(block == 0)
+    def _():
+        grad_ref[...] = total[...].astype(grad_ref.dtype)
 
 
 def norm_back_kernel(
@@ -527,7 +555,7 @@
         out_shape=found_shapes
         + [
             shaped((count, length, inner)),
-            shaped((count, length, inner)),
+            shaped((count, length, inner), BF16),
             shaped((count, 2, length)),
         ],
         compiler_params=params(),
@@ -547,7 +575,7 @@
     return specs, [shaped((count, 2 * ROWS, D), BF16)] * 2
 
 
-def run_gate_back(split, order, upstream, weight, gate, mixed, gate_gain, d_out, stats):
+def run_gate_back(split, order, upstream, weight, gate, mixed, gate_gain, d_out, stats, low):
     count, length, inner = gate.shape
 
     def place(group):
@@ -569,25 +597,33 @@
                 pl.BlockSpec(
                     (stats.shape[0], 1, 2, ROWS), lambda s, b, order: (0, s, 0, order[b])
                 ),
+                by_order(D),
             ],
             out_specs=branch_specs
-            + [whole((inner, D)), by_order(inner), by_order(inner), whole((1, inner))],
-            scratch_shapes=[pltpu.VMEM((inner, D), F32)],
+            + [
+                whole((inner, D)),
+                whole((D, inner)),
+                by_order(inner),
+                by_order(inner),
+                whole((1, inner)),
+            ],
+            scratch_shapes=[pltpu.VMEM((inner, D), F32), pltpu.VMEM((D, inner), F32)],
         ),
         out_shape=branch_shapes
         + [
             shaped((inner, D), BF16),
-            shaped((count, length, inner)),
+            shaped((D, inner), BF16),
+            shaped((count, length, inner), BF16),
             shaped((count, length, inner), BF16),
             shaped((1, inner)),
         ],
         compiler_params=params(),
         cost_estimate=cost(1),
         name="gate_back",
-    )(order, upstream, weight, gate, mixed, gate_gain, d_out, stats)
-
-
-def run_mixer_back(s, rest, mixed, d_mixed, incoming, taps, heads, skip, after, before):
+    )(order, upstream, weight, gate, mixed, gate_gain, d_out, stats, low)
+
+
+def run_mixer_back(s, rest, mixed, d_mixed, incoming, taps, heads, skip, low, after, before, part):
     count, length, inner = mixed.shape
     conv = inner + 2 * NS
     last = length // ROWS - 1
@@ -598,7 +634,7 @@
         return pl.BlockSpec((1, ROWS, width), lambda b: (s, last - b, 0))
 
     return pl.pallas_call(
-        functools.partial(mixer_back_kernel, inner),
+        functools.partial(mixer_back_kernel, inner, s == 0),
         grid=(length // ROWS,),
         in_specs=[
             rows(width),
@@ -612,27 +648,37 @@
             whole((RIM, conv)),
             whole((8, LANES)),
             whole((1, inner)),
+            rows(D),
+            left_alone(),
             left_alone(),
             left_alone(),
         ],
-        out_specs=[rows(width), whole((RIM, conv)), whole((8, LANES)), whole((1, inner))],
+        out_specs=[
+            rows(width),
+            whole((D, width)),
+            whole((RIM, conv)),
+            whole((8, LANES)),
+            whole((1, inner)),
+        ],
         scratch_shapes=[
             pltpu.VMEM((RIM + ROWS, conv), F32),
             pltpu.VMEM((RIM + ROWS, conv), F32),
             pltpu.VMEM((NS, inner), F32),
             pltpu.VMEM((ROWS, conv), F32),
+            pltpu.VMEM((D, width), F32),
         ],
         out_shape=[
             shaped((count, length, width), BF16),
+            shaped((D, width), BF16 if s == count - 1 else F32),
             shaped((RIM, conv)),
             shaped((8, LANES)),
             shaped((1, inner)),
         ],
-        input_output_aliases={9: 0} if s > 0 else {},
+        input_output_aliases={10: 0} if s > 0 else {},
         compiler_params=params(),
         cost_estimate=cost(1),
         name="mixer_back",
-    )(rest, rest, mixed, d_mixed, incoming, taps, heads, skip, after, before)
+    )(rest, rest, mixed, d_mixed, incoming, taps, heads, skip, low, after, before, part)
 
 
 def run_norm_back(split, s, order, d_gate, d_rest, weight_gate, weight_rest, tokens, after):
@@ -695,6 +741,17 @@
     for axis in axes:
         value = value + swapped(value, axis)
     return value
+
+
+def by_rank(value):
+    if lax.axis_size("ctx") != 4:
+        return lax.all_gather(value, "ctx", axis=0)
+    rank = lax.axis_index("ctx")
+    near, across = swapped(value, "ctx", 1), swapped(value, "ctx", 2)
+    found = [value, near, across, swapped(across, "ctx", 1)]
+    odd, high = (rank & 1) == 1, rank >= 2
+    found = [jnp.where(odd, found[k ^ 1], found[k]) for k in range(4)]
+    return jnp.stack([jnp.where(high, found[k ^ 2], found[k]) for k in range(4)])
 
 
 def to_all(value, axes):
@@ -767,13 +824,16 @@
             )
         )
     rest = conv + LANES
-    mine_in = to_all(jnp.concatenate(slices, axis=0), "ctx")
+    sent = jnp.concatenate(slices, axis=0)
+    mine_in = to_all(sent, "ctx")
     mine_rest = mine_in[:, :rest]
     if len(dp) > 1:
         columns = [mine_out[:, k * inner : (k + 1) * inner] for k in range(D // inner)]
         mine_both = jnp.concatenate([mine_in[:, rest:]] + columns, axis=0)
         other_rest = swapped(mine_rest, dp[0])
         other_both = swapped(mine_both, dp[0])
+        mine_rest, mine_out = lax.optimization_barrier((mine_rest, mine_out))
+        other_rest, other_both = lax.optimization_barrier((other_rest, other_both))
         weight_halves = [to_every(mine_rest, dp[1:]), to_every(other_rest, dp[1:])]
         both = jnp.concatenate([mine_both, other_both], axis=0)
         both, *weight_halves = lax.optimization_barrier((both, *weight_halves))
@@ -816,8 +876,8 @@
         high, upstream, low, mixed, gate_gain, weights
     )
     stats = lax.all_gather(stats, "ctx")
-    *branch, grad_out, d_mixed, d_gate, d_gate_gain = run_gate_back(
-        split, order, upstream, weight_out, gate, mixed, gate_gain, d_out, stats
+    *branch, grad_out, grad_gate, d_mixed, d_gate, d_gate_gain = run_gate_back(
+        split, order, upstream, weight_out, gate, mixed, gate_gain, d_out, stats, low
     )
     grad_out = to_all(grad_out, dp)
     branch, branch_sent = chip_sums(branch)
@@ -827,25 +887,21 @@
     def summed(got):
         return jnp.sum(got.astype(F32).reshape(-1, n_ctx, own_rows, got.shape[1]), axis=0)
 
-    grad_gate = dot(low.reshape(-1, D), d_gate.reshape(-1, inner), COL_COL).astype(BF16)
     after = grad_gate if branch_sent is None else branch_sent
     branch = across_sums(branch, branch_sent)
-    d_rest = after
+    d_rest = grad_rest = after
     smalls = []
     normeds = []
     for s in range(count):
-        d_rest, *small = run_mixer_back(
-            s, rest, mixed, d_mixed, incoming, taps, head_rows, skip, after, d_rest
+        d_rest, grad_rest, *small = run_mixer_back(
+            s, rest, mixed, d_mixed, incoming, taps, head_rows, skip, low, after, d_rest, grad_rest
         )
         after = grad_out
         if s == 0:
+            grad_gate, small[0] = lax.optimization_barrier((grad_gate, small[0]))
             grad_gate = to_all(grad_gate, axes)
         if s == count - 1:
-            grad_rest = dot(
-                low.reshape(-1, D), d_rest.reshape(-1, d_rest.shape[2]), COL_COL
-            ).astype(BF16)
-            after = grad_gate[:16, :LANES] + grad_rest[:16, :LANES]
-            grad_rest = to_all(grad_rest, axes)
+            after = grad_gate
         *d_normed, d_gain = run_norm_back(
             split, s, order, d_gate, d_rest, weight_gate, weight_rest, tokens, after
         )
@@ -853,8 +909,20 @@
         d_normed, normed_sent = chip_sums(d_normed)
         after = d_normed if normed_sent is None else normed_sent
         normeds.append(across_sums(d_normed, normed_sent))
+    d_norm_gain, d_taps, d_heads, d_skip = (sum(parts) for parts in zip(*smalls))
+    parts = (
+        d_norm_gain.reshape(-1),
+        d_gate_gain.reshape(-1),
+        d_taps[: KCONV + 1].reshape(-1),
+        d_heads[0, :heads],
+        d_heads[1, :heads],
+        jnp.sum(d_skip.reshape(heads, HD), axis=1),
+    )
+    mine = jnp.concatenate(parts)
+    mine = jnp.pad(mine, (0, -mine.shape[0] % (8 * LANES))).reshape(-1, LANES)
+    mine = sum_over(mine, dp)
+    grad_rest = to_all(grad_rest, axes)
     d_normed = jnp.concatenate(normeds, axis=0)
-    d_norm_gain, d_taps, d_heads, d_skip = (sum(parts) for parts in zip(*smalls))
     grad_out = jnp.sum(grad_out.astype(F32).reshape(n_dp, -1, D), axis=0)
     grad_out = lax.ppermute(grad_out, axes, [(b, a) for a, b in moves])
     grad_gate = summed(grad_gate)
@@ -865,17 +933,7 @@
     columns += [grad_rest[r, :, conv : conv + heads] for r in range(n_ctx)]
     grad_in = jnp.concatenate(columns, axis=1)
 
-    parts = (
-        d_norm_gain.reshape(-1),
-        d_gate_gain.reshape(-1),
-        d_taps[: KCONV + 1].reshape(-1),
-        d_heads[0, :heads],
-        d_heads[1, :heads],
-        jnp.sum(d_skip.reshape(heads, HD), axis=1),
-    )
-    mine = jnp.concatenate(parts)
-    mine = jnp.pad(mine, (0, -mine.shape[0] % (8 * LANES))).reshape(-1, LANES)
-    every = lax.all_gather(sum_over(mine, dp), "ctx", axis=0).reshape(n_ctx, -1)
+    every = by_rank(mine).reshape(n_ctx, -1)
     offset = 0
     found = []
     for part in parts:

time: 340 us -> 341 us (level)
  blocking collectives: 58.7 us -> 5.7 us
  waiting for transfers between devices: 50.6 us -> 90.6 us
  matrix products: 12.7 us -> 0 us
  local copies, waits for them, and re-layouts: 20.5 us -> 29.6 us
  Pallas kernels: 105 us -> 114 us
  starting transfers between devices: 53.7 us -> 58.6 us
    all_gather x1 -> x0, blocking collectives: 45.3 us -> none  [shards(): every = lax.all_gather(sum_over(mine, dp), 'ctx', axis=0).reshape(n_ctx, -1)]
    ppermute x11 -> x14, waiting for transfers between devices: 30.7 us -> 69.7 us  [swapped(): return lax.ppermute(value, axis, [(a, a ^ mask) for a in range(count)])]
    dot_general x2 -> x0, matrix products: 12.7 us -> none  [dot(): lax.dot_general(a, b, (contract, ((), ())), preferred_element_type=F32)]
    all_to_all x1 -> x0, blocking collectives: 9.37 us -> none  [to_all(): return lax.all_to_all(value, axes, split_axis=0, concat_axis=0, tiled=True)]
    all_to_all x6 -> x7, waiting for transfers between devices: 5.44 us -> 13 us  [to_all(): return lax.all_to_all(value, axes, split_axis=0, concat_axis=0, tiled=True)]
    pallas_call x2, Pallas kernels: 39.9 us -> 46.5 us  [run_mixer_back(): pl.pallas_call(functools.partial(mixer_back_kernel, inner, s == 0), grid=...]
    ppermute x1, waiting for transfers between devices: 13 us -> 6.53 us  [shards(): mine_out = lax.ppermute(w_out.astype(BF16), axes, moves)]
    unnamed x85 -> x80, local copies, waits for them, and re-layouts: 14.9 us -> 21.3 us
  transfers between devices with their start and end apart: 21 -> 25, of which waited for: 7 -> 9; matrix products, arithmetic and copies ran while one was open for 11% -> 8% of each run, Pallas kernels for 20% -> 24%
where the time goes in v3:
time: 341 us; the launch traced here: 336 us
  Pallas kernels  114 us (33%)
  waiting for transfers between devices  90.6 us (27%)
  starting transfers between devices  58.6 us (17%)
  local copies, waits for them, and re-layouts  29.6 us (9%)
  other arithmetic  22.8 us (7%)
  between operations  14.7 us (4%)
  blocking collectives  5.7 us (2%)
    ppermute x14, waiting for transfers between devices, swapped(): return lax.ppermute(value, axis, [(a, a ^ mask) for a in range(count)])  69.7 us
    pallas_call x2, Pallas kernels, run_mixer_back(): pl.pallas_call(functools.partial(mixer_back_kernel, inner, s == 0), grid=...  46.5 us
    all_to_all x7, starting transfers between devices, to_all(): return lax.all_to_all(value, axes, split_axis=0, concat_axis=0, tiled=True)  36.5 us
    pallas_call x1, Pallas kernels, run_forward(): pl.pallas_call(functools.partial(forward_kernel, inner), grid_spec=pltpu....  21.9 us
    unnamed x80, local copies, waits for them, and re-layouts  21.3 us
    pallas_call x1, Pallas kernels, run_gate_back(): pl.pallas_call(gate_back_kernel, grid_spec=pltpu.PrefetchScalarGridSpec(n...  19.9 us
    ppermute x14, starting transfers between devices, swapped(): return lax.ppermute(value, axis, [(a, a ^ mask) for a in range(count)])  14.6 us
    pallas_call x2, Pallas kernels, run_norm_back(): pl.pallas_call(norm_back_kernel, grid_spec=pltpu.PrefetchScalarGridSpec(n...  13.6 us
  transfers between devices with their start and end apart: 25, of which 9 were waited for; matrix products, arithmetic and copies ran while one was open for 8% of the time, Pallas kernels for 24%

profile of v3, /device:TPU:5, one launch (start us, length us, event | category | flops | bytes accessed | tf_op | source)
XLA Modules:
  0.0 336.3 jit_solution(3401759034356181742)
XLA Ops:
  9.6 4.1 %all-to-all-start = ((bf16[4,32,1408]{2,1,0:T(8,128)(2,1)}), bf16[4,32,1408]{2,1,0:T(8,128)(2,1)S(1)}, u32[]{:S(2)}, u32[]{:S(2)}) async-start(bf16[4,32,1408]{2,1,0:T(8,128)(2,1)} %bitcast.4), calls=%async_computation | async-start | bytes 720896 | tf_op jit(solution)/shard_map/all_to_all | solution.py:758
  13.7 4.2 %collective-permute-start = (bf16[64,1024]{1,0:T(8,128)(2,1)S(1)}, bf16[64,1024]{1,0:T(8,128)(2,1)S(1)}, u32[]{:S(2)}, u32[]{:S(2)}) collective-permute-start(bf16[64,1024]{1,0:T(8,128)(2,1)S(1)} %convert_element_type.103), channel_id=1, source_target_pairs={{0,0},{1,4},{2,8},{3,12},{4,16},{5,20},{6,24},{7,28},{8,1},{9,5},{... | collective-permute-start | bytes 393224 | tf_op jit(solution)/shard_map/ppermute | solution.py:808
  20.0 6.5 %collective-permute-done = bf16[64,1024]{1,0:T(8,128)(2,1)S(1)} collective-permute-done((bf16[64,1024]{1,0:T(8,128)(2,1)S(1)}, bf16[64,1024]{1,0:T(8,128)(2,1)S(1)}, u32[]{:S(2)}, u32[]{:S(2)}) %collective-permute-start) | collective-permute-done | bytes 131104 | tf_op jit(solution)/shard_map/ppermute | solution.py:808
  27.5 6.2 %all-to-all-start.1 = ((bf16[4,128,896]{2,1,0:T(8,128)(2,1)}), bf16[4,128,896]{2,1,0:T(8,128)(2,1)S(1)}, u32[]{:S(2)}, u32[]{:S(2)}) async-start(bf16[4,128,896]{2,1,0:T(8,128)(2,1)} %broadcast_in_dim.12), calls=%async_computation.1 | async-start | bytes 1835008 | tf_op jit(solution)/shard_map/all_to_all | solution.py:758
  36.1 20.4 %collective-permute-done.1 = bf16[128,896]{1,0:T(8,128)(2,1)S(1)} collective-permute-done((bf16[128,896]{1,0:T(8,128)(2,1)S(1)}, bf16[128,896]{1,0:T(8,128)(2,1)S(1)}, u32[]{:S(2)}, u32[]{:S(2)}) %collective-permute-start.1) | collective-permute-done | bytes 229408 | tf_op jit(solution)/shard_map/ppermute | solution.py:719
  57.6 3.5 %all-to-all-start.2 = ((bf16[4,128,896]{2,1,0:T(8,128)(2,1)}), bf16[4,128,896]{2,1,0:T(8,128)(2,1)S(1)}, u32[]{:S(2)}, u32[]{:S(2)}) async-start(bf16[4,128,896]{2,1,0:T(8,128)(2,1)} %broadcast_in_dim.13), calls=%async_computation.2 | async-start | bytes 1835008 | tf_op jit(solution)/shard_map/all_to_all | solution.py:758
  62.2 11.0 %all-to-all-done.2 = bf16[4,128,896]{2,1,0:T(8,128)(2,1)S(1)} async-done(((bf16[4,128,896]{2,1,0:T(8,128)(2,1)}), bf16[4,128,896]{2,1,0:T(8,128)(2,1)S(1)}, u32[]{:S(2)}, u32[]{:S(2)}) %all-to-all-start.2) | async-done | bytes 917536 | tf_op jit(solution)/shard_map/all_to_all | solution.py:758
  74.7 5.4 %all-to-all-start.3 = ((bf16[4,512,512]{2,1,0:T(8,128)(2,1)}), bf16[4,512,512]{2,1,0:T(8,128)(2,1)}, u32[]{:S(2)}, u32[]{:S(2)}) async-start(bf16[4,512,512]{2,1,0:T(8,128)(2,1)} %broadcast_in_dim.14), calls=%async_computation.3 | async-start | bytes 4194304 | tf_op jit(solution)/shard_map/all_to_all | solution.py:758
  80.7 21.9 %forward_mixer.1 = (bf16[2,1024,1024]{2,1,0:T(8,128)(2,1)}, f32[2,1024,896]{2,1,0:T(8,128)}, f32[2,1024,512]{2,1,0:T(8,128)}, bf16[2,8,128,512]{3,2,1,0:T(8,128)(2,1)S(1)}, bf16[1024,896]{1,0:T(8,128)(2,1)S(1)}) custom-call(s32[1]{0:T(128)} %bitcast.order_ref, bf16[2,1024,1024]{2,1,0:T(8,128)(2,1)} %all-gather.6.cloned.1.call-done.tokens_ref, ...), custom_call_target="tpu_custom_call" | custom-call | flops 1100000000 | bytes 2000000 | tf_op jit(solution)/shard_map/forward_mixer/pallas_call | solution.py:508
  105.2 12.4 %gate_stats.1 = (bf16[512,1024]{1,0:T(8,128)(2,1)S(1)}, bf16[1024,512]{1,0:T(8,128)(2,1)S(1)}, f32[2,1024,512]{2,1,0:T(8,128)}, bf16[2,1024,512]{2,1,0:T(8,128)(2,1)S(1)}, f32[2,2,1024]{2,1,0:T(2,128)S(1)}) custom-call(s32[1]{0:T(128)} %bitcast.order_ref, bf16[2,1024,1024]{2,1,0:T(8,128)(2,1)} %all-gather.4.cloned.1.call-done.up_ref, ...), custom_call_target="tpu_custom_call" | custom-call | flops 1100000000 | bytes 2000000 | tf_op jit(solution)/shard_map/gate_stats/pallas_call | solution.py:541
  119.9 5.7 %all-gather = f32[8,2,1024]{2,1,0:T(2,128)S(1)} all-gather(f32[2,2,1024]{2,1,0:T(2,128)S(1)} %get-tuple-element.63), channel_id=2, replica_groups=mesh['high'=2,'low'=2,'side'=2,'ctx'=4] {'ctx'}, dimensions={0}, use_global_device_ids=true | all-gather | bytes 81920 | tf_op jit(solution)/shard_map/all_gather | solution.py:878
  125.6 19.9 %gate_back.1 = (bf16[2,512,1024]{2,1,0:T(8,128)(2,1)S(1)}, bf16[2,512,1024]{2,1,0:T(8,128)(2,1)}, bf16[512,1024]{1,0:T(8,128)(2,1)}, bf16[1024,512]{1,0:T(8,128)...) custom-call(s32[4]{0:T(128)S(1)} %broadcast_xor_fusion.order_ref, ...), custom_call_target="tpu_custom_call" | custom-call | flops 1100000000 | bytes 2000000 | tf_op jit(solution)/shard_map/gate_back/pallas_call | solution.py:585
  148.1 5.9 %all-to-all-start.4 = ((bf16[8,64,1024]{2,1,0:T(8,128)(2,1)}), bf16[8,64,1024]{2,1,0:T(8,128)(2,1)S(1)}, u32[]{:S(2)}, u32[]{:S(2)}) async-start(bf16[8,64,1024]{2,1,0:T(8,128)(2,1)} %bitcast.11), calls=%async_computation.4 | async-start | bytes 2097152 | tf_op jit(solution)/shard_map/all_to_all | solution.py:758
  158.9 22.7 %mixer_back.2 = (bf16[2,1024,896]{2,1,0:T(8,128)(2,1)}, f32[1024,896]{1,0:T(8,128)}, f32[8,768]{1,0:T(8,128)S(1)}, f32[8,128]{1,0:T(8,128)S(1)}, f32[1,512]{1,0:T(1,128)S(1)}) custom-call(f32[2,1024,896]{2,1,0:T(8,128)} %get-tuple-element.67.rest_ref.rim_ref, f32[2,1024,896]{2,1,0:T(8,128)} %get-tuple-element.67.rest_ref.rim_ref, ...), custom_call_target="tpu_custom_call" | custom-call | flops 1100000000 | bytes 2000000 | tf_op jit(solution)/shard_map/mixer_back/pallas_call | solution.py:636
  181.6 5.4 %all-to-all-start.5 = ((bf16[32,32,512]{2,1,0:T(8,128)(2,1)}), bf16[32,32,512]{2,1,0:T(8,128)(2,1)S(1)}, u32[]{:S(2)}, u32[]{:S(2)}) async-start(bf16[32,32,512]{2,1,0:T(8,128)(2,1)} %bitcast.74), calls=%async_computation.5 | async-start | bytes 2097152 | tf_op jit(solution)/shard_map/all_to_all | solution.py:758
  189.7 6.4 %norm_back.2 = (bf16[1,512,1024]{2,1,0:T(8,128)(2,1)S(1)}, bf16[1,512,1024]{2,1,0:T(8,128)(2,1)S(1)}, f32[1,1024]{1,0:T(1,128)S(1)}) custom-call(s32[4]{0:T(128)S(1)} %broadcast_xor_fusion.order_ref, bf16[2,1024,512]{2,1,0:T(8,128)(2,1)} %get-tuple-element.66.d_gate_ref, bf16[2,1024,896]{2,1,0:T(8,128)(2,1)} %get-tuple-element.70.d_rest_ref.before_ref, ...), custom_call_target="tpu_custom_call" | custom-call | flops 1100000000 | bytes 2000000 | tf_op jit(solution)/shard_map/norm_back/pallas_call | solution.py:695
  197.5 3.3 collective-permute-start.9
  201.8 23.8 %mixer_back.3 = (bf16[2,1024,896]{2,1,0:T(8,128)(2,1)}, bf16[1024,896]{1,0:T(8,128)(2,1)S(1)}, f32[8,768]{1,0:T(8,128)S(1)}, f32[8,128]{1,0:T(8,128)S(1)}, f32[1,512]{1,0:T(1,128)S(1)}) custom-call(f32[2,1024,896]{2,1,0:T(8,128)} %get-tuple-element.67.rest_ref.rim_ref, ...), custom_call_target="tpu_custom_call", output_to_operand_aliasing={{0}: (10, {})} | custom-call | flops 1100000000 | bytes 2000000 | tf_op jit(solution)/shard_map/mixer_back/pallas_call | solution.py:636
  228.5 7.2 %norm_back.3 = (bf16[1,512,1024]{2,1,0:T(8,128)(2,1)S(1)}, bf16[1,512,1024]{2,1,0:T(8,128)(2,1)}, f32[1,1024]{1,0:T(1,128)S(1)}) custom-call(s32[4]{0:T(128)S(1)} %broadcast_xor_fusion.order_ref, bf16[2,1024,512]{2,1,0:T(8,128)(2,1)} %get-tuple-element.66.d_gate_ref, bf16[2,1024,896]{2,1,0:T(8,128)(2,1)} %get-tuple-element.77.d_rest_ref, ...), custom_call_target="tpu_custom_call" | custom-call | flops 1100000000 | bytes 2000000 | tf_op jit(solution)/shard_map/norm_back/pallas_call | solution.py:695
  243.9 6.1 %all-to-all-start.6 = ((bf16[32,32,896]{2,1,0:T(8,128)(2,1)}), bf16[32,32,896]{2,1,0:T(8,128)(2,1)}, u32[]{:S(2)}, u32[]{:S(2)}) async-start(bf16[32,32,896]{2,1,0:T(8,128)(2,1)} %bitcast.73), calls=%async_computation.6 | async-start | bytes 3670016 | tf_op jit(solution)/shard_map/all_to_all | solution.py:758
  250.1 39.0 %collective-permute-done.6 = bf16[1,256,1024]{2,1,0:T(8,128)(2,1)} collective-permute-done((bf16[1,256,1024]{2,1,0:T(8,128)(2,1)}, bf16[1,256,1024]{2,1,0:T(8,128)(2,1)}, u32[]{:S(2)}, u32[]{:S(2)}) %collective-permute-start.6) | collective-permute-done | bytes 524320 | tf_op jit(solution)/shard_map/ppermute | solution.py:719
  289.1 2.4 convert_add_fusion.2
  307.6 9.8 %collective-permute-done.8 = bf16[1,256,1024]{2,1,0:T(8,128)(2,1)} collective-permute-done((bf16[1,256,1024]{2,1,0:T(8,128)(2,1)}, bf16[1,256,1024]{2,1,0:T(8,128)(2,1)}, u32[]{:S(2)}, u32[]{:S(2)}) %collective-permute-start.8) | collective-permute-done | bytes 524320 | tf_op jit(solution)/shard_map/ppermute | solution.py:719
  320.7 3.4 %fusion.7 = (bf16[2,256,1024]{2,1,0:T(8,128)(2,1)}, bf16[2,256,1024]{2,1,0:T(8,128)(2,1)}) fusion(bf16[2,256,1024]{2,1,0:T(8,128)(2,1)S(1)} %copy-done.20, bf16[2,256,1024]{2,1,0:T(8,128)(2,1)S(1)} %copy-done.22, f32[1,256,1024]{2,1,0:T(8,128)S(1)} %convert_add_fusion.1, f32[1,256,1024]{2,1,0:T(8,128)S(1)} %copy-done.21, ...), kind=kLoop, calls=%fused_computation.12 | loop fusion | flops 9437184 | bytes 9445376 | tf_op jit(solution)/shard_map/convert_element_type | solution.py:962
  (199 shorter events, 65.1 us)
Async XLA Ops:
  7.2 73.5 %all-gather.6.cloned.1.call-start = ((), (), s32[]{:S(2)}) async-start(), calls=%async_computation.8 | async-start | bytes 5242880 | tf_op jit(solution)/shard_map/all_gather | solution.py:809
  7.9 97.3 %all-gather.4.cloned.1.call-start = ((), (), s32[]{:S(2)}) async-start(), calls=%async_computation.7 | async-start | bytes 5242880 | tf_op jit(solution)/shard_map/all_gather | solution.py:810
  9.6 10.3 %all-to-all-start = ((bf16[4,32,1408]{2,1,0:T(8,128)(2,1)}), bf16[4,32,1408]{2,1,0:T(8,128)(2,1)S(1)}, u32[]{:S(2)}, u32[]{:S(2)}) async-start(bf16[4,32,1408]{2,1,0:T(8,128)(2,1)} %bitcast.4), calls=%async_computation | async-start | bytes 720896 | tf_op jit(solution)/shard_map/all_to_all | solution.py:758
  13.7 12.8 %collective-permute-start = (bf16[64,1024]{1,0:T(8,128)(2,1)S(1)}, bf16[64,1024]{1,0:T(8,128)(2,1)S(1)}, u32[]{:S(2)}, u32[]{:S(2)}) collective-permute-start(bf16[64,1024]{1,0:T(8,128)(2,1)S(1)} %convert_element_type.103), channel_id=1, source_target_pairs={{0,0},{1,4},{2,8},{3,12},{4,16},{5,20},{6,24},{7,28},{8,1},{9,5},{... | collective-permute-start | bytes 393224 | tf_op jit(solution)/shard_map/ppermute | solution.py:808
  27.5 29.1 %all-to-all-start.1 = ((bf16[4,128,896]{2,1,0:T(8,128)(2,1)}), bf16[4,128,896]{2,1,0:T(8,128)(2,1)S(1)}, u32[]{:S(2)}, u32[]{:S(2)}) async-start(bf16[4,128,896]{2,1,0:T(8,128)(2,1)} %broadcast_in_dim.12), calls=%async_computation.1 | async-start | bytes 1835008 | tf_op jit(solution)/shard_map/all_to_all | solution.py:758
  33.7 22.9 %collective-permute-start.2 = (bf16[256,512]{1,0:T(8,128)(2,1)S(1)}, bf16[256,512]{1,0:T(8,128)(2,1)S(1)}, u32[]{:S(2)}, u32[]{:S(2)}) collective-permute-start(bf16[256,512]{1,0:T(8,128)(2,1)S(1)} %pad_maximum_fusion.1), channel_id=1, source_target_pairs={{0,16},{16,0},{1,17},{17,1},{2,18},{18,2},{3,19},{19,3},{4,20},{20... | collective-permute-start | bytes 786440 | tf_op jit(solution)/shard_map/ppermute | solution.py:719
  33.8 22.8 %collective-permute-start.1 = (bf16[128,896]{1,0:T(8,128)(2,1)S(1)}, bf16[128,896]{1,0:T(8,128)(2,1)S(1)}, u32[]{:S(2)}, u32[]{:S(2)}) collective-permute-start(bf16[128,896]{1,0:T(8,128)(2,1)S(1)} %slice.264), channel_id=1, source_target_pairs={{0,16},{16,0},{1,17},{17,1},{2,18},{18,2},{3,19},{19,3},{4,20},{20... | collective-permute-start | bytes 688136 | tf_op jit(solution)/shard_map/ppermute | solution.py:719
  57.6 15.5 %all-to-all-start.2 = ((bf16[4,128,896]{2,1,0:T(8,128)(2,1)}), bf16[4,128,896]{2,1,0:T(8,128)(2,1)S(1)}, u32[]{:S(2)}, u32[]{:S(2)}) async-start(bf16[4,128,896]{2,1,0:T(8,128)(2,1)} %broadcast_in_dim.13), calls=%async_computation.2 | async-start | bytes 1835008 | tf_op jit(solution)/shard_map/all_to_all | solution.py:758
  74.7 30.6 %all-to-all-start.3 = ((bf16[4,512,512]{2,1,0:T(8,128)(2,1)}), bf16[4,512,512]{2,1,0:T(8,128)(2,1)}, u32[]{:S(2)}, u32[]{:S(2)}) async-start(bf16[4,512,512]{2,1,0:T(8,128)(2,1)} %broadcast_in_dim.14), calls=%async_computation.3 | async-start | bytes 4194304 | tf_op jit(solution)/shard_map/all_to_all | solution.py:758
  147.9 6.0 %collective-permute-start.3 = (bf16[2,512,1024]{2,1,0:T(8,128)(2,1)}, bf16[2,512,1024]{2,1,0:T(8,128)(2,1)S(1)}, u32[]{:S(2)}, u32[]{:S(2)}) collective-permute-start(bf16[2,512,1024]{2,1,0:T(8,128)(2,1)} %get-tuple-element.65), channel_id=1, source_target_pairs={{0,1},{1,0},{2,3},{3,2},{4,5},{5,4},{6,7},{7,6},{8,9},{9,8},{10,11... | collective-permute-start | bytes 6291464 | tf_op jit(solution)/shard_map/ppermute | solution.py:719
  148.1 33.5 %all-to-all-start.4 = ((bf16[8,64,1024]{2,1,0:T(8,128)(2,1)}), bf16[8,64,1024]{2,1,0:T(8,128)(2,1)S(1)}, u32[]{:S(2)}, u32[]{:S(2)}) async-start(bf16[8,64,1024]{2,1,0:T(8,128)(2,1)} %bitcast.11), calls=%async_computation.4 | async-start | bytes 2097152 | tf_op jit(solution)/shard_map/all_to_all | solution.py:758
  181.6 45.4 %all-to-all-start.5 = ((bf16[32,32,512]{2,1,0:T(8,128)(2,1)}), bf16[32,32,512]{2,1,0:T(8,128)(2,1)S(1)}, u32[]{:S(2)}, u32[]{:S(2)}) async-start(bf16[32,32,512]{2,1,0:T(8,128)(2,1)} %bitcast.74), calls=%async_computation.5 | async-start | bytes 2097152 | tf_op jit(solution)/shard_map/all_to_all | solution.py:758
  196.2 4.6 %collective-permute-start.5 = (bf16[1,512,1024]{2,1,0:T(8,128)(2,1)S(1)}, bf16[1,512,1024]{2,1,0:T(8,128)(2,1)S(1)}, u32[]{:S(2)}, u32[]{:S(2)}) collective-permute-start(bf16[1,512,1024]{2,1,0:T(8,128)(2,1)S(1)} %get-tuple-element.75), channel_id=1, source_target_pairs={{0,1},{1,0},{2,3},{3,2},{4,5},{5,4},{6,7},{7,6},{8,9},{9,8},{10,11... | collective-permute-start | bytes 3145736 | tf_op jit(solution)/shard_map/ppermute | solution.py:719
  197.5 44.3 %collective-permute-start.9 = (f32[64,1024]{1,0:T(8,128)}, f32[64,1024]{1,0:T(8,128)}, u32[]{:S(2)}, u32[]{:S(2)}) collective-permute-start(f32[64,1024]{1,0:T(8,128)} %convert_reduce_fusion.2), channel_id=1, source_target_pairs={{0,0},{4,1},{8,2},{12,3},{16,4},{20,5},{24,6},{28,7},{1,8},{5,9},{... | collective-permute-start | bytes 786440 | tf_op jit(solution)/shard_map/ppermute | solution.py:927
  236.8 3.6 %collective-permute-start.10 = (f32[48,128]{1,0:T(8,128)S(1)}, f32[48,128]{1,0:T(8,128)S(1)}, u32[]{:S(2)}, u32[]{:S(2)}) collective-permute-start(f32[48,128]{1,0:T(8,128)S(1)} %pad_bitcast_fusion), channel_id=1, source_target_pairs={{0,16},{16,0},{1,17},{17,1},{2,18},{18,2},{3,19},{19,3},{4,20},{20... | collective-permute-start | bytes 73736 | tf_op jit(solution)/shard_map/ppermute | solution.py:719
  238.0 81.5 %collective-permute-start.4 = (bf16[2,256,1024]{2,1,0:T(8,128)(2,1)S(1)}, bf16[2,256,1024]{2,1,0:T(8,128)(2,1)}, u32[]{:S(2)}, u32[]{:S(2)}) collective-permute-start(bf16[2,256,1024]{2,1,0:T(8,128)(2,1)S(1)} %add_convert_fusion.after_ref.before_ref.part_ref), channel_id=1, source_target_pairs={{0,2},{1,3},{2,0},{3,1},{4,6},{5,7},{6,4},{7,5},{8,10},{9,11},{10,... | collective-permute-start | bytes 3145736 | tf_op jit(solution)/shard_map/ppermute | solution.py:719
  240.2 48.9 %collective-permute-start.6 = (bf16[1,256,1024]{2,1,0:T(8,128)(2,1)}, bf16[1,256,1024]{2,1,0:T(8,128)(2,1)}, u32[]{:S(2)}, u32[]{:S(2)}) collective-permute-start(bf16[1,256,1024]{2,1,0:T(8,128)(2,1)} %copy-done.10), channel_id=1, source_target_pairs={{0,2},{1,3},{2,0},{3,1},{4,6},{5,7},{6,4},{7,5},{8,10},{9,11},{10,... | collective-permute-start | bytes 1572872 | tf_op jit(solution)/shard_map/ppermute | solution.py:719
  240.4 9.5 %collective-permute-start.11 = (f32[48,128]{1,0:T(8,128)S(1)}, f32[48,128]{1,0:T(8,128)S(1)}, u32[]{:S(2)}, u32[]{:S(2)}) collective-permute-start(f32[48,128]{1,0:T(8,128)S(1)} %fusion.43), channel_id=1, source_target_pairs={{0,8},{8,0},{1,9},{9,1},{2,10},{10,2},{3,11},{11,3},{4,12},{12,4},... | collective-permute-start | bytes 73736 | tf_op jit(solution)/shard_map/ppermute | solution.py:719
  243.9 80.3 %all-to-all-start.6 = ((bf16[32,32,896]{2,1,0:T(8,128)(2,1)}), bf16[32,32,896]{2,1,0:T(8,128)(2,1)}, u32[]{:S(2)}, u32[]{:S(2)}) async-start(bf16[32,32,896]{2,1,0:T(8,128)(2,1)} %bitcast.73), calls=%async_computation.6 | async-start | bytes 3670016 | tf_op jit(solution)/shard_map/all_to_all | solution.py:758
  250.0 41.6 %collective-permute-start.12 = (f32[48,128]{1,0:T(8,128)S(1)}, f32[48,128]{1,0:T(8,128)S(1)}, u32[]{:S(2)}, u32[]{:S(2)}) collective-permute-start(f32[48,128]{1,0:T(8,128)S(1)} %fusion.51), channel_id=1, source_target_pairs={{0,4},{4,0},{1,5},{5,1},{2,6},{6,2},{3,7},{7,3},{8,12},{12,8},{9,1... | collective-permute-start | bytes 73736 | tf_op jit(solution)/shard_map/ppermute | solution.py:719
  291.5 3.5 %collective-permute-start.13 = (f32[48,128]{1,0:T(8,128)S(1)}, f32[48,128]{1,0:T(8,128)S(1)}, u32[]{:S(2)}, u32[]{:S(2)}) collective-permute-start(f32[48,128]{1,0:T(8,128)S(1)} %add.167), channel_id=1, source_target_pairs={{0,2},{1,3},{2,0},{3,1},{4,6},{5,7},{6,4},{7,5},{8,10},{9,11},{10,... | collective-permute-start | bytes 73736 | tf_op jit(solution)/shard_map/ppermute | solution.py:719
  293.9 3.4 collective-permute-start.15
  297.3 2.9 collective-permute-start.7
  303.3 14.1 %collective-permute-start.8 = (bf16[1,256,1024]{2,1,0:T(8,128)(2,1)}, bf16[1,256,1024]{2,1,0:T(8,128)(2,1)}, u32[]{:S(2)}, u32[]{:S(2)}) collective-permute-start(bf16[1,256,1024]{2,1,0:T(8,128)(2,1)} %add_convert_fusion.1), channel_id=1, source_target_pairs={{0,2},{1,3},{2,0},{3,1},{4,6},{5,7},{6,4},{7,5},{8,10},{9,11},{10,... | collective-permute-start | bytes 1572872 | tf_op jit(solution)/shard_map/ppermute | solution.py:719
  (43 other events, 263.0 us)
Sparse Core Ops, SparseCore 0:
  9.6 36.0 all-gather.5
  47.3 39.2 all-gather.3

commit v4 on v3

--- a/solution.py
+++ b/solution.py
@@ -33,7 +33,7 @@
 
 F32 = jnp.float32
 BF16 = jnp.bfloat16
-VMEM_BYTES = 48 * 1024 * 1024
+VMEM_BYTES = 60 * 1024 * 1024
 
 
 def dot(a, b, contract=((1,), (0,))):
@@ -244,16 +244,16 @@
     return jnp.broadcast_to(row, (LANES, row.shape[1])).T[:, 0:1]
 
 
-def keep_or_send(refs, step, value):
+def keep_or_send(refs, kept, value):
     if len(refs) == 1:
         refs[0][0] = value
         return
 
-    @pl.when(step < 2)
+    @pl.when(kept)
     def _():
         refs[0][0] = value
 
-    @pl.when(step >= 2)
+    @pl.when(jnp.logical_not(kept))
     def _():
         refs[1][0] = value
 
@@ -297,7 +297,7 @@
     gated = mixed * silu
     unit = gated * scale
     low = (unit * gain).astype(BF16)
-    keep_or_send(branch_refs, pl.program_id(1), dot(low, weight_ref[...]).astype(BF16))
+    keep_or_send(branch_refs, pl.program_id(1) < 2, dot(low, weight_ref[...]).astype(BF16))
     total[...] += dot(low, up_ref[0], COL_COL)
     d_gain_ref[...] += jnp.sum(d_out * unit, axis=0, keepdims=True)
     d_gated = scale * (gain * d_out - unit * (scale * products * (1.0 / DI)))
@@ -315,6 +315,7 @@
 def mixer_back_kernel(
     inner,
     first,
+    table_ref,
     rest_ref,
     rim_ref,
     mixed_ref,
@@ -324,20 +325,16 @@
     heads_ref,
     skip_ref,
     low_ref,
+    d_gate_ref,
+    tokens_ref,
+    weight_gate_ref,
+    weight_rest_ref,
     after_ref,
-    before_ref,
     part_ref,
-    d_rest_ref,
-    grad_ref,
-    d_taps_ref,
-    d_heads_ref,
-    d_skip_ref,
-    padded,
-    later,
-    carried,
-    d_active,
-    total,
+    *refs,
 ):
+    *normed_refs, d_gain_ref, grad_ref, d_taps_ref, d_heads_ref, d_skip_ref = refs[:-6]
+    padded, later, carried, d_active, total, d_rest_ref = refs[-6:]
     rows = rest_ref.shape[1]
     conv = inner + 2 * NS
     block = pl.num_programs(0) - 1 - pl.program_id(0)
@@ -347,6 +344,7 @@
         d_taps_ref[...] = jnp.zeros_like(d_taps_ref)
         d_heads_ref[...] = jnp.zeros_like(d_heads_ref)
         d_skip_ref[...] = jnp.zeros_like(d_skip_ref)
+        d_gain_ref[...] = jnp.zeros_like(d_gain_ref)
         if first:
             total[...] = jnp.zeros_like(total)
         else:
@@ -424,7 +422,7 @@
         d_heads_ref[0:1, :] += jnp.sum(d_raw, axis=0, keepdims=True)
         d_heads_ref[1:2, :] += jnp.sum(d_rate * rate, axis=0, keepdims=True)
         d_skip_ref[...] += jnp.sum(d_mixed * values, axis=0, keepdims=True)
-        d_rest_ref[0, part, conv:] = d_raw.astype(BF16)
+        d_rest_ref[part, conv:] = d_raw.astype(BF16)
         d_active[part, :inner] = d_stepped * step_x + skip * d_mixed
         d_active[part, inner : inner + NS] = d_in_b
         d_active[part, inner + NS :] = d_out_c
@@ -440,30 +438,20 @@
             d_conv_out * padded[start : start + rows, :], axis=0, keepdims=True
         )
     d_taps_ref[KCONV : KCONV + 1, :] += jnp.sum(d_conv_out, axis=0, keepdims=True)
-    d_rest_ref[0, :, :conv] = d_conv_in.astype(BF16)
-    total[...] += dot(low_ref[0], d_rest_ref[0], COL_COL)
+    d_rest_ref[:, :conv] = d_conv_in.astype(BF16)
+    d_rest = d_rest_ref[...]
+    total[...] += dot(low_ref[0], d_rest, COL_COL)
+    d_normed = dot(d_gate_ref[0], weight_gate_ref[...], ROW_ROW) + dot(
+        d_rest, weight_rest_ref[...], ROW_ROW
+    )
+    tokens = tokens_ref[0].astype(F32)
+    scale = lax.rsqrt(jnp.mean(tokens * tokens, axis=1, keepdims=True) + NORM_EPS)
+    d_gain_ref[...] += jnp.sum(d_normed * (tokens * scale), axis=0, keepdims=True)
+    keep_or_send(normed_refs, table_ref[pl.program_id(0)] == 1, d_normed.astype(BF16))
 
     @pl.when(block == 0)
     def _():
         grad_ref[...] = total[...].astype(grad_ref.dtype)
-
-
-def norm_back_kernel(
-    order_ref, d_gate_ref, d_rest_ref, weight_gate_ref, weight_rest_ref, tokens_ref, after_ref, *refs
-):
-    *d_normed_refs, d_gain_ref = refs
-
-    @pl.when(pl.program_id(0) == 0)
-    def _():
-        d_gain_ref[...] = jnp.zeros_like(d_gain_ref)
-
-    d_normed = dot(d_gate_ref[0], weight_gate_ref[...], ROW_ROW) + dot(
-        d_rest_ref[0], weight_rest_ref[...], ROW_ROW
-    )
-    tokens = tokens_ref[0].astype(F32)
-    scale = lax.rsqrt(jnp.mean(tokens * tokens, axis=1, keepdims=True) + NORM_EPS)
-    d_gain_ref[...] += jnp.sum(d_normed * (tokens * scale), axis=0, keepdims=True)
-    keep_or_send(d_normed_refs, pl.program_id(0), d_normed.astype(BF16))
 
 
 def whole(shape):
@@ -623,7 +611,9 @@
     )(order, upstream, weight, gate, mixed, gate_gain, d_out, stats, low)
 
 
-def run_mixer_back(s, rest, mixed, d_mixed, incoming, taps, heads, skip, low, after, before, part):
+def run_mixer_back(split, s, table, saved, fixed, weights, after, part):
+    rest, mixed, d_mixed, incoming, low, d_gate, tokens = saved
+    taps, heads, skip = fixed
     count, length, inner = mixed.shape
     conv = inner + 2 * NS
     last = length // ROWS - 1
@@ -631,87 +621,71 @@
     width = rest.shape[2]
 
     def rows(width):
-        return pl.BlockSpec((1, ROWS, width), lambda b: (s, last - b, 0))
-
+        return pl.BlockSpec((1, ROWS, width), lambda b, table: (s, last - b, 0))
+
+    if split:
+        normed_specs = [
+            pl.BlockSpec((1, ROWS, D), lambda b, table: (0, table[4 + b], 0)),
+            pl.BlockSpec((1, ROWS, D), lambda b, table: (0, table[8 + b], 0)),
+        ]
+        normed_shapes = [shaped((1, 2 * ROWS, D), BF16)] * 2
+    else:
+        normed_specs = [pl.BlockSpec((1, ROWS, D), lambda b, table: (0, last - b, 0))]
+        normed_shapes = [shaped((1, length, D), BF16)]
     return pl.pallas_call(
         functools.partial(mixer_back_kernel, inner, s == 0),
-        grid=(length // ROWS,),
-        in_specs=[
-            rows(width),
-            pl.BlockSpec(
-                (1, RIM, width),
-                lambda b: (s, jnp.maximum((last - b) * (ROWS // RIM) - 1, 0), 0),
-            ),
-            rows(inner),
-            rows(inner),
-            pl.BlockSpec((1, chunks, NS, inner), lambda b: (s, last - b, 0, 0)),
-            whole((RIM, conv)),
-            whole((8, LANES)),
-            whole((1, inner)),
-            rows(D),
-            left_alone(),
-            left_alone(),
-            left_alone(),
-        ],
-        out_specs=[
-            rows(width),
-            whole((D, width)),
-            whole((RIM, conv)),
-            whole((8, LANES)),
-            whole((1, inner)),
-        ],
-        scratch_shapes=[
-            pltpu.VMEM((RIM + ROWS, conv), F32),
-            pltpu.VMEM((RIM + ROWS, conv), F32),
-            pltpu.VMEM((NS, inner), F32),
-            pltpu.VMEM((ROWS, conv), F32),
-            pltpu.VMEM((D, width), F32),
-        ],
-        out_shape=[
-            shaped((count, length, width), BF16),
+        grid_spec=pltpu.PrefetchScalarGridSpec(
+            num_scalar_prefetch=1,
+            grid=(length // ROWS,),
+            in_specs=[
+                rows(width),
+                pl.BlockSpec(
+                    (1, RIM, width),
+                    lambda b, table: (s, jnp.maximum((last - b) * (ROWS // RIM) - 1, 0), 0),
+                ),
+                rows(inner),
+                rows(inner),
+                pl.BlockSpec((1, chunks, NS, inner), lambda b, table: (s, last - b, 0, 0)),
+                whole((RIM, conv)),
+                whole((8, LANES)),
+                whole((1, inner)),
+                rows(D),
+                rows(inner),
+                rows(D),
+                whole((D, inner)),
+                whole((D, width)),
+                left_alone(),
+                left_alone(),
+            ],
+            out_specs=normed_specs
+            + [
+                whole((1, D)),
+                whole((D, width)),
+                whole((RIM, conv)),
+                whole((8, LANES)),
+                whole((1, inner)),
+            ],
+            scratch_shapes=[
+                pltpu.VMEM((RIM + ROWS, conv), F32),
+                pltpu.VMEM((RIM + ROWS, conv), F32),
+                pltpu.VMEM((NS, inner), F32),
+                pltpu.VMEM((ROWS, conv), F32),
+                pltpu.VMEM((D, width), F32),
+                pltpu.VMEM((ROWS, width), BF16),
+            ],
+        ),
+        out_shape=normed_shapes
+        + [
+            shaped((1, D)),
             shaped((D, width), BF16 if s == count - 1 else F32),
             shaped((RIM, conv)),
             shaped((8, LANES)),
             shaped((1, inner)),
         ],
-        input_output_aliases={10: 0} if s > 0 else {},
         compiler_params=params(),
         cost_estimate=cost(1),
         name="mixer_back",
-    )(rest, rest, mixed, d_mixed, incoming, taps, heads, skip, low, after, before, part)
-
-
-def run_norm_back(split, s, order, d_gate, d_rest, weight_gate, weight_rest, tokens, after):
-    _, length, inner = d_gate.shape
-    width = d_rest.shape[2]
-
-    def rows(width, s):
-        return pl.BlockSpec((1, ROWS, width), lambda b, order: (s, order[b], 0))
-
-    def place(group):
-        return pl.BlockSpec((1, ROWS, D), lambda b, order: (0, group(order, b), 0))
-
-    specs, shapes = kept_and_sent(split, 1, length, place)
-    return pl.pallas_call(
-        norm_back_kernel,
-        grid_spec=pltpu.PrefetchScalarGridSpec(
-            num_scalar_prefetch=1,
-            grid=(length // ROWS,),
-            in_specs=[
-                rows(inner, s),
-                rows(width, s),
-                whole(weight_gate.shape),
-                whole(weight_rest.shape),
-                rows(D, s),
-                left_alone(),
-            ],
-            out_specs=specs + [whole((1, D))],
-        ),
-        out_shape=shapes + [shaped((1, D))],
-        compiler_params=params(),
-        cost_estimate=cost(1),
-        name="norm_back",
-    )(order, d_gate, d_rest, weight_gate, weight_rest, tokens, after)
+    )(table, rest, rest, mixed, d_mixed, incoming, *fixed, low, d_gate, tokens, *weights, after, part)
 
 
 def swapped(value, axis, mask=1):
@@ -833,7 +807,6 @@
         other_rest = swapped(mine_rest, dp[0])
         other_both = swapped(mine_both, dp[0])
         mine_rest, mine_out = lax.optimization_barrier((mine_rest, mine_out))
-        other_rest, other_both = lax.optimization_barrier((other_rest, other_both))
         weight_halves = [to_every(mine_rest, dp[1:]), to_every(other_rest, dp[1:])]
         both = jnp.concatenate([mine_both, other_both], axis=0)
         both, *weight_halves = lax.optimization_barrier((both, *weight_halves))
@@ -889,25 +862,35 @@
 
     after = grad_gate if branch_sent is None else branch_sent
     branch = across_sums(branch, branch_sent)
-    d_rest = grad_rest = after
+    table = jnp.zeros((12,), jnp.int32)
+    if split:
+        masks = rank.astype(jnp.int32) ^ jnp.array([3, 2, 1, 0], jnp.int32)
+        kept = 1 - (masks & 1)
+        places = masks >> 1
+        early, late = places[jnp.array([0, 0, 2, 2])], places[jnp.array([1, 1, 1, 3])]
+        one_first = kept[0] == 1
+        table = jnp.concatenate(
+            [kept, jnp.where(one_first, early, late), jnp.where(one_first, late, early)]
+        )
+    saved = (rest, mixed, d_mixed, incoming, low, d_gate, tokens)
+    fixed = (taps, head_rows, skip)
+    weights = (weight_gate, weight_rest)
+    grad_rest = after
     smalls = []
     normeds = []
     for s in range(count):
-        d_rest, grad_rest, *small = run_mixer_back(
-            s, rest, mixed, d_mixed, incoming, taps, head_rows, skip, low, after, d_rest, grad_rest
-        )
-        after = grad_out
+        found = run_mixer_back(split, s, table, saved, fixed, weights, after, grad_rest)
+        *d_normed, d_gain, grad_rest, d_taps, d_heads, d_skip = found
+        smalls.append([d_gain, d_taps, d_heads, d_skip])
         if s == 0:
-            grad_gate, small[0] = lax.optimization_barrier((grad_gate, small[0]))
-            grad_gate = to_all(grad_gate, axes)
-        if s == count - 1:
-            after = grad_gate
-        *d_normed, d_gain = run_norm_back(
-            split, s, order, d_gate, d_rest, weight_gate, weight_rest, tokens, after
-        )
-        smalls.append([d_gain] + small)
+            grad_out, *d_normed = lax.optimization_barrier((grad_out, *d_normed))
+        else:
+            grad_gate, *d_normed = lax.optimization_barrier((grad_gate, *d_normed))
         d_normed, normed_sent = chip_sums(d_normed)
         after = d_normed if normed_sent is None else normed_sent
+        if s == 0:
+            grad_gate, after = lax.optimization_barrier((grad_gate, after))
+            grad_gate = to_all(grad_gate, axes)
         normeds.append(across_sums(d_normed, normed_sent))
     d_norm_gain, d_taps, d_heads, d_skip = (sum(parts) for parts in zip(*smalls))
     parts = (
@@ -920,7 +903,8 @@
     )
     mine = jnp.concatenate(parts)
     mine = jnp.pad(mine, (0, -mine.shape[0] % (8 * LANES))).reshape(-1, LANES)
-    mine = sum_over(mine, dp)
+    every = by_rank(sum_over(mine, dp)).reshape(n_ctx, -1)
+    grad_rest, every, *normeds = lax.optimization_barrier((grad_rest, every, *normeds))
     grad_rest = to_all(grad_rest, axes)
     d_normed = jnp.concatenate(normeds, axis=0)
     grad_out = jnp.sum(grad_out.astype(F32).reshape(n_dp, -1, D), axis=0)
@@ -933,7 +917,6 @@
     columns += [grad_rest[r, :, conv : conv + heads] for r in range(n_ctx)]
     grad_in = jnp.concatenate(columns, axis=1)
 
-    every = by_rank(mine).reshape(n_ctx, -1)
     offset = 0
     found = []
     for part in parts:

time: 341 us -> 352 us (1.032)
  waiting for transfers between devices: 90.6 us -> 108 us
  local copies, waits for them, and re-layouts: 29.6 us -> 13.4 us
  other arithmetic: 22.8 us -> 29.3 us
    ppermute x14, waiting for transfers between devices: 69.7 us -> 93.6 us  [swapped(): return lax.ppermute(value, axis, [(a, a ^ mask) for a in range(count)])]
    unnamed x80 -> x73, local copies, waits for them, and re-layouts: 21.3 us -> 4.09 us
    all_to_all x7, waiting for transfers between devices: 13 us -> 6.68 us  [to_all(): return lax.all_to_all(value, axes, split_axis=0, concat_axis=0, tiled=True)]
    pallas_call x4 -> x2, Pallas kernels: 60.1 us -> 59.8 us  [run_mixer_back(): pl.pallas_call(functools.partial(mixer_back_kernel, inner, s == 0), grid_...]
  transfers between devices with their start and end apart: 25 -> 25, of which waited for: 9 -> 13; matrix products, arithmetic and copies ran while one was open for 8% -> 9% of each run, Pallas kernels for 24% -> 23%
where the time goes in v4:
time: 352 us; the launch traced here: 349 us
  Pallas kernels  116 us (33%)
  waiting for transfers between devices  108 us (31%)
  starting transfers between devices  59.7 us (17%)
  other arithmetic  29.3 us (8%)
  between operations  14.8 us (4%)
  local copies, waits for them, and re-layouts  13.4 us (4%)
  blocking collectives  7.11 us (2%)
    ppermute x14, waiting for transfers between devices, swapped(): return lax.ppermute(value, axis, [(a, a ^ mask) for a in range(count)])  93.6 us
    pallas_call x2, Pallas kernels, run_mixer_back(): pl.pallas_call(functools.partial(mixer_back_kernel, inner, s == 0), grid_...  59.8 us
    all_to_all x7, starting transfers between devices, to_all(): return lax.all_to_all(value, axes, split_axis=0, concat_axis=0, tiled=True)  35.2 us
    pallas_call x1, Pallas kernels, run_forward(): pl.pallas_call(functools.partial(forward_kernel, inner), grid_spec=pltpu....  22.2 us
    pallas_call x1, Pallas kernels, run_gate_back(): pl.pallas_call(gate_back_kernel, grid_spec=pltpu.PrefetchScalarGridSpec(n...  21.6 us
    ppermute x14, starting transfers between devices, swapped(): return lax.ppermute(value, axis, [(a, a ^ mask) for a in range(count)])  17.2 us
    pallas_call x1, Pallas kernels, run_stats(): pl.pallas_call(functools.partial(stats_kernel, joined), grid_spec=pltpu.P...  12.9 us
    all_gather x1, blocking collectives, shards(): stats = lax.all_gather(stats, 'ctx')  7.11 us
  transfers between devices with their start and end apart: 25, of which 13 were waited for; matrix products, arithmetic and copies ran while one was open for 9% of the time, Pallas kernels for 23%

profile of v4, /device:TPU:5, one launch (start us, length us, event | category | flops | bytes accessed | tf_op | source)
XLA Modules:
  0.0 348.9 jit_solution(5509860075015187491)
XLA Ops:
  9.6 4.1 %all-to-all-start = ((bf16[4,32,1408]{2,1,0:T(8,128)(2,1)}), bf16[4,32,1408]{2,1,0:T(8,128)(2,1)S(1)}, u32[]{:S(2)}, u32[]{:S(2)}) async-start(bf16[4,32,1408]{2,1,0:T(8,128)(2,1)} %bitcast.4), calls=%async_computation | async-start | bytes 720896 | tf_op jit(solution)/shard_map/all_to_all | solution.py:732
  13.7 4.2 %collective-permute-start = (bf16[64,1024]{1,0:T(8,128)(2,1)S(1)}, bf16[64,1024]{1,0:T(8,128)(2,1)S(1)}, u32[]{:S(2)}, u32[]{:S(2)}) collective-permute-start(bf16[64,1024]{1,0:T(8,128)(2,1)S(1)} %convert_element_type.94), channel_id=1, source_target_pairs={{0,0},{1,4},{2,8},{3,12},{4,16},{5,20},{6,24},{7,28},{8,1},{9,5},{... | collective-permute-start | bytes 393224 | tf_op jit(solution)/shard_map/ppermute | solution.py:782
  20.0 6.5 %collective-permute-done = bf16[64,1024]{1,0:T(8,128)(2,1)S(1)} collective-permute-done((bf16[64,1024]{1,0:T(8,128)(2,1)S(1)}, bf16[64,1024]{1,0:T(8,128)(2,1)S(1)}, u32[]{:S(2)}, u32[]{:S(2)}) %collective-permute-start) | collective-permute-done | bytes 131104 | tf_op jit(solution)/shard_map/ppermute | solution.py:782
  27.5 6.2 %all-to-all-start.1 = ((bf16[4,128,896]{2,1,0:T(8,128)(2,1)}), bf16[4,128,896]{2,1,0:T(8,128)(2,1)S(1)}, u32[]{:S(2)}, u32[]{:S(2)}) async-start(bf16[4,128,896]{2,1,0:T(8,128)(2,1)} %broadcast_in_dim.16), calls=%async_computation.1 | async-start | bytes 1835008 | tf_op jit(solution)/shard_map/all_to_all | solution.py:732
  33.7 11.4 %collective-permute-done.2 = bf16[128,896]{1,0:T(8,128)(2,1)S(1)} collective-permute-done((bf16[128,896]{1,0:T(8,128)(2,1)S(1)}, bf16[128,896]{1,0:T(8,128)(2,1)S(1)}, u32[]{:S(2)}, u32[]{:S(2)}) %collective-permute-start.2) | collective-permute-done | bytes 229408 | tf_op jit(solution)/shard_map/ppermute | solution.py:693
  47.8 4.8 %all-to-all-start.2 = ((bf16[4,128,896]{2,1,0:T(8,128)(2,1)}), bf16[4,128,896]{2,1,0:T(8,128)(2,1)S(1)}, u32[]{:S(2)}, u32[]{:S(2)}) async-start(bf16[4,128,896]{2,1,0:T(8,128)(2,1)} %broadcast_in_dim.17), calls=%async_computation.2 | async-start | bytes 1835008 | tf_op jit(solution)/shard_map/all_to_all | solution.py:732
  52.7 13.8 %collective-permute-done.1 = bf16[256,512]{1,0:T(8,128)(2,1)S(1)} collective-permute-done((bf16[256,512]{1,0:T(8,128)(2,1)S(1)}, bf16[256,512]{1,0:T(8,128)(2,1)S(1)}, u32[]{:S(2)}, u32[]{:S(2)}) %collective-permute-start.1) | collective-permute-done | bytes 262176 | tf_op jit(solution)/shard_map/ppermute | solution.py:693
  71.2 5.8 %all-to-all-start.3 = ((bf16[4,512,512]{2,1,0:T(8,128)(2,1)}), bf16[4,512,512]{2,1,0:T(8,128)(2,1)S(1)}, u32[]{:S(2)}, u32[]{:S(2)}) async-start(bf16[4,512,512]{2,1,0:T(8,128)(2,1)} %broadcast_in_dim.36), calls=%async_computation.3 | async-start | bytes 4194304 | tf_op jit(solution)/shard_map/all_to_all | solution.py:732
  81.1 22.2 %forward_mixer.1 = (bf16[2,1024,1024]{2,1,0:T(8,128)(2,1)}, f32[2,1024,896]{2,1,0:T(8,128)}, f32[2,1024,512]{2,1,0:T(8,128)}, bf16[2,8,128,512]{3,2,1,0:T(8,128)(2,1)}, bf16[1024,896]{1,0:T(8,128)(2,1)}) custom-call(s32[1]{0:T(128)} %bitcast.order_ref, bf16[2,1024,1024]{2,1,0:T(8,128)(2,1)} %all-gather.6.cloned.1.call-done.tokens_ref, f32[1,1024]{1,0:T(1,128)} %bitcast.86, ...), custom_call_target="tpu_custom_call" | custom-call | flops 1100000000 | bytes 2000000 | tf_op jit(solution)/shard_map/forward_mixer/pallas_call | solution.py:496
  104.6 12.9 %gate_stats.1 = (bf16[512,1024]{1,0:T(8,128)(2,1)}, bf16[1024,512]{1,0:T(8,128)(2,1)}, f32[2,1024,512]{2,1,0:T(8,128)}, bf16[2,1024,512]{2,1,0:T(8,128)(2,1)}, f32[2,2,1024]{2,1,0:T(2,128)}) custom-call(s32[1]{0:T(128)} %bitcast.order_ref, bf16[2,1024,1024]{2,1,0:T(8,128)(2,1)} %all-gather.4.cloned.1.call-done.up_ref, ...), custom_call_target="tpu_custom_call" | custom-call | flops 1100000000 | bytes 2000000 | tf_op jit(solution)/shard_map/gate_stats/pallas_call | solution.py:529
  117.5 7.1 %all-gather = f32[8,2,1024]{2,1,0:T(2,128)} all-gather(f32[2,2,1024]{2,1,0:T(2,128)} %get-tuple-element.67), channel_id=2, replica_groups=mesh['high'=2,'low'=2,'side'=2,'ctx'=4] {'ctx'}, dimensions={0}, use_global_device_ids=true | all-gather | bytes 81920 | tf_op jit(solution)/shard_map/all_gather | solution.py:851
  124.6 21.6 %gate_back.1 = (bf16[2,512,1024]{2,1,0:T(8,128)(2,1)}, bf16[2,512,1024]{2,1,0:T(8,128)(2,1)}, bf16[512,1024]{1,0:T(8,128)(2,1)}, bf16[1024,512]{1,0:T(8,128)(2,1...) custom-call(s32[4]{0:T(128)} %broadcast_xor_fusion.order_ref, ...), custom_call_target="tpu_custom_call" | custom-call | flops 1100000000 | bytes 2000000 | tf_op jit(solution)/shard_map/gate_back/pallas_call | solution.py:573
  146.5 4.5 %all-to-all-start.4 = ((bf16[8,64,1024]{2,1,0:T(8,128)(2,1)}), bf16[8,64,1024]{2,1,0:T(8,128)(2,1)S(1)}, u32[]{:S(2)}, u32[]{:S(2)}) async-start(bf16[8,64,1024]{2,1,0:T(8,128)(2,1)} %bitcast.79), calls=%async_computation.4 | async-start | bytes 2097152 | tf_op jit(solution)/shard_map/all_to_all | solution.py:732
  155.6 29.1 %mixer_back.2 = (bf16[1,512,1024]{2,1,0:T(8,128)(2,1)}, bf16[1,512,1024]{2,1,0:T(8,128)(2,1)}, f32[1,1024]{1,0:T(1,128)}, f32[1024,896]{1,0:T(8,128)}, f32[8,768...) custom-call(s32[12]{0:T(128)} %pad_add_fusion.table_ref, f32[2,1024,896]{2,1,0:T(8,128)} %get-tuple-element.70.rest_ref.rim_ref, ...), custom_call_target="tpu_custom_call" | custom-call | flops 1100000000 | bytes 2000000 | tf_op jit(solution)/shard_map/mixer_back/pallas_call | solution.py:635
  191.2 5.1 %all-to-all-start.5 = ((bf16[32,32,512]{2,1,0:T(8,128)(2,1)}), bf16[32,32,512]{2,1,0:T(8,128)(2,1)S(1)}, u32[]{:S(2)}, u32[]{:S(2)}) async-start(bf16[32,32,512]{2,1,0:T(8,128)(2,1)} %bitcast.23), calls=%async_computation.5 | async-start | bytes 2097152 | tf_op jit(solution)/shard_map/all_to_all | solution.py:732
  196.3 30.6 %mixer_back.3 = (bf16[1,512,1024]{2,1,0:T(8,128)(2,1)}, bf16[1,512,1024]{2,1,0:T(8,128)(2,1)}, f32[1,1024]{1,0:T(1,128)}, bf16[1024,896]{1,0:T(8,128)(2,1)}, f32...) custom-call(s32[12]{0:T(128)} %pad_add_fusion.table_ref, f32[2,1024,896]{2,1,0:T(8,128)} %get-tuple-element.70.rest_ref.rim_ref, ...), custom_call_target="tpu_custom_call" | custom-call | flops 1100000000 | bytes 2000000 | tf_op jit(solution)/shard_map/mixer_back/pallas_call | solution.py:635
  240.6 3.9 %collective-permute-start.11 = (f32[48,128]{1,0:T(8,128)S(1)}, f32[48,128]{1,0:T(8,128)S(1)}, u32[]{:S(2)}, u32[]{:S(2)}) collective-permute-start(f32[48,128]{1,0:T(8,128)S(1)} %add.159), channel_id=1, source_target_pairs={{0,1},{1,0},{2,3},{3,2},{4,5},{5,4},{6,7},{7,6},{8,9},{9,8},{10,11... | collective-permute-start | bytes 73736 | tf_op jit(solution)/shard_map/ppermute | solution.py:693
  247.7 3.1 collective-permute-start.15
  250.8 3.3 collective-permute-start.12
  255.9 14.8 %collective-permute-done.12 = bf16[1,256,1024]{2,1,0:T(8,128)(2,1)S(1)} collective-permute-done((bf16[1,256,1024]{2,1,0:T(8,128)(2,1)S(1)}, bf16[1,256,1024]{2,1,0:T(8,128)(2,1)S(1)}, u32[]{:S(2)}, u32[]{:S(2)}) %collective-permute-start.12) | collective-permute-done | bytes 524320 | tf_op jit(solution)/shard_map/ppermute | solution.py:693
  270.9 11.0 %collective-permute-done.14 = bf16[1,256,1024]{2,1,0:T(8,128)(2,1)S(1)} collective-permute-done((bf16[1,256,1024]{2,1,0:T(8,128)(2,1)S(1)}, bf16[1,256,1024]{2,1,0:T(8,128)(2,1)S(1)}, u32[]{:S(2)}, u32[]{:S(2)}) %collective-permute-start.14) | collective-permute-done | bytes 524320 | tf_op jit(solution)/shard_map/ppermute | solution.py:693
  284.2 4.8 %all-to-all-start.6 = ((bf16[32,32,896]{2,1,0:T(8,128)(2,1)}), bf16[32,32,896]{2,1,0:T(8,128)(2,1)}, u32[]{:S(2)}, u32[]{:S(2)}) async-start(bf16[32,32,896]{2,1,0:T(8,128)(2,1)} %bitcast.76), calls=%async_computation.6 | async-start | bytes 3670016 | tf_op jit(solution)/shard_map/all_to_all | solution.py:732
  298.5 34.7 %collective-permute-done.4 = bf16[2,256,1024]{2,1,0:T(8,128)(2,1)} collective-permute-done((bf16[2,256,1024]{2,1,0:T(8,128)(2,1)S(1)}, bf16[2,256,1024]{2,1,0:T(8,128)(2,1)}, u32[]{:S(2)}, u32[]{:S(2)}) %collective-permute-start.4) | collective-permute-done | bytes 1048608 | tf_op jit(solution)/shard_map/ppermute | solution.py:693
  333.2 3.5 %fusion.7 = (bf16[2,256,1024]{2,1,0:T(8,128)(2,1)}, bf16[2,256,1024]{2,1,0:T(8,128)(2,1)}) fusion(bf16[2,256,1024]{2,1,0:T(8,128)(2,1)S(1)} %copy-done.1, bf16[2,256,1024]{2,1,0:T(8,128)(2,1)S(1)} %copy-done.5, f32[1,256,1024]{2,1,0:T(8,128)S(1)} %copy-done.2, f32[1,256,1024]{2,1,0:T(8,128)S(1)} %convert_add_fusion.2, ...), kind=kLoop, calls=%fused_computation.14 | loop fusion | flops 9437184 | bytes 9445376 | tf_op jit(solution)/shard_map/convert_element_type | solution.py:945
  (196 shorter events, 65.3 us)
Async XLA Ops:
  7.2 73.9 %all-gather.6.cloned.1.call-start = ((), (), s32[]{:S(2)}) async-start(), calls=%async_computation.8 | async-start | bytes 5242880 | tf_op jit(solution)/shard_map/all_gather | solution.py:783
  7.9 95.4 %all-gather.4.cloned.1.call-start = ((), (), s32[]{:S(2)}) async-start(), calls=%async_computation.7 | async-start | bytes 5242880 | tf_op jit(solution)/shard_map/all_gather | solution.py:784
  9.6 10.3 %all-to-all-start = ((bf16[4,32,1408]{2,1,0:T(8,128)(2,1)}), bf16[4,32,1408]{2,1,0:T(8,128)(2,1)S(1)}, u32[]{:S(2)}, u32[]{:S(2)}) async-start(bf16[4,32,1408]{2,1,0:T(8,128)(2,1)} %bitcast.4), calls=%async_computation | async-start | bytes 720896 | tf_op jit(solution)/shard_map/all_to_all | solution.py:732
  13.7 12.8 %collective-permute-start = (bf16[64,1024]{1,0:T(8,128)(2,1)S(1)}, bf16[64,1024]{1,0:T(8,128)(2,1)S(1)}, u32[]{:S(2)}, u32[]{:S(2)}) collective-permute-start(bf16[64,1024]{1,0:T(8,128)(2,1)S(1)} %convert_element_type.94), channel_id=1, source_target_pairs={{0,0},{1,4},{2,8},{3,12},{4,16},{5,20},{6,24},{7,28},{8,1},{9,5},{... | collective-permute-start | bytes 393224 | tf_op jit(solution)/shard_map/ppermute | solution.py:782
  27.5 19.2 %all-to-all-start.1 = ((bf16[4,128,896]{2,1,0:T(8,128)(2,1)}), bf16[4,128,896]{2,1,0:T(8,128)(2,1)S(1)}, u32[]{:S(2)}, u32[]{:S(2)}) async-start(bf16[4,128,896]{2,1,0:T(8,128)(2,1)} %broadcast_in_dim.16), calls=%async_computation.1 | async-start | bytes 1835008 | tf_op jit(solution)/shard_map/all_to_all | solution.py:732
  33.7 11.4 %collective-permute-start.2 = (bf16[128,896]{1,0:T(8,128)(2,1)S(1)}, bf16[128,896]{1,0:T(8,128)(2,1)S(1)}, u32[]{:S(2)}, u32[]{:S(2)}) collective-permute-start(bf16[128,896]{1,0:T(8,128)(2,1)S(1)} %slice.272), channel_id=1, source_target_pairs={{0,16},{16,0},{1,17},{17,1},{2,18},{18,2},{3,19},{19,3},{4,20},{20... | collective-permute-start | bytes 688136 | tf_op jit(solution)/shard_map/ppermute | solution.py:693
  47.8 21.8 %all-to-all-start.2 = ((bf16[4,128,896]{2,1,0:T(8,128)(2,1)}), bf16[4,128,896]{2,1,0:T(8,128)(2,1)S(1)}, u32[]{:S(2)}, u32[]{:S(2)}) async-start(bf16[4,128,896]{2,1,0:T(8,128)(2,1)} %broadcast_in_dim.17), calls=%async_computation.2 | async-start | bytes 1835008 | tf_op jit(solution)/shard_map/all_to_all | solution.py:732
  52.6 13.9 %collective-permute-start.1 = (bf16[256,512]{1,0:T(8,128)(2,1)S(1)}, bf16[256,512]{1,0:T(8,128)(2,1)S(1)}, u32[]{:S(2)}, u32[]{:S(2)}) collective-permute-start(bf16[256,512]{1,0:T(8,128)(2,1)S(1)} %pad_maximum_fusion.1), channel_id=1, source_target_pairs={{0,16},{16,0},{1,17},{17,1},{2,18},{18,2},{3,19},{19,3},{4,20},{20... | collective-permute-start | bytes 786440 | tf_op jit(solution)/shard_map/ppermute | solution.py:693
  71.2 32.1 %all-to-all-start.3 = ((bf16[4,512,512]{2,1,0:T(8,128)(2,1)}), bf16[4,512,512]{2,1,0:T(8,128)(2,1)S(1)}, u32[]{:S(2)}, u32[]{:S(2)}) async-start(bf16[4,512,512]{2,1,0:T(8,128)(2,1)} %broadcast_in_dim.36), calls=%async_computation.3 | async-start | bytes 4194304 | tf_op jit(solution)/shard_map/all_to_all | solution.py:732
  146.2 6.8 %collective-permute-start.3 = (bf16[2,512,1024]{2,1,0:T(8,128)(2,1)}, bf16[2,512,1024]{2,1,0:T(8,128)(2,1)}, u32[]{:S(2)}, u32[]{:S(2)}) collective-permute-start(bf16[2,512,1024]{2,1,0:T(8,128)(2,1)} %get-tuple-element.69), channel_id=1, source_target_pairs={{0,1},{1,0},{2,3},{3,2},{4,5},{5,4},{6,7},{7,6},{8,9},{9,8},{10,11... | collective-permute-start | bytes 6291464 | tf_op jit(solution)/shard_map/ppermute | solution.py:693
  146.5 38.3 %all-to-all-start.4 = ((bf16[8,64,1024]{2,1,0:T(8,128)(2,1)}), bf16[8,64,1024]{2,1,0:T(8,128)(2,1)S(1)}, u32[]{:S(2)}, u32[]{:S(2)}) async-start(bf16[8,64,1024]{2,1,0:T(8,128)(2,1)} %bitcast.79), calls=%async_computation.4 | async-start | bytes 2097152 | tf_op jit(solution)/shard_map/all_to_all | solution.py:732
  184.8 3.4 collective-permute-start.5
  191.2 38.9 %all-to-all-start.5 = ((bf16[32,32,512]{2,1,0:T(8,128)(2,1)}), bf16[32,32,512]{2,1,0:T(8,128)(2,1)S(1)}, u32[]{:S(2)}, u32[]{:S(2)}) async-start(bf16[32,32,512]{2,1,0:T(8,128)(2,1)} %bitcast.23), calls=%async_computation.5 | async-start | bytes 2097152 | tf_op jit(solution)/shard_map/all_to_all | solution.py:732
  230.1 24.1 %collective-permute-start.13 = (bf16[1,512,1024]{2,1,0:T(8,128)(2,1)}, bf16[1,512,1024]{2,1,0:T(8,128)(2,1)}, u32[]{:S(2)}, u32[]{:S(2)}) collective-permute-start(bf16[1,512,1024]{2,1,0:T(8,128)(2,1)} %get-tuple-element.98), channel_id=1, source_target_pairs={{0,1},{1,0},{2,3},{3,2},{4,5},{5,4},{6,7},{7,6},{8,9},{9,8},{10,11... | collective-permute-start | bytes 3145736 | tf_op jit(solution)/shard_map/ppermute | solution.py:693
  230.5 3.6 %collective-permute-start.6 = (f32[48,128]{1,0:T(8,128)S(1)}, f32[48,128]{1,0:T(8,128)S(1)}, u32[]{:S(2)}, u32[]{:S(2)}) collective-permute-start(f32[48,128]{1,0:T(8,128)S(1)} %pad_bitcast_fusion), channel_id=1, source_target_pairs={{0,16},{16,0},{1,17},{17,1},{2,18},{18,2},{3,19},{19,3},{4,20},{20... | collective-permute-start | bytes 73736 | tf_op jit(solution)/shard_map/ppermute | solution.py:693
  234.1 2.7 collective-permute-start.7
  239.4 5.1 %collective-permute-start.9 = (f32[48,128]{1,0:T(8,128)S(1)}, f32[48,128]{1,0:T(8,128)S(1)}, u32[]{:S(2)}, u32[]{:S(2)}) collective-permute-start(f32[48,128]{1,0:T(8,128)S(1)} %add.159), channel_id=1, source_target_pairs={{0,2},{1,3},{2,0},{3,1},{4,6},{5,7},{6,4},{7,5},{8,10},{9,11},{10,... | collective-permute-start | bytes 73736 | tf_op jit(solution)/shard_map/ppermute | solution.py:693
  240.6 13.5 %collective-permute-start.11 = (f32[48,128]{1,0:T(8,128)S(1)}, f32[48,128]{1,0:T(8,128)S(1)}, u32[]{:S(2)}, u32[]{:S(2)}) collective-permute-start(f32[48,128]{1,0:T(8,128)S(1)} %add.159), channel_id=1, source_target_pairs={{0,1},{1,0},{2,3},{3,2},{4,5},{5,4},{6,7},{7,6},{8,9},{9,8},{10,11... | collective-permute-start | bytes 73736 | tf_op jit(solution)/shard_map/ppermute | solution.py:693
  244.5 9.6 %collective-permute-start.10 = (f32[48,128]{1,0:T(8,128)S(1)}, f32[48,128]{1,0:T(8,128)S(1)}, u32[]{:S(2)}, u32[]{:S(2)}) collective-permute-start(f32[48,128]{1,0:T(8,128)S(1)} %collective-permute-done.9), channel_id=1, source_target_pairs={{0,1},{1,0},{2,3},{3,2},{4,5},{5,4},{6,7},{7,6},{8,9},{9,8},{10,11... | collective-permute-start | bytes 73736 | tf_op jit(solution)/shard_map/ppermute | solution.py:693
  247.7 42.6 %collective-permute-start.15 = (f32[64,1024]{1,0:T(8,128)}, f32[64,1024]{1,0:T(8,128)}, u32[]{:S(2)}, u32[]{:S(2)}) collective-permute-start(f32[64,1024]{1,0:T(8,128)} %convert_reduce_fusion.1), channel_id=1, source_target_pairs={{0,0},{4,1},{8,2},{12,3},{16,4},{20,5},{24,6},{28,7},{1,8},{5,9},{... | collective-permute-start | bytes 786440 | tf_op jit(solution)/shard_map/ppermute | solution.py:911
  250.8 19.8 %collective-permute-start.12 = (bf16[1,256,1024]{2,1,0:T(8,128)(2,1)S(1)}, bf16[1,256,1024]{2,1,0:T(8,128)(2,1)S(1)}, u32[]{:S(2)}, u32[]{:S(2)}) collective-permute-start(bf16[1,256,1024]{2,1,0:T(8,128)(2,1)S(1)} %copy-done.11), channel_id=1, source_target_pairs={{0,2},{1,3},{2,0},{3,1},{4,6},{5,7},{6,4},{7,5},{8,10},{9,11},{10,... | collective-permute-start | bytes 1572872 | tf_op jit(solution)/shard_map/ppermute | solution.py:693
  255.7 26.2 %collective-permute-start.14 = (bf16[1,256,1024]{2,1,0:T(8,128)(2,1)S(1)}, bf16[1,256,1024]{2,1,0:T(8,128)(2,1)S(1)}, u32[]{:S(2)}, u32[]{:S(2)}) collective-permute-start(bf16[1,256,1024]{2,1,0:T(8,128)(2,1)S(1)} %add_convert_fusion.1), channel_id=1, source_target_pairs={{0,2},{1,3},{2,0},{3,1},{4,6},{5,7},{6,4},{7,5},{8,10},{9,11},{10,... | collective-permute-start | bytes 1572872 | tf_op jit(solution)/shard_map/ppermute | solution.py:693
  284.2 52.7 %all-to-all-start.6 = ((bf16[32,32,896]{2,1,0:T(8,128)(2,1)}), bf16[32,32,896]{2,1,0:T(8,128)(2,1)}, u32[]{:S(2)}, u32[]{:S(2)}) async-start(bf16[32,32,896]{2,1,0:T(8,128)(2,1)} %bitcast.76), calls=%async_computation.6 | async-start | bytes 3670016 | tf_op jit(solution)/shard_map/all_to_all | solution.py:732
  289.0 44.2 %collective-permute-start.4 = (bf16[2,256,1024]{2,1,0:T(8,128)(2,1)S(1)}, bf16[2,256,1024]{2,1,0:T(8,128)(2,1)}, u32[]{:S(2)}, u32[]{:S(2)}) collective-permute-start(bf16[2,256,1024]{2,1,0:T(8,128)(2,1)S(1)} %copy-done), channel_id=1, source_target_pairs={{0,2},{1,3},{2,0},{3,1},{4,6},{5,7},{6,4},{7,5},{8,10},{9,11},{10,... | collective-permute-start | bytes 3145736 | tf_op jit(solution)/shard_map/ppermute | solution.py:693
  (39 other events, 571.7 us)
Sparse Core Ops, SparseCore 0:
  9.6 36.0 all-gather.5
  47.3 39.2 all-gather.3

commit v5 on v4

--- a/solution.py
+++ b/solution.py
@@ -703,10 +703,12 @@
     return own, (kept[:, ROWS:].astype(F32) + got[:, ROWS:].astype(F32)).astype(BF16)
 
 
-def across_sums(own, sent):
-    if sent is None:
-        return own
-    return own + swapped(sent, "ctx", 2).astype(F32)
+def across(sent):
+    return [] if sent is None else [swapped(sent, "ctx", 2)]
+
+
+def added(own, got):
+    return own + got[0].astype(F32) if got else own
 
 
 def sum_over(value, axes):
@@ -780,6 +782,40 @@
     for block in range(n_dp * n_ctx):
         moves.append((block, (block % n_dp) * n_ctx + block // n_dp))
     mine_out = lax.ppermute(w_out.astype(BF16), axes, moves)
+    offset = 0
+    pieces = []
+    for amount in (D, DI, KCONV * CHANNELS, CHANNELS, HEADS, HEADS, HEADS):
+        pieces.append(small_params[offset : offset + amount])
+        offset = offset + amount
+    norm_gain = pieces[0].reshape(1, D)
+    gate_gain = lax.dynamic_slice(pieces[1], (rank * inner,), (inner,)).reshape(1, inner)
+    taps_all = jnp.concatenate([pieces[2].reshape(KCONV, CHANNELS), pieces[3][None]], axis=0)
+    taps = jnp.concatenate(
+        [lax.dynamic_slice(taps_all, (0, rank * inner), (KCONV + 1, inner)), taps_all[:, DI:]],
+        axis=1,
+    )
+    taps = jnp.pad(taps, ((0, RIM - KCONV - 1), (0, 0)))
+    dt_bias = lax.dynamic_slice(pieces[4], (rank * heads,), (heads,))
+    decay = -jnp.exp(lax.dynamic_slice(pieces[5], (rank * heads,), (heads,)))
+    head_rows = jnp.pad(jnp.stack([dt_bias, decay]), ((0, 6), (0, LANES - heads)))
+    skip = jnp.repeat(lax.dynamic_slice(pieces[6], (rank * heads,), (heads,)), HD).reshape(1, inner)
+
+    split = n_ctx == 4 and block_in.shape[1] == ROWS
+    order = jnp.arange(n_ctx * block_in.shape[1] // ROWS, dtype=jnp.int32)
+    if split:
+        order = rank.astype(jnp.int32) ^ jnp.array([0, 2, 1, 3], jnp.int32)
+    high = lax.axis_index(dp[0]) if len(dp) > 1 else rank * 0
+    high = high.astype(jnp.int32).reshape(1)
+    table = jnp.zeros((12,), jnp.int32)
+    if split:
+        masks = rank.astype(jnp.int32) ^ jnp.array([3, 2, 1, 0], jnp.int32)
+        kept = 1 - (masks & 1)
+        places = masks >> 1
+        early, late = places[jnp.array([0, 0, 2, 2])], places[jnp.array([1, 1, 1, 3])]
+        one_first = kept[0] == 1
+        table = jnp.concatenate(
+            [kept, jnp.where(one_first, early, late), jnp.where(one_first, late, early)]
+        )
     tokens = lax.all_gather(block_in, "ctx", axis=1, tiled=True)
     upstream = lax.all_gather(out_grad, "ctx", axis=1, tiled=True)
     w_in_low = w_in.astype(BF16)
@@ -807,7 +843,13 @@
         other_rest = swapped(mine_rest, dp[0])
         other_both = swapped(mine_both, dp[0])
         mine_rest, mine_out = lax.optimization_barrier((mine_rest, mine_out))
-        weight_halves = [to_every(mine_rest, dp[1:]), to_every(other_rest, dp[1:])]
+        first_half = to_every(mine_rest, dp[1:])
+        other_rest, taps, head_rows, skip, norm_gain, gate_gain, order, high, table = (
+            lax.optimization_barrier(
+                (other_rest, taps, head_rows, skip, norm_gain, gate_gain, order, high, table)
+            )
+        )
+        weight_halves = [first_half, to_every(other_rest, dp[1:])]
         both = jnp.concatenate([mine_both, other_both], axis=0)
         both, *weight_halves = lax.optimization_barrier((both, *weight_halves))
         weights = [to_every(both, dp[1:])]
@@ -818,30 +860,6 @@
             for value in (mine_out, mine_in[:, rest:])
         ]
 
-    offset = 0
-    pieces = []
-    for amount in (D, DI, KCONV * CHANNELS, CHANNELS, HEADS, HEADS, HEADS):
-        pieces.append(small_params[offset : offset + amount])
-        offset = offset + amount
-    norm_gain = pieces[0].reshape(1, D)
-    gate_gain = lax.dynamic_slice(pieces[1], (rank * inner,), (inner,)).reshape(1, inner)
-    taps_all = jnp.concatenate([pieces[2].reshape(KCONV, CHANNELS), pieces[3][None]], axis=0)
-    taps = jnp.concatenate(
-        [lax.dynamic_slice(taps_all, (0, rank * inner), (KCONV + 1, inner)), taps_all[:, DI:]],
-        axis=1,
-    )
-    taps = jnp.pad(taps, ((0, RIM - KCONV - 1), (0, 0)))
-    dt_bias = lax.dynamic_slice(pieces[4], (rank * heads,), (heads,))
-    decay = -jnp.exp(lax.dynamic_slice(pieces[5], (rank * heads,), (heads,)))
-    head_rows = jnp.pad(jnp.stack([dt_bias, decay]), ((0, 6), (0, LANES - heads)))
-    skip = jnp.repeat(lax.dynamic_slice(pieces[6], (rank * heads,), (heads,)), HD).reshape(1, inner)
-
-    split = n_ctx == 4 and block_in.shape[1] == ROWS
-    order = jnp.arange(n_ctx * block_in.shape[1] // ROWS, dtype=jnp.int32)
-    if split:
-        order = rank.astype(jnp.int32) ^ jnp.array([0, 2, 1, 3], jnp.int32)
-    high = lax.axis_index(dp[0]) if len(dp) > 1 else rank * 0
-    high = high.astype(jnp.int32).reshape(1)
     low, rest, mixed, incoming, weight_rest = run_forward(
         high, tokens, norm_gain, weight_halves, taps, head_rows, skip
     )
@@ -861,37 +879,31 @@
         return jnp.sum(got.astype(F32).reshape(-1, n_ctx, own_rows, got.shape[1]), axis=0)
 
     after = grad_gate if branch_sent is None else branch_sent
-    branch = across_sums(branch, branch_sent)
-    table = jnp.zeros((12,), jnp.int32)
-    if split:
-        masks = rank.astype(jnp.int32) ^ jnp.array([3, 2, 1, 0], jnp.int32)
-        kept = 1 - (masks & 1)
-        places = masks >> 1
-        early, late = places[jnp.array([0, 0, 2, 2])], places[jnp.array([1, 1, 1, 3])]
-        one_first = kept[0] == 1
-        table = jnp.concatenate(
-            [kept, jnp.where(one_first, early, late), jnp.where(one_first, late, early)]
-        )
+    branch_got = across(branch_sent)
     saved = (rest, mixed, d_mixed, incoming, low, d_gate, tokens)
     fixed = (taps, head_rows, skip)
     weights = (weight_gate, weight_rest)
     grad_rest = after
     smalls = []
+    owns = []
     normeds = []
     for s in range(count):
         found = run_mixer_back(split, s, table, saved, fixed, weights, after, grad_rest)
         *d_normed, d_gain, grad_rest, d_taps, d_heads, d_skip = found
         smalls.append([d_gain, d_taps, d_heads, d_skip])
         if s == 0:
-            grad_out, *d_normed = lax.optimization_barrier((grad_out, *d_normed))
+            grad_out, branch_got, d_normed = lax.optimization_barrier(
+                (grad_out, branch_got, d_normed)
+            )
         else:
-            grad_gate, *d_normed = lax.optimization_barrier((grad_gate, *d_normed))
-        d_normed, normed_sent = chip_sums(d_normed)
-        after = d_normed if normed_sent is None else normed_sent
+            grad_gate, normeds, d_normed = lax.optimization_barrier((grad_gate, normeds, d_normed))
+        own, normed_sent = chip_sums(d_normed)
+        after = own if normed_sent is None else normed_sent
         if s == 0:
             grad_gate, after = lax.optimization_barrier((grad_gate, after))
             grad_gate = to_all(grad_gate, axes)
-        normeds.append(across_sums(d_normed, normed_sent))
+        owns.append(own)
+        normeds.append(across(normed_sent))
     d_norm_gain, d_taps, d_heads, d_skip = (sum(parts) for parts in zip(*smalls))
     parts = (
         d_norm_gain.reshape(-1),
@@ -904,9 +916,10 @@
     mine = jnp.concatenate(parts)
     mine = jnp.pad(mine, (0, -mine.shape[0] % (8 * LANES))).reshape(-1, LANES)
     every = by_rank(sum_over(mine, dp)).reshape(n_ctx, -1)
-    grad_rest, every, *normeds = lax.optimization_barrier((grad_rest, every, *normeds))
+    grad_rest, every, normeds = lax.optimization_barrier((grad_rest, every, normeds))
     grad_rest = to_all(grad_rest, axes)
-    d_normed = jnp.concatenate(normeds, axis=0)
+    d_normed = jnp.concatenate([added(own, got) for own, got in zip(owns, normeds)], axis=0)
+    branch = added(branch, branch_got)
     grad_out = jnp.sum(grad_out.astype(F32).reshape(n_dp, -1, D), axis=0)
     grad_out = lax.ppermute(grad_out, axes, [(b, a) for a, b in moves])
     grad_gate = summed(grad_gate)

time: 352 us -> 327 us (0.929)
  waiting for transfers between devices: 108 us -> 85.7 us
  other arithmetic: 29.3 us -> 22.6 us
  local copies, waits for them, and re-layouts: 13.4 us -> 17.6 us
    ppermute x14, waiting for transfers between devices: 93.6 us -> 35 us  [swapped(): return lax.ppermute(value, axis, [(a, a ^ mask) for a in range(count)])]
    all_to_all x7, waiting for transfers between devices: 6.68 us -> 38.2 us  [to_all(): return lax.all_to_all(value, axes, split_axis=0, concat_axis=0, tiled=True)]
    ppermute x1, waiting for transfers between devices: 0.01 us -> 4.54 us  [shards(): grad_out = lax.ppermute(grad_out, axes, [(b, a) for a, b in moves])]
  transfers between devices with their start and end apart: 25 -> 25, of which waited for: 13 -> 14; matrix products, arithmetic and copies ran while one was open for 9% -> 9% of each run, Pallas kernels for 23% -> 25%
where the time goes in v5:
time: 327 us; the launch traced here: 324 us
  Pallas kernels  116 us (35%)
  waiting for transfers between devices  85.7 us (26%)
  starting transfers between devices  59.7 us (18%)
  other arithmetic  22.6 us (7%)
  local copies, waits for them, and re-layouts  17.6 us (5%)
  between operations  14.9 us (5%)
  blocking collectives  7.01 us (2%)
    pallas_call x2, Pallas kernels, run_mixer_back(): pl.pallas_call(functools.partial(mixer_back_kernel, inner, s == 0), grid_...  59.8 us
    all_to_all x7, waiting for transfers between devices, to_all(): return lax.all_to_all(value, axes, split_axis=0, concat_axis=0, tiled=True)  38.2 us
    all_to_all x7, starting transfers between devices, to_all(): return lax.all_to_all(value, axes, split_axis=0, concat_axis=0, tiled=True)  36.3 us
    ppermute x14, waiting for transfers between devices, swapped(): return lax.ppermute(value, axis, [(a, a ^ mask) for a in range(count)])  35 us
    pallas_call x1, Pallas kernels, run_forward(): pl.pallas_call(functools.partial(forward_kernel, inner), grid_spec=pltpu....  22.2 us
    pallas_call x1, Pallas kernels, run_gate_back(): pl.pallas_call(gate_back_kernel, grid_spec=pltpu.PrefetchScalarGridSpec(n...  21.5 us
    ppermute x14, starting transfers between devices, swapped(): return lax.ppermute(value, axis, [(a, a ^ mask) for a in range(count)])  16.9 us
    pallas_call x1, Pallas kernels, run_stats(): pl.pallas_call(functools.partial(stats_kernel, joined), grid_spec=pltpu.P...  12.8 us
  transfers between devices with their start and end apart: 25, of which 14 were waited for; matrix products, arithmetic and copies ran while one was open for 9% of the time, Pallas kernels for 25%

profile of v5, /device:TPU:5, one launch (start us, length us, event | category | flops | bytes accessed | tf_op | source)
XLA Modules:
  0.0 323.8 jit_solution(3146403036309081790)
XLA Ops:
  9.6 4.1 %all-to-all-start = ((bf16[4,32,1408]{2,1,0:T(8,128)(2,1)}), bf16[4,32,1408]{2,1,0:T(8,128)(2,1)S(1)}, u32[]{:S(2)}, u32[]{:S(2)}) async-start(bf16[4,32,1408]{2,1,0:T(8,128)(2,1)} %bitcast), calls=%async_computation | async-start | bytes 720896 | tf_op jit(solution)/shard_map/all_to_all | solution.py:734
  13.8 4.2 %collective-permute-start.1 = (bf16[64,1024]{1,0:T(8,128)(2,1)S(1)}, bf16[64,1024]{1,0:T(8,128)(2,1)S(1)}, u32[]{:S(2)}, u32[]{:S(2)}) collective-permute-start(bf16[64,1024]{1,0:T(8,128)(2,1)S(1)} %convert_element_type.94), channel_id=1, source_target_pairs={{0,0},{1,4},{2,8},{3,12},{4,16},{5,20},{6,24},{7,28},{8,1},{9,5},{... | collective-permute-start | bytes 393224 | tf_op jit(solution)/shard_map/ppermute | solution.py:784
  20.0 6.5 %collective-permute-done.1 = bf16[64,1024]{1,0:T(8,128)(2,1)S(1)} collective-permute-done((bf16[64,1024]{1,0:T(8,128)(2,1)S(1)}, bf16[64,1024]{1,0:T(8,128)(2,1)S(1)}, u32[]{:S(2)}, u32[]{:S(2)}) %collective-permute-start.1) | collective-permute-done | bytes 131104 | tf_op jit(solution)/shard_map/ppermute | solution.py:784
  27.6 6.0 %all-to-all-start.1 = ((bf16[4,128,896]{2,1,0:T(8,128)(2,1)}), bf16[4,128,896]{2,1,0:T(8,128)(2,1)S(1)}, u32[]{:S(2)}, u32[]{:S(2)}) async-start(bf16[4,128,896]{2,1,0:T(8,128)(2,1)} %broadcast_in_dim.18), calls=%async_computation.1 | async-start | bytes 1835008 | tf_op jit(solution)/shard_map/all_to_all | solution.py:734
  39.7 5.4 %collective-permute-done = bf16[128,896]{1,0:T(8,128)(2,1)S(1)} collective-permute-done((bf16[128,896]{1,0:T(8,128)(2,1)S(1)}, bf16[128,896]{1,0:T(8,128)(2,1)S(1)}, u32[]{:S(2)}, u32[]{:S(2)}) %collective-permute-start) | collective-permute-done | bytes 229408 | tf_op jit(solution)/shard_map/ppermute | solution.py:693
  47.8 5.9 %all-to-all-start.2 = ((bf16[4,128,896]{2,1,0:T(8,128)(2,1)}), bf16[4,128,896]{2,1,0:T(8,128)(2,1)S(1)}, u32[]{:S(2)}, u32[]{:S(2)}) async-start(bf16[4,128,896]{2,1,0:T(8,128)(2,1)} %broadcast_in_dim.38), calls=%async_computation.2 | async-start | bytes 1835008 | tf_op jit(solution)/shard_map/all_to_all | solution.py:734
  54.0 14.6 %collective-permute-done.2 = bf16[256,512]{1,0:T(8,128)(2,1)S(1)} collective-permute-done((bf16[256,512]{1,0:T(8,128)(2,1)S(1)}, bf16[256,512]{1,0:T(8,128)(2,1)S(1)}, u32[]{:S(2)}, u32[]{:S(2)}) %collective-permute-start.2) | collective-permute-done | bytes 262176 | tf_op jit(solution)/shard_map/ppermute | solution.py:693
  72.4 5.6 %all-to-all-start.3 = ((bf16[4,512,512]{2,1,0:T(8,128)(2,1)}), bf16[4,512,512]{2,1,0:T(8,128)(2,1)S(1)}, u32[]{:S(2)}, u32[]{:S(2)}) async-start(bf16[4,512,512]{2,1,0:T(8,128)(2,1)} %broadcast_in_dim.39), calls=%async_computation.3 | async-start | bytes 4194304 | tf_op jit(solution)/shard_map/all_to_all | solution.py:734
  78.0 22.2 %forward_mixer.1 = (bf16[2,1024,1024]{2,1,0:T(8,128)(2,1)}, f32[2,1024,896]{2,1,0:T(8,128)}, f32[2,1024,512]{2,1,0:T(8,128)}, bf16[2,8,128,512]{3,2,1,0:T(8,128)(2,1)}, bf16[1024,896]{1,0:T(8,128)(2,1)}) custom-call(s32[1]{0:T(128)} %bitcast.6.order_ref, bf16[2,1024,1024]{2,1,0:T(8,128)(2,1)} %all-gather.6.cloned.1.call-done.tokens_ref, f32[1,1024]{1,0:T(1,128)} %bitcast.89, ...), custom_call_target="tpu_custom_call" | custom-call | flops 1100000000 | bytes 2000000 | tf_op jit(solution)/shard_map/forward_mixer/pallas_call | solution.py:496
  103.6 12.8 %gate_stats.1 = (bf16[512,1024]{1,0:T(8,128)(2,1)}, bf16[1024,512]{1,0:T(8,128)(2,1)}, f32[2,1024,512]{2,1,0:T(8,128)}, bf16[2,1024,512]{2,1,0:T(8,128)(2,1)}, f32[2,2,1024]{2,1,0:T(2,128)}) custom-call(s32[1]{0:T(128)} %bitcast.6.order_ref, bf16[2,1024,1024]{2,1,0:T(8,128)(2,1)} %all-gather.4.cloned.1.call-done.up_ref, ...), custom_call_target="tpu_custom_call" | custom-call | flops 1100000000 | bytes 2000000 | tf_op jit(solution)/shard_map/gate_stats/pallas_call | solution.py:529
  116.4 7.0 %all-gather = f32[8,2,1024]{2,1,0:T(2,128)} all-gather(f32[2,2,1024]{2,1,0:T(2,128)} %get-tuple-element.86), channel_id=2, replica_groups=mesh['high'=2,'low'=2,'side'=2,'ctx'=4] {'ctx'}, dimensions={0}, use_global_device_ids=true | all-gather | bytes 81920 | tf_op jit(solution)/shard_map/all_gather | solution.py:869
  123.5 21.5 %gate_back.1 = (bf16[2,512,1024]{2,1,0:T(8,128)(2,1)}, bf16[2,512,1024]{2,1,0:T(8,128)(2,1)}, bf16[512,1024]{1,0:T(8,128)(2,1)}, bf16[1024,512]{1,0:T(8,128)(2,1...) custom-call(s32[4]{0:T(128)} %broadcast_xor_fusion.order_ref, ...), custom_call_target="tpu_custom_call" | custom-call | flops 1100000000 | bytes 2000000 | tf_op jit(solution)/shard_map/gate_back/pallas_call | solution.py:573
  145.3 3.7 %all-to-all-start.4 = ((bf16[8,64,1024]{2,1,0:T(8,128)(2,1)}), bf16[8,64,1024]{2,1,0:T(8,128)(2,1)S(1)}, u32[]{:S(2)}, u32[]{:S(2)}) async-start(bf16[8,64,1024]{2,1,0:T(8,128)(2,1)} %bitcast.82), calls=%async_computation.4 | async-start | bytes 2097152 | tf_op jit(solution)/shard_map/all_to_all | solution.py:734
  153.9 29.2 %mixer_back.2 = (bf16[1,512,1024]{2,1,0:T(8,128)(2,1)}, bf16[1,512,1024]{2,1,0:T(8,128)(2,1)}, f32[1,1024]{1,0:T(1,128)}, f32[1024,896]{1,0:T(8,128)}, f32[8,768...) custom-call(s32[12]{0:T(128)} %pad_add_fusion.table_ref, f32[2,1024,896]{2,1,0:T(8,128)} %get-tuple-element.91.rest_ref.rim_ref, ...), custom_call_target="tpu_custom_call" | custom-call | flops 1100000000 | bytes 2000000 | tf_op jit(solution)/shard_map/mixer_back/pallas_call | solution.py:635
  187.8 5.2 %all-to-all-start.5 = ((bf16[32,32,512]{2,1,0:T(8,128)(2,1)}), bf16[32,32,512]{2,1,0:T(8,128)(2,1)S(1)}, u32[]{:S(2)}, u32[]{:S(2)}) async-start(bf16[32,32,512]{2,1,0:T(8,128)(2,1)} %bitcast.81), calls=%async_computation.5 | async-start | bytes 2097152 | tf_op jit(solution)/shard_map/all_to_all | solution.py:734
  194.3 30.6 %mixer_back.3 = (bf16[1,512,1024]{2,1,0:T(8,128)(2,1)}, bf16[1,512,1024]{2,1,0:T(8,128)(2,1)}, f32[1,1024]{1,0:T(1,128)}, bf16[1024,896]{1,0:T(8,128)(2,1)}, f32...) custom-call(s32[12]{0:T(128)} %pad_add_fusion.table_ref, f32[2,1024,896]{2,1,0:T(8,128)} %get-tuple-element.91.rest_ref.rim_ref, ...), custom_call_target="tpu_custom_call" | custom-call | flops 1100000000 | bytes 2000000 | tf_op jit(solution)/shard_map/mixer_back/pallas_call | solution.py:635
  233.7 2.2 collective-permute-start.15
  235.9 2.4 collective-permute-start.8
  239.5 2.9 collective-permute-start.9
  246.2 4.5 %collective-permute-done.15 = f32[64,1024]{1,0:T(8,128)S(1)} collective-permute-done((f32[64,1024]{1,0:T(8,128)}, f32[64,1024]{1,0:T(8,128)S(1)}, u32[]{:S(2)}, u32[]{:S(2)}) %collective-permute-start.15) | collective-permute-done | bytes 262176 | tf_op jit(solution)/shard_map/ppermute | solution.py:924
  254.3 10.9 %collective-permute-done.14 = bf16[1,256,1024]{2,1,0:T(8,128)(2,1)S(1)} collective-permute-done((bf16[1,256,1024]{2,1,0:T(8,128)(2,1)S(1)}, bf16[1,256,1024]{2,1,0:T(8,128)(2,1)S(1)}, u32[]{:S(2)}, u32[]{:S(2)}) %collective-permute-start.14) | collective-permute-done | bytes 524320 | tf_op jit(solution)/shard_map/ppermute | solution.py:693
  265.2 5.8 %all-to-all-start.6 = ((bf16[32,32,896]{2,1,0:T(8,128)(2,1)}), bf16[32,32,896]{2,1,0:T(8,128)(2,1)S(1)}, u32[]{:S(2)}, u32[]{:S(2)}) async-start(bf16[32,32,896]{2,1,0:T(8,128)(2,1)} %bitcast.78), calls=%async_computation.6 | async-start | bytes 3670016 | tf_op jit(solution)/shard_map/all_to_all | solution.py:734
  280.6 2.2 fusion.7
  282.7 30.5 %all-to-all-done.6 = bf16[32,32,896]{2,1,0:T(8,128)(2,1)S(1)} async-done(((bf16[32,32,896]{2,1,0:T(8,128)(2,1)}), bf16[32,32,896]{2,1,0:T(8,128)(2,1)S(1)}, u32[]{:S(2)}, u32[]{:S(2)}) %all-to-all-start.6) | async-done | bytes 1835040 | tf_op jit(solution)/shard_map/all_to_all | solution.py:734
  (212 shorter events, 62.9 us)
Async XLA Ops:
  7.2 70.8 %all-gather.6.cloned.1.call-start = ((), (), s32[]{:S(2)}) async-start(), calls=%async_computation.8 | async-start | bytes 5242880 | tf_op jit(solution)/shard_map/all_gather | solution.py:819
  7.9 94.3 %all-gather.4.cloned.1.call-start = ((), (), s32[]{:S(2)}) async-start(), calls=%async_computation.7 | async-start | bytes 5242880 | tf_op jit(solution)/shard_map/all_gather | solution.py:820
  9.6 10.3 %all-to-all-start = ((bf16[4,32,1408]{2,1,0:T(8,128)(2,1)}), bf16[4,32,1408]{2,1,0:T(8,128)(2,1)S(1)}, u32[]{:S(2)}, u32[]{:S(2)}) async-start(bf16[4,32,1408]{2,1,0:T(8,128)(2,1)} %bitcast), calls=%async_computation | async-start | bytes 720896 | tf_op jit(solution)/shard_map/all_to_all | solution.py:734
  13.8 12.8 %collective-permute-start.1 = (bf16[64,1024]{1,0:T(8,128)(2,1)S(1)}, bf16[64,1024]{1,0:T(8,128)(2,1)S(1)}, u32[]{:S(2)}, u32[]{:S(2)}) collective-permute-start(bf16[64,1024]{1,0:T(8,128)(2,1)S(1)} %convert_element_type.94), channel_id=1, source_target_pairs={{0,0},{1,4},{2,8},{3,12},{4,16},{5,20},{6,24},{7,28},{8,1},{9,5},{... | collective-permute-start | bytes 393224 | tf_op jit(solution)/shard_map/ppermute | solution.py:784
  27.6 19.1 %all-to-all-start.1 = ((bf16[4,128,896]{2,1,0:T(8,128)(2,1)}), bf16[4,128,896]{2,1,0:T(8,128)(2,1)S(1)}, u32[]{:S(2)}, u32[]{:S(2)}) async-start(bf16[4,128,896]{2,1,0:T(8,128)(2,1)} %broadcast_in_dim.18), calls=%async_computation.1 | async-start | bytes 1835008 | tf_op jit(solution)/shard_map/all_to_all | solution.py:734
  35.9 9.2 %collective-permute-start = (bf16[128,896]{1,0:T(8,128)(2,1)S(1)}, bf16[128,896]{1,0:T(8,128)(2,1)S(1)}, u32[]{:S(2)}, u32[]{:S(2)}) collective-permute-start(bf16[128,896]{1,0:T(8,128)(2,1)S(1)} %slice.269), channel_id=1, source_target_pairs={{0,16},{16,0},{1,17},{17,1},{2,18},{18,2},{3,19},{19,3},{4,20},{20... | collective-permute-start | bytes 688136 | tf_op jit(solution)/shard_map/ppermute | solution.py:693
  47.8 22.9 %all-to-all-start.2 = ((bf16[4,128,896]{2,1,0:T(8,128)(2,1)}), bf16[4,128,896]{2,1,0:T(8,128)(2,1)S(1)}, u32[]{:S(2)}, u32[]{:S(2)}) async-start(bf16[4,128,896]{2,1,0:T(8,128)(2,1)} %broadcast_in_dim.38), calls=%async_computation.2 | async-start | bytes 1835008 | tf_op jit(solution)/shard_map/all_to_all | solution.py:734
  53.8 14.8 %collective-permute-start.2 = (bf16[256,512]{1,0:T(8,128)(2,1)S(1)}, bf16[256,512]{1,0:T(8,128)(2,1)S(1)}, u32[]{:S(2)}, u32[]{:S(2)}) collective-permute-start(bf16[256,512]{1,0:T(8,128)(2,1)S(1)} %pad_maximum_fusion.1), channel_id=1, source_target_pairs={{0,16},{16,0},{1,17},{17,1},{2,18},{18,2},{3,19},{19,3},{4,20},{20... | collective-permute-start | bytes 786440 | tf_op jit(solution)/shard_map/ppermute | solution.py:693
  72.4 29.9 %all-to-all-start.3 = ((bf16[4,512,512]{2,1,0:T(8,128)(2,1)}), bf16[4,512,512]{2,1,0:T(8,128)(2,1)S(1)}, u32[]{:S(2)}, u32[]{:S(2)}) async-start(bf16[4,512,512]{2,1,0:T(8,128)(2,1)} %broadcast_in_dim.39), calls=%async_computation.3 | async-start | bytes 4194304 | tf_op jit(solution)/shard_map/all_to_all | solution.py:734
  145.0 4.4 %collective-permute-start.3 = (bf16[2,512,1024]{2,1,0:T(8,128)(2,1)}, bf16[2,512,1024]{2,1,0:T(8,128)(2,1)S(1)}, u32[]{:S(2)}, u32[]{:S(2)}) collective-permute-start(bf16[2,512,1024]{2,1,0:T(8,128)(2,1)} %get-tuple-element.88), channel_id=1, source_target_pairs={{0,1},{1,0},{2,3},{3,2},{4,5},{5,4},{6,7},{7,6},{8,9},{9,8},{10,11... | collective-permute-start | bytes 6291464 | tf_op jit(solution)/shard_map/ppermute | solution.py:693
  145.3 37.8 %all-to-all-start.4 = ((bf16[8,64,1024]{2,1,0:T(8,128)(2,1)}), bf16[8,64,1024]{2,1,0:T(8,128)(2,1)S(1)}, u32[]{:S(2)}, u32[]{:S(2)}) async-start(bf16[8,64,1024]{2,1,0:T(8,128)(2,1)} %bitcast.82), calls=%async_computation.4 | async-start | bytes 2097152 | tf_op jit(solution)/shard_map/all_to_all | solution.py:734
  152.8 30.4 %collective-permute-start.4 = (bf16[2,256,1024]{2,1,0:T(8,128)(2,1)S(1)}, bf16[2,256,1024]{2,1,0:T(8,128)(2,1)S(1)}, u32[]{:S(2)}, u32[]{:S(2)}) collective-permute-start(bf16[2,256,1024]{2,1,0:T(8,128)(2,1)S(1)} %add_convert_fusion.after_ref.part_ref), channel_id=1, source_target_pairs={{0,2},{1,3},{2,0},{3,1},{4,6},{5,7},{6,4},{7,5},{8,10},{9,11},{10,... | collective-permute-start | bytes 3145736 | tf_op jit(solution)/shard_map/ppermute | solution.py:693
  187.8 42.4 %all-to-all-start.5 = ((bf16[32,32,512]{2,1,0:T(8,128)(2,1)}), bf16[32,32,512]{2,1,0:T(8,128)(2,1)S(1)}, u32[]{:S(2)}, u32[]{:S(2)}) async-start(bf16[32,32,512]{2,1,0:T(8,128)(2,1)} %bitcast.81), calls=%async_computation.5 | async-start | bytes 2097152 | tf_op jit(solution)/shard_map/all_to_all | solution.py:734
  193.0 37.2 %collective-permute-start.12 = (bf16[1,256,1024]{2,1,0:T(8,128)(2,1)S(1)}, bf16[1,256,1024]{2,1,0:T(8,128)(2,1)}, u32[]{:S(2)}, u32[]{:S(2)}) collective-permute-start(bf16[1,256,1024]{2,1,0:T(8,128)(2,1)S(1)} %add_convert_fusion.2.after_ref), channel_id=1, source_target_pairs={{0,2},{1,3},{2,0},{3,1},{4,6},{5,7},{6,4},{7,5},{8,10},{9,11},{10,... | collective-permute-start | bytes 1572872 | tf_op jit(solution)/shard_map/ppermute | solution.py:693
  228.1 3.6 %collective-permute-start.6 = (f32[48,128]{1,0:T(8,128)S(1)}, f32[48,128]{1,0:T(8,128)S(1)}, u32[]{:S(2)}, u32[]{:S(2)}) collective-permute-start(f32[48,128]{1,0:T(8,128)S(1)} %pad_bitcast_fusion), channel_id=1, source_target_pairs={{0,16},{16,0},{1,17},{17,1},{2,18},{18,2},{3,19},{19,3},{4,20},{20... | collective-permute-start | bytes 73736 | tf_op jit(solution)/shard_map/ppermute | solution.py:693
  230.2 22.6 %collective-permute-start.13 = (bf16[1,512,1024]{2,1,0:T(8,128)(2,1)}, bf16[1,512,1024]{2,1,0:T(8,128)(2,1)}, u32[]{:S(2)}, u32[]{:S(2)}) collective-permute-start(bf16[1,512,1024]{2,1,0:T(8,128)(2,1)} %get-tuple-element.120), channel_id=1, source_target_pairs={{0,1},{1,0},{2,3},{3,2},{4,5},{5,4},{6,7},{7,6},{8,9},{9,8},{10,11... | collective-permute-start | bytes 3145736 | tf_op jit(solution)/shard_map/ppermute | solution.py:693
  231.7 4.3 %collective-permute-start.7 = (f32[48,128]{1,0:T(8,128)S(1)}, f32[48,128]{1,0:T(8,128)S(1)}, u32[]{:S(2)}, u32[]{:S(2)}) collective-permute-start(f32[48,128]{1,0:T(8,128)S(1)} %fusion.44), channel_id=1, source_target_pairs={{0,8},{8,0},{1,9},{9,1},{2,10},{10,2},{3,11},{11,3},{4,12},{12,4},... | collective-permute-start | bytes 73736 | tf_op jit(solution)/shard_map/ppermute | solution.py:693
  233.7 17.0 %collective-permute-start.15 = (f32[64,1024]{1,0:T(8,128)}, f32[64,1024]{1,0:T(8,128)S(1)}, u32[]{:S(2)}, u32[]{:S(2)}) collective-permute-start(f32[64,1024]{1,0:T(8,128)} %convert_reduce_fusion.1), channel_id=1, source_target_pairs={{0,0},{4,1},{8,2},{12,3},{16,4},{20,5},{24,6},{28,7},{1,8},{5,9},{... | collective-permute-start | bytes 786440 | tf_op jit(solution)/shard_map/ppermute | solution.py:924
  235.9 3.6 %collective-permute-start.8 = (f32[48,128]{1,0:T(8,128)S(1)}, f32[48,128]{1,0:T(8,128)S(1)}, u32[]{:S(2)}, u32[]{:S(2)}) collective-permute-start(f32[48,128]{1,0:T(8,128)S(1)} %fusion.53), channel_id=1, source_target_pairs={{0,4},{4,0},{1,5},{5,1},{2,6},{6,2},{3,7},{7,3},{8,12},{12,8},{9,1... | collective-permute-start | bytes 73736 | tf_op jit(solution)/shard_map/ppermute | solution.py:693
  239.5 4.7 %collective-permute-start.9 = (f32[48,128]{1,0:T(8,128)S(1)}, f32[48,128]{1,0:T(8,128)S(1)}, u32[]{:S(2)}, u32[]{:S(2)}) collective-permute-start(f32[48,128]{1,0:T(8,128)S(1)} %add.160), channel_id=1, source_target_pairs={{0,2},{1,3},{2,0},{3,1},{4,6},{5,7},{6,4},{7,5},{8,10},{9,11},{10,... | collective-permute-start | bytes 73736 | tf_op jit(solution)/shard_map/ppermute | solution.py:693
  242.5 10.3 %collective-permute-start.11 = (f32[48,128]{1,0:T(8,128)S(1)}, f32[48,128]{1,0:T(8,128)S(1)}, u32[]{:S(2)}, u32[]{:S(2)}) collective-permute-start(f32[48,128]{1,0:T(8,128)S(1)} %add.160), channel_id=1, source_target_pairs={{0,1},{1,0},{2,3},{3,2},{4,5},{5,4},{6,7},{7,6},{8,9},{9,8},{10,11... | collective-permute-start | bytes 73736 | tf_op jit(solution)/shard_map/ppermute | solution.py:693
  244.3 8.5 %collective-permute-start.10 = (f32[48,128]{1,0:T(8,128)S(1)}, f32[48,128]{1,0:T(8,128)S(1)}, u32[]{:S(2)}, u32[]{:S(2)}) collective-permute-start(f32[48,128]{1,0:T(8,128)S(1)} %collective-permute-done.9), channel_id=1, source_target_pairs={{0,1},{1,0},{2,3},{3,2},{4,5},{5,4},{6,7},{7,6},{8,9},{9,8},{10,11... | collective-permute-start | bytes 73736 | tf_op jit(solution)/shard_map/ppermute | solution.py:693
  254.1 11.1 %collective-permute-start.14 = (bf16[1,256,1024]{2,1,0:T(8,128)(2,1)S(1)}, bf16[1,256,1024]{2,1,0:T(8,128)(2,1)S(1)}, u32[]{:S(2)}, u32[]{:S(2)}) collective-permute-start(bf16[1,256,1024]{2,1,0:T(8,128)(2,1)S(1)} %add_convert_fusion.1), channel_id=1, source_target_pairs={{0,2},{1,3},{2,0},{3,1},{4,6},{5,7},{6,4},{7,5},{8,10},{9,11},{10,... | collective-permute-start | bytes 1572872 | tf_op jit(solution)/shard_map/ppermute | solution.py:693
  265.2 48.1 %all-to-all-start.6 = ((bf16[32,32,896]{2,1,0:T(8,128)(2,1)}), bf16[32,32,896]{2,1,0:T(8,128)(2,1)S(1)}, u32[]{:S(2)}, u32[]{:S(2)}) async-start(bf16[32,32,896]{2,1,0:T(8,128)(2,1)} %bitcast.78), calls=%async_computation.6 | async-start | bytes 3670016 | tf_op jit(solution)/shard_map/all_to_all | solution.py:734
  (47 other events, 531.0 us)
Sparse Core Ops, SparseCore 0:
  9.6 36.0 all-gather.5
  47.3 39.2 all-gather.3

commit v6 on v5

--- a/solution.py
+++ b/solution.py
@@ -22,6 +22,7 @@
 LANES = 128
 RIM = 8
 ROWS = 256
+TALL = 512
 
 NORM_EPS = 1e-05
 ADAM_EPS = 1e-08
@@ -244,22 +245,7 @@
     return jnp.broadcast_to(row, (LANES, row.shape[1])).T[:, 0:1]
 
 
-def keep_or_send(refs, kept, value):
-    if len(refs) == 1:
-        refs[0][0] = value
-        return
-
-    @pl.when(kept)
-    def _():
-        refs[0][0] = value
-
-    @pl.when(jnp.logical_not(kept))
-    def _():
-        refs[1][0] = value
-
-
 def gate_back_kernel(
-    order_ref,
     up_ref,
     weight_ref,
     gate_ref,
@@ -297,7 +283,13 @@
     gated = mixed * silu
     unit = gated * scale
     low = (unit * gain).astype(BF16)
-    keep_or_send(branch_refs, pl.program_id(1) < 2, dot(low, weight_ref[...]).astype(BF16))
+    branch = dot(low, weight_ref[...]).astype(BF16)
+    for s, branch_ref in enumerate(branch_refs):
+
+        @pl.when(pl.program_id(0) == s)
+        def _(branch_ref=branch_ref):
+            branch_ref[0] = branch
+
     total[...] += dot(low, up_ref[0], COL_COL)
     d_gain_ref[...] += jnp.sum(d_out * unit, axis=0, keepdims=True)
     d_gated = scale * (gain * d_out - unit * (scale * products * (1.0 / DI)))
@@ -315,7 +307,6 @@
 def mixer_back_kernel(
     inner,
     first,
-    table_ref,
     rest_ref,
     rim_ref,
     mixed_ref,
@@ -331,10 +322,19 @@
     weight_rest_ref,
     after_ref,
     part_ref,
-    *refs,
+    d_normed_ref,
+    d_gain_ref,
+    grad_ref,
+    d_taps_ref,
+    d_heads_ref,
+    d_skip_ref,
+    padded,
+    later,
+    carried,
+    d_active,
+    total,
+    d_rest_ref,
 ):
-    *normed_refs, d_gain_ref, grad_ref, d_taps_ref, d_heads_ref, d_skip_ref = refs[:-6]
-    padded, later, carried, d_active, total, d_rest_ref = refs[-6:]
     rows = rest_ref.shape[1]
     conv = inner + 2 * NS
     block = pl.num_programs(0) - 1 - pl.program_id(0)
@@ -447,7 +447,7 @@
     tokens = tokens_ref[0].astype(F32)
     scale = lax.rsqrt(jnp.mean(tokens * tokens, axis=1, keepdims=True) + NORM_EPS)
     d_gain_ref[...] += jnp.sum(d_normed * (tokens * scale), axis=0, keepdims=True)
-    keep_or_send(normed_refs, table_ref[pl.program_id(0)] == 1, d_normed.astype(BF16))
+    d_normed_ref[0] = d_normed.astype(BF16)
 
     @pl.when(block == 0)
     def _():
@@ -458,12 +458,8 @@
     return pl.BlockSpec(shape, lambda *_: (0,) * len(shape))
 
 
-def by_rows(width):
-    return pl.BlockSpec((1, ROWS, width), lambda s, b, *_: (s, b, 0))
-
-
-def by_order(width):
-    return pl.BlockSpec((1, ROWS, width), lambda s, b, order: (s, order[b], 0))
+def by_rows(width, rows=ROWS):
+    return pl.BlockSpec((1, rows, width), lambda s, b, *_: (s, b, 0))
 
 
 def left_alone():
@@ -530,14 +526,14 @@
         functools.partial(stats_kernel, joined),
         grid_spec=pltpu.PrefetchScalarGridSpec(
             num_scalar_prefetch=1,
-            grid=(count, length // ROWS),
-            in_specs=[by_rows(D), by_rows(D), by_rows(inner), whole((1, inner))]
+            grid=(count, length // TALL),
+            in_specs=[by_rows(D, TALL), by_rows(D, TALL), by_rows(inner, TALL), whole((1, inner))]
             + [whole(weight.shape) for weight in weights],
             out_specs=found_specs
             + [
-                by_rows(inner),
-                by_rows(inner),
-                pl.BlockSpec((1, 2, ROWS), lambda s, b, *_: (s, 0, b)),
+                by_rows(inner, TALL),
+                by_rows(inner, TALL),
+                pl.BlockSpec((1, 2, TALL), lambda s, b, *_: (s, 0, b)),
             ],
         ),
         out_shape=found_shapes
@@ -553,51 +549,38 @@
     return found if joined else [*weights, *found]
 
 
-def kept_and_sent(split, count, length, place):
-    if not split:
-        return [place(lambda order, b: order[b])], [shaped((count, length, D), BF16)]
-    specs = [
-        place(lambda order, b: jnp.minimum(b, 1)),
-        place(lambda order, b: jnp.maximum(b - 2, 0)),
-    ]
-    return specs, [shaped((count, 2 * ROWS, D), BF16)] * 2
-
-
-def run_gate_back(split, order, upstream, weight, gate, mixed, gate_gain, d_out, stats, low):
+def run_gate_back(upstream, weight, gate, mixed, gate_gain, d_out, stats, low):
     count, length, inner = gate.shape
-
-    def place(group):
-        return pl.BlockSpec((1, ROWS, D), lambda s, b, order: (s, group(order, b), 0))
-
-    branch_specs, branch_shapes = kept_and_sent(split, count, length, place)
+    last = length // TALL - 1
+
+    def branch_rows(own):
+        def place(s, b):
+            return (0, jnp.where(s < own, 0, jnp.where(s > own, last, b)), 0)
+
+        return pl.BlockSpec((1, TALL, D), place)
+
     return pl.pallas_call(
         gate_back_kernel,
-        grid_spec=pltpu.PrefetchScalarGridSpec(
-            num_scalar_prefetch=1,
-            grid=(count, length // ROWS),
-            in_specs=[
-                by_order(D),
-                whole((inner, D)),
-                by_order(inner),
-                by_order(inner),
-                whole((1, inner)),
-                by_order(inner),
-                pl.BlockSpec(
-                    (stats.shape[0], 1, 2, ROWS), lambda s, b, order: (0, s, 0, order[b])
-                ),
-                by_order(D),
-            ],
-            out_specs=branch_specs
-            + [
-                whole((inner, D)),
-                whole((D, inner)),
-                by_order(inner),
-                by_order(inner),
-                whole((1, inner)),
-            ],
-            scratch_shapes=[pltpu.VMEM((inner, D), F32), pltpu.VMEM((D, inner), F32)],
-        ),
-        out_shape=branch_shapes
+        grid=(count, length // TALL),
+        in_specs=[
+            by_rows(D, TALL),
+            whole((inner, D)),
+            by_rows(inner, TALL),
+            by_rows(inner, TALL),
+            whole((1, inner)),
+            by_rows(inner, TALL),
+            pl.BlockSpec((stats.shape[0], 1, 2, TALL), lambda s, b: (0, s, 0, b)),
+            by_rows(D, TALL),
+        ],
+        out_specs=[branch_rows(s) for s in range(count)]
+        + [
+            whole((inner, D)),
+            whole((D, inner)),
+            by_rows(inner, TALL),
+            by_rows(inner, TALL),
+            whole((1, inner)),
+        ],
+        out_shape=[shaped((1, length, D), BF16)] * count
         + [
             shaped((inner, D), BF16),
             shaped((D, inner), BF16),
@@ -605,13 +588,14 @@
             shaped((count, length, inner), BF16),
             shaped((1, inner)),
         ],
+        scratch_shapes=[pltpu.VMEM((inner, D), F32), pltpu.VMEM((D, inner), F32)],
         compiler_params=params(),
         cost_estimate=cost(1),
         name="gate_back",
-    )(order, upstream, weight, gate, mixed, gate_gain, d_out, stats, low)
-
-
-def run_mixer_back(split, s, table, saved, fixed, weights, after, part):
+    )(upstream, weight, gate, mixed, gate_gain, d_out, stats, low)
+
+
+def run_mixer_back(s, saved, fixed, weights, after, part):
     rest, mixed, d_mixed, incoming, low, d_gate, tokens = saved
     taps, heads, skip = fixed
     count, length, inner = mixed.shape
@@ -621,71 +605,59 @@
     width = rest.shape[2]
 
     def rows(width):
-        return pl.BlockSpec((1, ROWS, width), lambda b, table: (s, last - b, 0))
-
-    if split:
-        normed_specs = [
-            pl.BlockSpec((1, ROWS, D), lambda b, table: (0, table[4 + b], 0)),
-            pl.BlockSpec((1, ROWS, D), lambda b, table: (0, table[8 + b], 0)),
-        ]
-        normed_shapes = [shaped((1, 2 * ROWS, D), BF16)] * 2
-    else:
-        normed_specs = [pl.BlockSpec((1, ROWS, D), lambda b, table: (0, last - b, 0))]
-        normed_shapes = [shaped((1, length, D), BF16)]
+        return pl.BlockSpec((1, ROWS, width), lambda b: (s, last - b, 0))
+
     return pl.pallas_call(
         functools.partial(mixer_back_kernel, inner, s == 0),
-        grid_spec=pltpu.PrefetchScalarGridSpec(
-            num_scalar_prefetch=1,
-            grid=(length // ROWS,),
-            in_specs=[
-                rows(width),
-                pl.BlockSpec(
-                    (1, RIM, width),
-                    lambda b, table: (s, jnp.maximum((last - b) * (ROWS // RIM) - 1, 0), 0),
-                ),
-                rows(inner),
-                rows(inner),
-                pl.BlockSpec((1, chunks, NS, inner), lambda b, table: (s, last - b, 0, 0)),
-                whole((RIM, conv)),
-                whole((8, LANES)),
-                whole((1, inner)),
-                rows(D),
-                rows(inner),
-                rows(D),
-                whole((D, inner)),
-                whole((D, width)),
-                left_alone(),
-                left_alone(),
-            ],
-            out_specs=normed_specs
-            + [
-                whole((1, D)),
-                whole((D, width)),
-                whole((RIM, conv)),
-                whole((8, LANES)),
-                whole((1, inner)),
-            ],
-            scratch_shapes=[
-                pltpu.VMEM((RIM + ROWS, conv), F32),
-                pltpu.VMEM((RIM + ROWS, conv), F32),
-                pltpu.VMEM((NS, inner), F32),
-                pltpu.VMEM((ROWS, conv), F32),
-                pltpu.VMEM((D, width), F32),
-                pltpu.VMEM((ROWS, width), BF16),
-            ],
-        ),
-        out_shape=normed_shapes
-        + [
+        grid=(length // ROWS,),
+        in_specs=[
+            rows(width),
+            pl.BlockSpec(
+                (1, RIM, width),
+                lambda b: (s, jnp.maximum((last - b) * (ROWS // RIM) - 1, 0), 0),
+            ),
+            rows(inner),
+            rows(inner),
+            pl.BlockSpec((1, chunks, NS, inner), lambda b: (s, last - b, 0, 0)),
+            whole((RIM, conv)),
+            whole((8, LANES)),
+            whole((1, inner)),
+            rows(D),
+            rows(inner),
+            rows(D),
+            whole((D, inner)),
+            whole((D, width)),
+            left_alone(),
+            left_alone(),
+        ],
+        out_specs=[
+            pl.BlockSpec((1, ROWS, D), lambda b: (0, last - b, 0)),
+            whole((1, D)),
+            whole((D, width)),
+            whole((RIM, conv)),
+            whole((8, LANES)),
+            whole((1, inner)),
+        ],
+        out_shape=[
+            shaped((1, length, D), BF16),
             shaped((1, D)),
             shaped((D, width), BF16 if s == count - 1 else F32),
             shaped((RIM, conv)),
             shaped((8, LANES)),
             shaped((1, inner)),
         ],
+        scratch_shapes=[
+            pltpu.VMEM((RIM + ROWS, conv), F32),
+            pltpu.VMEM((RIM + ROWS, conv), F32),
+            pltpu.VMEM((NS, inner), F32),
+            pltpu.VMEM((ROWS, conv), F32),
+            pltpu.VMEM((D, width), F32),
+            pltpu.VMEM((ROWS, width), BF16),
+        ],
         compiler_params=params(),
         cost_estimate=cost(1),
         name="mixer_back",
-    )(table, rest, rest, mixed, d_mixed, incoming, *fixed, low, d_gate, tokens, *weights, after, part)
+    )(rest, rest, mixed, d_mixed, incoming, *fixed, low, d_gate, tokens, *weights, after, part)
 
 
 def swapped(value, axis, mask=1):
@@ -693,22 +665,8 @@
     return lax.ppermute(value, axis, [(a, a ^ mask) for a in range(count)])
 
 
-def chip_sums(parts):
-    if len(parts) == 1:
-        total = lax.psum_scatter(parts[0], "ctx", scatter_dimension=1, tiled=True)
-        return total.astype(F32), None
-    kept, sent = parts
-    got = swapped(sent, "ctx", 1)
-    own = kept[:, :ROWS].astype(F32) + got[:, :ROWS].astype(F32)
-    return own, (kept[:, ROWS:].astype(F32) + got[:, ROWS:].astype(F32)).astype(BF16)
-
-
-def across(sent):
-    return [] if sent is None else [swapped(sent, "ctx", 2)]
-
-
-def added(own, got):
-    return own + got[0].astype(F32) if got else own
+def summed_over_ctx(value):
+    return lax.psum_scatter(value, "ctx", scatter_dimension=1, tiled=True)
 
 
 def sum_over(value, axes):
@@ -800,22 +758,8 @@
     head_rows = jnp.pad(jnp.stack([dt_bias, decay]), ((0, 6), (0, LANES - heads)))
     skip = jnp.repeat(lax.dynamic_slice(pieces[6], (rank * heads,), (heads,)), HD).reshape(1, inner)
 
-    split = n_ctx == 4 and block_in.shape[1] == ROWS
-    order = jnp.arange(n_ctx * block_in.shape[1] // ROWS, dtype=jnp.int32)
-    if split:
-        order = rank.astype(jnp.int32) ^ jnp.array([0, 2, 1, 3], jnp.int32)
     high = lax.axis_index(dp[0]) if len(dp) > 1 else rank * 0
     high = high.astype(jnp.int32).reshape(1)
-    table = jnp.zeros((12,), jnp.int32)
-    if split:
-        masks = rank.astype(jnp.int32) ^ jnp.array([3, 2, 1, 0], jnp.int32)
-        kept = 1 - (masks & 1)
-        places = masks >> 1
-        early, late = places[jnp.array([0, 0, 2, 2])], places[jnp.array([1, 1, 1, 3])]
-        one_first = kept[0] == 1
-        table = jnp.concatenate(
-            [kept, jnp.where(one_first, early, late), jnp.where(one_first, late, early)]
-        )
     tokens = lax.all_gather(block_in, "ctx", axis=1, tiled=True)
     upstream = lax.all_gather(out_grad, "ctx", axis=1, tiled=True)
     w_in_low = w_in.astype(BF16)
@@ -844,10 +788,8 @@
         other_both = swapped(mine_both, dp[0])
         mine_rest, mine_out = lax.optimization_barrier((mine_rest, mine_out))
         first_half = to_every(mine_rest, dp[1:])
-        other_rest, taps, head_rows, skip, norm_gain, gate_gain, order, high, table = (
-            lax.optimization_barrier(
-                (other_rest, taps, head_rows, skip, norm_gain, gate_gain, order, high, table)
-            )
+        other_rest, taps, head_rows, skip, norm_gain, gate_gain, high = lax.optimization_barrier(
+            (other_rest, taps, head_rows, skip, norm_gain, gate_gain, high)
         )
         weight_halves = [first_half, to_every(other_rest, dp[1:])]
         both = jnp.concatenate([mine_both, other_both], axis=0)
@@ -867,43 +809,37 @@
         high, upstream, low, mixed, gate_gain, weights
     )
     stats = lax.all_gather(stats, "ctx")
-    *branch, grad_out, grad_gate, d_mixed, d_gate, d_gate_gain = run_gate_back(
-        split, order, upstream, weight_out, gate, mixed, gate_gain, d_out, stats, low
+    *branches, grad_out, grad_gate, d_mixed, d_gate, d_gate_gain = run_gate_back(
+        upstream, weight_out, gate, mixed, gate_gain, d_out, stats, low
     )
     grad_out = to_all(grad_out, dp)
-    branch, branch_sent = chip_sums(branch)
+    branches = [summed_over_ctx(branch) for branch in branches]
 
     own_rows = w_in.shape[0]
 
     def summed(got):
         return jnp.sum(got.astype(F32).reshape(-1, n_ctx, own_rows, got.shape[1]), axis=0)
 
-    after = grad_gate if branch_sent is None else branch_sent
-    branch_got = across(branch_sent)
     saved = (rest, mixed, d_mixed, incoming, low, d_gate, tokens)
     fixed = (taps, head_rows, skip)
     weights = (weight_gate, weight_rest)
-    grad_rest = after
+    after = grad_rest = d_gate
     smalls = []
-    owns = []
     normeds = []
     for s in range(count):
-        found = run_mixer_back(split, s, table, saved, fixed, weights, after, grad_rest)
-        *d_normed, d_gain, grad_rest, d_taps, d_heads, d_skip = found
+        d_normed, d_gain, grad_rest, d_taps, d_heads, d_skip = run_mixer_back(
+            s, saved, fixed, weights, after, grad_rest
+        )
+        normeds.append(summed_over_ctx(d_normed))
+        branches[s], d_gain = lax.optimization_barrier((branches[s], d_gain))
+        if s == 0:
+            grad_gate, branches[s], d_gain, after = lax.optimization_barrier(
+                (grad_gate, branches[s], d_gain, grad_out)
+            )
+            grad_gate = to_all(grad_gate, axes)
+        else:
+            grad_gate, d_gain = lax.optimization_barrier((grad_gate, d_gain))
         smalls.append([d_gain, d_taps, d_heads, d_skip])
-        if s == 0:
-            grad_out, branch_got, d_normed = lax.optimization_barrier(
-                (grad_out, branch_got, d_normed)
-            )
-        else:
-            grad_gate, normeds, d_normed = lax.optimization_barrier((grad_gate, normeds, d_normed))
-        own, normed_sent = chip_sums(d_normed)
-        after = own if normed_sent is None else normed_sent
-        if s == 0:
-            grad_gate, after = lax.optimization_barrier((grad_gate, after))
-            grad_gate = to_all(grad_gate, axes)
-        owns.append(own)
-        normeds.append(across(normed_sent))
     d_norm_gain, d_taps, d_heads, d_skip = (sum(parts) for parts in zip(*smalls))
     parts = (
         d_norm_gain.reshape(-1),
@@ -916,10 +852,9 @@
     mine = jnp.concatenate(parts)
     mine = jnp.pad(mine, (0, -mine.shape[0] % (8 * LANES))).reshape(-1, LANES)
     every = by_rank(sum_over(mine, dp)).reshape(n_ctx, -1)
-    grad_rest, every, normeds = lax.optimization_barrier((grad_rest, every, normeds))
+    grad_rest, every = lax.optimization_barrier((grad_rest, every))
     grad_rest = to_all(grad_rest, axes)
-    d_normed = jnp.concatenate([added(own, got) for own, got in zip(owns, normeds)], axis=0)
-    branch = added(branch, branch_got)
+    d_normed = jnp.concatenate(normeds, axis=0).astype(F32)
     grad_out = jnp.sum(grad_out.astype(F32).reshape(n_dp, -1, D), axis=0)
     grad_out = lax.ppermute(grad_out, axes, [(b, a) for a, b in moves])
     grad_gate = summed(grad_gate)
@@ -949,6 +884,7 @@
     )
 
     own = block_in.astype(F32)
+    branch = jnp.concatenate(branches, axis=0)
     block_out = (own + branch.astype(F32)).astype(BF16)
     scale = lax.rsqrt(jnp.mean(own * own, axis=-1, keepdims=True) + NORM_EPS)
     d_scaled = d_normed * norm_gain

time: 327 us -> 334 us (1.021)
  waiting for transfers between devices: 85.7 us -> 121 us
  other arithmetic: 22.6 us -> 13.7 us
  Pallas kernels: 116 us -> 109 us
  local copies, waits for them, and re-layouts: 17.6 us -> 11.4 us
  starting transfers between devices: 59.7 us -> 55 us
    ppermute x1, waiting for transfers between devices: 4.54 us -> 50.5 us  [shards(): grad_out = lax.ppermute(grad_out, axes, [(b, a) for a, b in moves])]
    ppermute x14 -> x8, waiting for transfers between devices: 35 us -> 28.9 us  [swapped(): return lax.ppermute(value, axis, [(a, a ^ mask) for a in range(count)])]
    pallas_call x3, Pallas kernels: 81.4 us -> 75.6 us  [the longest x2 57.5 us: run_mixer_back(): pl.pallas_call(functools.partial(mixer_back_kernel, inner, s == 0), grid=...]
    ppermute x14 -> x8, starting transfers between devices: 16.9 us -> 11.5 us  [swapped(): return lax.ppermute(value, axis, [(a, a ^ mask) for a in range(count)])]
    all_to_all x7, waiting for transfers between devices: 38.2 us -> 33.1 us  [to_all(): return lax.all_to_all(value, axes, split_axis=0, concat_axis=0, tiled=True)]
    convert_element_type x3 -> x0, other arithmetic: 4.77 us -> none  [chip_sums(): (kept[:, ROWS:].astype(F32) + got[:, ROWS:].astype(F32)).astype(BF16)]
  transfers between devices with their start and end apart: 25 -> 23, of which waited for: 14 -> 13; matrix products, arithmetic and copies ran while one was open for 9% -> 6% of each run, Pallas kernels for 25% -> 24%
where the time goes in v6:
time: 334 us; the launch traced here: 333 us
  waiting for transfers between devices  121 us (36%)
  Pallas kernels  109 us (33%)
  starting transfers between devices  55 us (16%)
  between operations  14.8 us (4%)
  other arithmetic  13.7 us (4%)
  local copies, waits for them, and re-layouts  11.4 us (3%)
  blocking collectives  7.01 us (2%)
    pallas_call x2, Pallas kernels, run_mixer_back(): pl.pallas_call(functools.partial(mixer_back_kernel, inner, s == 0), grid=...  57.5 us
    ppermute x1, waiting for transfers between devices, shards(): grad_out = lax.ppermute(grad_out, axes, [(b, a) for a, b in moves])  50.5 us
    all_to_all x7, starting transfers between devices, to_all(): return lax.all_to_all(value, axes, split_axis=0, concat_axis=0, tiled=True)  35.3 us
    all_to_all x7, waiting for transfers between devices, to_all(): return lax.all_to_all(value, axes, split_axis=0, concat_axis=0, tiled=True)  33.1 us
    ppermute x8, waiting for transfers between devices, swapped(): return lax.ppermute(value, axis, [(a, a ^ mask) for a in range(count)])  28.9 us
    pallas_call x1, Pallas kernels, run_forward(): pl.pallas_call(functools.partial(forward_kernel, inner), grid_spec=pltpu....  22.2 us
    pallas_call x1, Pallas kernels, run_gate_back(): pl.pallas_call(gate_back_kernel, grid=(count, length // TALL), in_specs=[...  18.1 us
    pallas_call x1, Pallas kernels, run_stats(): pl.pallas_call(functools.partial(stats_kernel, joined), grid_spec=pltpu.P...  11.5 us
  transfers between devices with their start and end apart: 23, of which 13 were waited for; matrix products, arithmetic and copies ran while one was open for 6% of the time, Pallas kernels for 24%

profile of v6, /device:TPU:5, one launch (start us, length us, event | category | flops | bytes accessed | tf_op | source)
XLA Modules:
  0.0 332.6 jit_solution(10398257499696538128)
XLA Ops:
  9.6 4.1 %all-to-all-start = ((bf16[4,32,1408]{2,1,0:T(8,128)(2,1)}), bf16[4,32,1408]{2,1,0:T(8,128)(2,1)S(1)}, u32[]{:S(2)}, u32[]{:S(2)}) async-start(bf16[4,32,1408]{2,1,0:T(8,128)(2,1)} %bitcast), calls=%async_computation | async-start | bytes 720896 | tf_op jit(solution)/shard_map/all_to_all | solution.py:692
  13.8 4.3 %collective-permute-start.1 = (bf16[64,1024]{1,0:T(8,128)(2,1)S(1)}, bf16[64,1024]{1,0:T(8,128)(2,1)S(1)}, u32[]{:S(2)}, u32[]{:S(2)}) collective-permute-start(bf16[64,1024]{1,0:T(8,128)(2,1)S(1)} %convert_element_type.49), channel_id=1, source_target_pairs={{0,0},{1,4},{2,8},{3,12},{4,16},{5,20},{6,24},{7,28},{8,1},{9,5},{... | collective-permute-start | bytes 393224 | tf_op jit(solution)/shard_map/ppermute | solution.py:742
  20.0 6.7 %collective-permute-done.1 = bf16[64,1024]{1,0:T(8,128)(2,1)S(1)} collective-permute-done((bf16[64,1024]{1,0:T(8,128)(2,1)S(1)}, bf16[64,1024]{1,0:T(8,128)(2,1)S(1)}, u32[]{:S(2)}, u32[]{:S(2)}) %collective-permute-start.1) | collective-permute-done | bytes 131104 | tf_op jit(solution)/shard_map/ppermute | solution.py:742
  27.7 5.8 %all-to-all-start.1 = ((bf16[4,128,896]{2,1,0:T(8,128)(2,1)}), bf16[4,128,896]{2,1,0:T(8,128)(2,1)S(1)}, u32[]{:S(2)}, u32[]{:S(2)}) async-start(bf16[4,128,896]{2,1,0:T(8,128)(2,1)} %broadcast_in_dim.12), calls=%async_computation.1 | async-start | bytes 1835008 | tf_op jit(solution)/shard_map/all_to_all | solution.py:692
  37.1 7.8 %collective-permute-done = bf16[128,896]{1,0:T(8,128)(2,1)S(1)} collective-permute-done((bf16[128,896]{1,0:T(8,128)(2,1)S(1)}, bf16[128,896]{1,0:T(8,128)(2,1)S(1)}, u32[]{:S(2)}, u32[]{:S(2)}) %collective-permute-start) | collective-permute-done | bytes 229408 | tf_op jit(solution)/shard_map/ppermute | solution.py:665
  47.6 6.0 %all-to-all-start.2 = ((bf16[4,128,896]{2,1,0:T(8,128)(2,1)}), bf16[4,128,896]{2,1,0:T(8,128)(2,1)S(1)}, u32[]{:S(2)}, u32[]{:S(2)}) async-start(bf16[4,128,896]{2,1,0:T(8,128)(2,1)} %broadcast_in_dim.13), calls=%async_computation.2 | async-start | bytes 1835008 | tf_op jit(solution)/shard_map/all_to_all | solution.py:692
  53.8 14.7 %collective-permute-done.2 = bf16[256,512]{1,0:T(8,128)(2,1)S(1)} collective-permute-done((bf16[256,512]{1,0:T(8,128)(2,1)S(1)}, bf16[256,512]{1,0:T(8,128)(2,1)S(1)}, u32[]{:S(2)}, u32[]{:S(2)}) %collective-permute-start.2) | collective-permute-done | bytes 262176 | tf_op jit(solution)/shard_map/ppermute | solution.py:665
  72.4 5.6 %all-to-all-start.3 = ((bf16[4,512,512]{2,1,0:T(8,128)(2,1)}), bf16[4,512,512]{2,1,0:T(8,128)(2,1)S(1)}, u32[]{:S(2)}, u32[]{:S(2)}) async-start(bf16[4,512,512]{2,1,0:T(8,128)(2,1)} %broadcast_in_dim.14), calls=%async_computation.3 | async-start | bytes 4194304 | tf_op jit(solution)/shard_map/all_to_all | solution.py:692
  78.0 22.2 %forward_mixer.1 = (bf16[2,1024,1024]{2,1,0:T(8,128)(2,1)}, f32[2,1024,896]{2,1,0:T(8,128)}, f32[2,1024,512]{2,1,0:T(8,128)}, bf16[2,8,128,512]{3,2,1,0:T(8,128)(2,1)}, bf16[1024,896]{1,0:T(8,128)(2,1)}) custom-call(s32[1]{0:T(128)} %bitcast.6.order_ref, bf16[2,1024,1024]{2,1,0:T(8,128)(2,1)} %all-gather.6.cloned.1.call-done.tokens_ref, f32[1,1024]{1,0:T(1,128)} %bitcast.84, ...), custom_call_target="tpu_custom_call" | custom-call | flops 1100000000 | bytes 2000000 | tf_op jit(solution)/shard_map/forward_mixer/pallas_call | solution.py:492
  103.6 11.5 %gate_stats.1 = (bf16[512,1024]{1,0:T(8,128)(2,1)}, bf16[1024,512]{1,0:T(8,128)(2,1)}, f32[2,1024,512]{2,1,0:T(8,128)}, bf16[2,1024,512]{2,1,0:T(8,128)(2,1)}, f32[2,2,1024]{2,1,0:T(2,128)}) custom-call(s32[1]{0:T(128)} %bitcast.6.order_ref, bf16[2,1024,1024]{2,1,0:T(8,128)(2,1)} %all-gather.4.cloned.1.call-done.up_ref, ...), custom_call_target="tpu_custom_call" | custom-call | flops 1100000000 | bytes 2000000 | tf_op jit(solution)/shard_map/gate_stats/pallas_call | solution.py:525
  115.1 7.0 %all-gather = f32[8,2,1024]{2,1,0:T(2,128)} all-gather(f32[2,2,1024]{2,1,0:T(2,128)} %get-tuple-element.79), channel_id=2, replica_groups=mesh['high'=2,'low'=2,'side'=2,'ctx'=4] {'ctx'}, dimensions={0}, use_global_device_ids=true | all-gather | bytes 81920 | tf_op jit(solution)/shard_map/all_gather | solution.py:811
  122.1 18.1 %gate_back.1 = (bf16[1,1024,1024]{2,1,0:T(8,128)(2,1)}, bf16[1,1024,1024]{2,1,0:T(8,128)(2,1)}, bf16[512,1024]{1,0:T(8,128)(2,1)}, bf16[1024,512]{1,0:T(8,128)(2...) custom-call(bf16[2,1024,1024]{2,1,0:T(8,128)(2,1)} %all-gather.4.cloned.1.call-done.up_ref, ...), custom_call_target="tpu_custom_call" | custom-call | flops 1100000000 | bytes 2000000 | tf_op jit(solution)/shard_map/gate_back/pallas_call | solution.py:562
  141.1 28.2 %mixer_back.2 = (bf16[1,1024,1024]{2,1,0:T(8,128)(2,1)}, f32[1,1024]{1,0:T(1,128)}, f32[1024,896]{1,0:T(8,128)}, f32[8,768]{1,0:T(8,128)}, f32[8,128]{1,0:T(8,128)}, /*index=5*/f32[1,512]{1,0:T(1,128)}) custom-call(f32[2,1024,896]{2,1,0:T(8,128)} %get-tuple-element.82.rest_ref.rim_ref, f32[2,1024,896]{2,1,0:T(8,128)} %get-tuple-element.82.rest_ref.rim_ref, ...), custom_call_target="tpu_custom_call" | custom-call | flops 1100000000 | bytes 2000000 | tf_op jit(solution)/shard_map/mixer_back/pallas_call | solution.py:610
  169.3 3.9 %all-to-all-start.4 = ((bf16[8,64,1024]{2,1,0:T(8,128)(2,1)}), bf16[8,64,1024]{2,1,0:T(8,128)(2,1)S(1)}, u32[]{:S(2)}, u32[]{:S(2)}) async-start(bf16[8,64,1024]{2,1,0:T(8,128)(2,1)} %bitcast.11), calls=%async_computation.5 | async-start | bytes 2097152 | tf_op jit(solution)/shard_map/all_to_all | solution.py:692
  173.2 25.4 %all-to-all-done.4 = bf16[8,64,1024]{2,1,0:T(8,128)(2,1)S(1)} async-done(((bf16[8,64,1024]{2,1,0:T(8,128)(2,1)}), bf16[8,64,1024]{2,1,0:T(8,128)(2,1)S(1)}, u32[]{:S(2)}, u32[]{:S(2)}) %all-to-all-start.4) | async-done | bytes 1048608 | tf_op jit(solution)/shard_map/all_to_all | solution.py:692
  198.7 4.1 %all-to-all-start.5 = ((bf16[32,32,512]{2,1,0:T(8,128)(2,1)}), bf16[32,32,512]{2,1,0:T(8,128)(2,1)S(1)}, u32[]{:S(2)}, u32[]{:S(2)}) async-start(bf16[32,32,512]{2,1,0:T(8,128)(2,1)} %bitcast.14), calls=%async_computation.9 | async-start | bytes 2097152 | tf_op jit(solution)/shard_map/all_to_all | solution.py:692
  203.1 29.3 %mixer_back.3 = (bf16[1,1024,1024]{2,1,0:T(8,128)(2,1)}, f32[1,1024]{1,0:T(1,128)}, bf16[1024,896]{1,0:T(8,128)(2,1)}, f32[8,768]{1,0:T(8,128)}, f32[8,128]{1,0:T(8,128)}, /*index=5*/f32[1,512]{1,0:T(1,128)}) custom-call(f32[2,1024,896]{2,1,0:T(8,128)} %get-tuple-element.82.rest_ref.rim_ref, f32[2,1024,896]{2,1,0:T(8,128)} %get-tuple-element.82.rest_ref.rim_ref, ...), custom_call_target="tpu_custom_call" | custom-call | flops 1100000000 | bytes 2000000 | tf_op jit(solution)/shard_map/mixer_back/pallas_call | solution.py:610
  240.2 2.6 collective-permute-done.5
  243.9 4.4 %collective-permute-start.8 = (f32[48,128]{1,0:T(8,128)S(1)}, f32[48,128]{1,0:T(8,128)S(1)}, u32[]{:S(2)}, u32[]{:S(2)}) collective-permute-start(f32[48,128]{1,0:T(8,128)S(1)} %add.129), channel_id=1, source_target_pairs={{0,1},{1,0},{2,3},{3,2},{4,5},{5,4},{6,7},{7,6},{8,9},{9,8},{10,11... | collective-permute-start | bytes 73736 | tf_op jit(solution)/shard_map/ppermute | solution.py:665
  248.3 2.4 collective-permute-start.7
  251.7 5.7 %all-to-all-start.6 = ((bf16[32,32,896]{2,1,0:T(8,128)(2,1)}), bf16[32,32,896]{2,1,0:T(8,128)(2,1)S(1)}, u32[]{:S(2)}, u32[]{:S(2)}) async-start(bf16[32,32,896]{2,1,0:T(8,128)(2,1)} %bitcast.75), calls=%async_computation.10 | async-start | bytes 3670016 | tf_op jit(solution)/shard_map/all_to_all | solution.py:692
  257.6 3.2 collective-permute-start.9
  260.9 50.5 %collective-permute-done.9 = f32[64,1024]{1,0:T(8,128)S(1)} collective-permute-done((f32[64,1024]{1,0:T(8,128)S(1)}, f32[64,1024]{1,0:T(8,128)S(1)}, u32[]{:S(2)}, u32[]{:S(2)}) %collective-permute-start.9) | collective-permute-done | bytes 262176 | tf_op jit(solution)/shard_map/ppermute | solution.py:859
  318.5 3.5 %fusion.7 = (bf16[2,256,1024]{2,1,0:T(8,128)(2,1)}, bf16[2,256,1024]{2,1,0:T(8,128)(2,1)}) fusion(bf16[2,256,1024]{2,1,0:T(8,128)(2,1)S(1)} %copy-done.2, bf16[2,256,1024]{2,1,0:T(8,128)(2,1)S(1)} %copy-done.6, f32[2,256]{1,0:T(2,128)S(1)} %broadcast_multiply_fusion, f32[1024]{0:T(1024)S(1)} %copy-done.22, f32[2,256]{1,0:T(2,128)S(1)} %add_rsqrt_fusion, ...), kind=kLoop, calls=%fused_computation.12 | loop fusion | flops 8388608 | bytes 6299648 | tf_op jit(solution)/shard_map/convert_element_type | solution.py:894
  (175 shorter events, 40.4 us)
Async XLA Ops:
  7.2 70.8 %all-gather.6.cloned.1.call-start = ((), (), s32[]{:S(2)}) async-start(), calls=%async_computation.12 | async-start | bytes 5242880 | tf_op jit(solution)/shard_map/all_gather | solution.py:763
  7.9 94.3 %all-gather.4.cloned.1.call-start = ((), (), s32[]{:S(2)}) async-start(), calls=%async_computation.11 | async-start | bytes 5242880 | tf_op jit(solution)/shard_map/all_gather | solution.py:764
  9.6 10.3 %all-to-all-start = ((bf16[4,32,1408]{2,1,0:T(8,128)(2,1)}), bf16[4,32,1408]{2,1,0:T(8,128)(2,1)S(1)}, u32[]{:S(2)}, u32[]{:S(2)}) async-start(bf16[4,32,1408]{2,1,0:T(8,128)(2,1)} %bitcast), calls=%async_computation | async-start | bytes 720896 | tf_op jit(solution)/shard_map/all_to_all | solution.py:692
  13.8 12.9 %collective-permute-start.1 = (bf16[64,1024]{1,0:T(8,128)(2,1)S(1)}, bf16[64,1024]{1,0:T(8,128)(2,1)S(1)}, u32[]{:S(2)}, u32[]{:S(2)}) collective-permute-start(bf16[64,1024]{1,0:T(8,128)(2,1)S(1)} %convert_element_type.49), channel_id=1, source_target_pairs={{0,0},{1,4},{2,8},{3,12},{4,16},{5,20},{6,24},{7,28},{8,1},{9,5},{... | collective-permute-start | bytes 393224 | tf_op jit(solution)/shard_map/ppermute | solution.py:742
  27.7 18.8 %all-to-all-start.1 = ((bf16[4,128,896]{2,1,0:T(8,128)(2,1)}), bf16[4,128,896]{2,1,0:T(8,128)(2,1)S(1)}, u32[]{:S(2)}, u32[]{:S(2)}) async-start(bf16[4,128,896]{2,1,0:T(8,128)(2,1)} %broadcast_in_dim.12), calls=%async_computation.1 | async-start | bytes 1835008 | tf_op jit(solution)/shard_map/all_to_all | solution.py:692
  33.7 11.2 %collective-permute-start = (bf16[128,896]{1,0:T(8,128)(2,1)S(1)}, bf16[128,896]{1,0:T(8,128)(2,1)S(1)}, u32[]{:S(2)}, u32[]{:S(2)}) collective-permute-start(bf16[128,896]{1,0:T(8,128)(2,1)S(1)} %slice.213), channel_id=1, source_target_pairs={{0,16},{16,0},{1,17},{17,1},{2,18},{18,2},{3,19},{19,3},{4,20},{20... | collective-permute-start | bytes 688136 | tf_op jit(solution)/shard_map/ppermute | solution.py:665
  47.6 23.1 %all-to-all-start.2 = ((bf16[4,128,896]{2,1,0:T(8,128)(2,1)}), bf16[4,128,896]{2,1,0:T(8,128)(2,1)S(1)}, u32[]{:S(2)}, u32[]{:S(2)}) async-start(bf16[4,128,896]{2,1,0:T(8,128)(2,1)} %broadcast_in_dim.13), calls=%async_computation.2 | async-start | bytes 1835008 | tf_op jit(solution)/shard_map/all_to_all | solution.py:692
  53.7 14.8 %collective-permute-start.2 = (bf16[256,512]{1,0:T(8,128)(2,1)S(1)}, bf16[256,512]{1,0:T(8,128)(2,1)S(1)}, u32[]{:S(2)}, u32[]{:S(2)}) collective-permute-start(bf16[256,512]{1,0:T(8,128)(2,1)S(1)} %pad_maximum_fusion.2), channel_id=1, source_target_pairs={{0,16},{16,0},{1,17},{17,1},{2,18},{18,2},{3,19},{19,3},{4,20},{20... | collective-permute-start | bytes 786440 | tf_op jit(solution)/shard_map/ppermute | solution.py:665
  72.4 29.9 %all-to-all-start.3 = ((bf16[4,512,512]{2,1,0:T(8,128)(2,1)}), bf16[4,512,512]{2,1,0:T(8,128)(2,1)S(1)}, u32[]{:S(2)}, u32[]{:S(2)}) async-start(bf16[4,512,512]{2,1,0:T(8,128)(2,1)} %broadcast_in_dim.14), calls=%async_computation.3 | async-start | bytes 4194304 | tf_op jit(solution)/shard_map/all_to_all | solution.py:692
  78.0 95.2 %reduce-scatter.5.cloned.1.call-start = ((), (), s32[]{:S(2)}) async-start(), calls=%async_computation.13 | async-start | bytes 2621440 | tf_op jit(solution)/shard_map/reduce_scatter | solution.py:669
  140.3 93.2 %reduce-scatter.7.cloned.1.call-start = ((), (), s32[]{:S(2)}) async-start(), calls=%async_computation.14 | async-start | bytes 2621440 | tf_op jit(solution)/shard_map/reduce_scatter | solution.py:669
  140.9 175.6 %reduce-scatter.9.cloned.1.call-start = ((), (), s32[]{:S(2)}) async-start(), calls=%async_computation.15 | async-start | bytes 2621440 | tf_op jit(solution)/shard_map/reduce_scatter | solution.py:669
  169.3 29.3 %all-to-all-start.4 = ((bf16[8,64,1024]{2,1,0:T(8,128)(2,1)}), bf16[8,64,1024]{2,1,0:T(8,128)(2,1)S(1)}, u32[]{:S(2)}, u32[]{:S(2)}) async-start(bf16[8,64,1024]{2,1,0:T(8,128)(2,1)} %bitcast.11), calls=%async_computation.5 | async-start | bytes 2097152 | tf_op jit(solution)/shard_map/all_to_all | solution.py:692
  198.7 34.9 %all-to-all-start.5 = ((bf16[32,32,512]{2,1,0:T(8,128)(2,1)}), bf16[32,32,512]{2,1,0:T(8,128)(2,1)S(1)}, u32[]{:S(2)}, u32[]{:S(2)}) async-start(bf16[32,32,512]{2,1,0:T(8,128)(2,1)} %bitcast.14), calls=%async_computation.9 | async-start | bytes 2097152 | tf_op jit(solution)/shard_map/all_to_all | solution.py:692
  202.8 113.7 %reduce-scatter.11.cloned.1.call-start = ((), (), s32[]{:S(2)}) async-start(), calls=%async_computation.16 | async-start | bytes 2621440 | tf_op jit(solution)/shard_map/reduce_scatter | solution.py:669
  233.7 3.6 %collective-permute-start.3 = (f32[48,128]{1,0:T(8,128)S(1)}, f32[48,128]{1,0:T(8,128)S(1)}, u32[]{:S(2)}, u32[]{:S(2)}) collective-permute-start(f32[48,128]{1,0:T(8,128)S(1)} %pad_bitcast_fusion), channel_id=1, source_target_pairs={{0,16},{16,0},{1,17},{17,1},{2,18},{18,2},{3,19},{19,3},{4,20},{20... | collective-permute-start | bytes 73736 | tf_op jit(solution)/shard_map/ppermute | solution.py:665
  237.3 2.7 collective-permute-start.4
  240.0 2.7 collective-permute-start.5
  242.8 5.5 %collective-permute-start.6 = (f32[48,128]{1,0:T(8,128)S(1)}, f32[48,128]{1,0:T(8,128)S(1)}, u32[]{:S(2)}, u32[]{:S(2)}) collective-permute-start(f32[48,128]{1,0:T(8,128)S(1)} %add.129), channel_id=1, source_target_pairs={{0,2},{1,3},{2,0},{3,1},{4,6},{5,7},{6,4},{7,5},{8,10},{9,11},{10,... | collective-permute-start | bytes 73736 | tf_op jit(solution)/shard_map/ppermute | solution.py:665
  243.9 6.7 %collective-permute-start.8 = (f32[48,128]{1,0:T(8,128)S(1)}, f32[48,128]{1,0:T(8,128)S(1)}, u32[]{:S(2)}, u32[]{:S(2)}) collective-permute-start(f32[48,128]{1,0:T(8,128)S(1)} %add.129), channel_id=1, source_target_pairs={{0,1},{1,0},{2,3},{3,2},{4,5},{5,4},{6,7},{7,6},{8,9},{9,8},{10,11... | collective-permute-start | bytes 73736 | tf_op jit(solution)/shard_map/ppermute | solution.py:665
  248.3 3.2 collective-permute-start.7
  251.7 59.8 %copy-start.19 = (f32[64,1024]{1,0:T(8,128)S(1)}, f32[64,1024]{1,0:T(8,128)}, u32[]{:S(2)}) copy-start(f32[64,1024]{1,0:T(8,128)} %param.17) | copy-start | bytes 786436
  251.7 70.3 %all-to-all-start.6 = ((bf16[32,32,896]{2,1,0:T(8,128)(2,1)}), bf16[32,32,896]{2,1,0:T(8,128)(2,1)S(1)}, u32[]{:S(2)}, u32[]{:S(2)}) async-start(bf16[32,32,896]{2,1,0:T(8,128)(2,1)} %bitcast.75), calls=%async_computation.10 | async-start | bytes 3670016 | tf_op jit(solution)/shard_map/all_to_all | solution.py:692
  257.6 53.8 %collective-permute-start.9 = (f32[64,1024]{1,0:T(8,128)S(1)}, f32[64,1024]{1,0:T(8,128)S(1)}, u32[]{:S(2)}, u32[]{:S(2)}) collective-permute-start(f32[64,1024]{1,0:T(8,128)S(1)} %convert_reduce_fusion.2), channel_id=1, source_target_pairs={{0,0},{4,1},{8,2},{12,3},{16,4},{20,5},{24,6},{28,7},{1,8},{5,9},{... | collective-permute-start | bytes 786440 | tf_op jit(solution)/shard_map/ppermute | solution.py:859
  (33 other events, 382.7 us)
Sparse Core Ops, SparseCore 0:
  9.6 36.0 all-gather.5
  47.3 39.2 all-gather.3
  140.4 28.9 reduce-scatter.4
  171.9 31.4 reduce-scatter.6
  205.8 32.9 reduce-scatter.8
  241.3 47.7 reduce-scatter.10

commit v7 on v6

--- a/solution.py
+++ b/solution.py
@@ -322,6 +322,7 @@
     weight_rest_ref,
     after_ref,
     part_ref,
+    before_ref,
     d_normed_ref,
     d_gain_ref,
     grad_ref,
@@ -595,7 +596,7 @@
     )(upstream, weight, gate, mixed, gate_gain, d_out, stats, low)
 
 
-def run_mixer_back(s, saved, fixed, weights, after, part):
+def run_mixer_back(s, saved, fixed, weights, after, part, before):
     rest, mixed, d_mixed, incoming, low, d_gate, tokens = saved
     taps, heads, skip = fixed
     count, length, inner = mixed.shape
@@ -629,9 +630,10 @@
             whole((D, width)),
             left_alone(),
             left_alone(),
+            left_alone(),
         ],
         out_specs=[
-            pl.BlockSpec((1, ROWS, D), lambda b: (0, last - b, 0)),
+            rows(D),
             whole((1, D)),
             whole((D, width)),
             whole((RIM, conv)),
@@ -639,7 +641,7 @@
             whole((1, inner)),
         ],
         out_shape=[
-            shaped((1, length, D), BF16),
+            shaped((count, length, D), BF16),
             shaped((1, D)),
             shaped((D, width), BF16 if s == count - 1 else F32),
             shaped((RIM, conv)),
@@ -656,8 +658,9 @@
         ],
         compiler_params=params(),
         cost_estimate=cost(1),
+        input_output_aliases={15: 0} if s > 0 else {},
         name="mixer_back",
-    )(rest, rest, mixed, d_mixed, incoming, *fixed, low, d_gate, tokens, *weights, after, part)
+    )(rest, rest, mixed, d_mixed, incoming, *fixed, low, d_gate, tokens, *weights, after, part, before)
 
 
 def swapped(value, axis, mask=1):
@@ -823,14 +826,12 @@
     saved = (rest, mixed, d_mixed, incoming, low, d_gate, tokens)
     fixed = (taps, head_rows, skip)
     weights = (weight_gate, weight_rest)
-    after = grad_rest = d_gate
+    after = grad_rest = d_normed = d_gate
     smalls = []
-    normeds = []
     for s in range(count):
         d_normed, d_gain, grad_rest, d_taps, d_heads, d_skip = run_mixer_back(
-            s, saved, fixed, weights, after, grad_rest
+            s, saved, fixed, weights, after, grad_rest, d_normed
         )
-        normeds.append(summed_over_ctx(d_normed))
         branches[s], d_gain = lax.optimization_barrier((branches[s], d_gain))
         if s == 0:
             grad_gate, branches[s], d_gain, after = lax.optimization_barrier(
@@ -854,7 +855,7 @@
     every = by_rank(sum_over(mine, dp)).reshape(n_ctx, -1)
     grad_rest, every = lax.optimization_barrier((grad_rest, every))
     grad_rest = to_all(grad_rest, axes)
-    d_normed = jnp.concatenate(normeds, axis=0).astype(F32)
+    d_normed = summed_over_ctx(d_normed).astype(F32)
     grad_out = jnp.sum(grad_out.astype(F32).reshape(n_dp, -1, D), axis=0)
     grad_out = lax.ppermute(grad_out, axes, [(b, a) for a, b in moves])
     grad_gate = summed(grad_gate)

time: 334 us -> 309 us (0.925)
  waiting for transfers between devices: 121 us -> 95.8 us
    all_to_all x7, waiting for transfers between devices: 33.1 us -> 7.64 us  [to_all(): return lax.all_to_all(value, axes, split_axis=0, concat_axis=0, tiled=True)]
  transfers between devices with their start and end apart: 23 -> 22, of which waited for: 13 -> 12; matrix products, arithmetic and copies ran while one was open for 6% -> 6% of each run, Pallas kernels for 24% -> 26%
where the time goes in v7:
time: 309 us; the launch traced here: 308 us
  Pallas kernels  110 us (36%)
  waiting for transfers between devices  95.8 us (31%)
  starting transfers between devices  56.1 us (18%)
  between operations  14.5 us (5%)
  other arithmetic  12.4 us (4%)
  local copies, waits for them, and re-layouts  12 us (4%)
  blocking collectives  7.02 us (2%)
    pallas_call x2, Pallas kernels, run_mixer_back(): pl.pallas_call(functools.partial(mixer_back_kernel, inner, s == 0), grid=...  58.5 us
    ppermute x1, waiting for transfers between devices, shards(): grad_out = lax.ppermute(grad_out, axes, [(b, a) for a, b in moves])  50.5 us
    all_to_all x7, starting transfers between devices, to_all(): return lax.all_to_all(value, axes, split_axis=0, concat_axis=0, tiled=True)  36.7 us
    ppermute x8, waiting for transfers between devices, swapped(): return lax.ppermute(value, axis, [(a, a ^ mask) for a in range(count)])  28.9 us
    pallas_call x1, Pallas kernels, run_forward(): pl.pallas_call(functools.partial(forward_kernel, inner), grid_spec=pltpu....  22.2 us
    pallas_call x1, Pallas kernels, run_gate_back(): pl.pallas_call(gate_back_kernel, grid=(count, length // TALL), in_specs=[...  18.1 us
    pallas_call x1, Pallas kernels, run_stats(): pl.pallas_call(functools.partial(stats_kernel, joined), grid_spec=pltpu.P...  11.6 us
    ppermute x8, starting transfers between devices, swapped(): return lax.ppermute(value, axis, [(a, a ^ mask) for a in range(count)])  11.4 us
  transfers between devices with their start and end apart: 22, of which 12 were waited for; matrix products, arithmetic and copies ran while one was open for 6% of the time, Pallas kernels for 26%

profile of v7, /device:TPU:5, one launch (start us, length us, event | category | flops | bytes accessed | tf_op | source)
XLA Modules:
  0.0 308.1 jit_solution(13012640527446194589)
XLA Ops:
  9.6 4.1 %all-to-all-start = ((bf16[4,32,1408]{2,1,0:T(8,128)(2,1)}), bf16[4,32,1408]{2,1,0:T(8,128)(2,1)S(1)}, u32[]{:S(2)}, u32[]{:S(2)}) async-start(bf16[4,32,1408]{2,1,0:T(8,128)(2,1)} %bitcast), calls=%async_computation | async-start | bytes 720896 | tf_op jit(solution)/shard_map/all_to_all | solution.py:695
  13.8 4.3 %collective-permute-start.1 = (bf16[64,1024]{1,0:T(8,128)(2,1)S(1)}, bf16[64,1024]{1,0:T(8,128)(2,1)S(1)}, u32[]{:S(2)}, u32[]{:S(2)}) collective-permute-start(bf16[64,1024]{1,0:T(8,128)(2,1)S(1)} %convert_element_type.49), channel_id=1, source_target_pairs={{0,0},{1,4},{2,8},{3,12},{4,16},{5,20},{6,24},{7,28},{8,1},{9,5},{... | collective-permute-start | bytes 393224 | tf_op jit(solution)/shard_map/ppermute | solution.py:745
  20.0 6.7 %collective-permute-done.1 = bf16[64,1024]{1,0:T(8,128)(2,1)S(1)} collective-permute-done((bf16[64,1024]{1,0:T(8,128)(2,1)S(1)}, bf16[64,1024]{1,0:T(8,128)(2,1)S(1)}, u32[]{:S(2)}, u32[]{:S(2)}) %collective-permute-start.1) | collective-permute-done | bytes 131104 | tf_op jit(solution)/shard_map/ppermute | solution.py:745
  27.7 5.8 %all-to-all-start.1 = ((bf16[4,128,896]{2,1,0:T(8,128)(2,1)}), bf16[4,128,896]{2,1,0:T(8,128)(2,1)S(1)}, u32[]{:S(2)}, u32[]{:S(2)}) async-start(bf16[4,128,896]{2,1,0:T(8,128)(2,1)} %broadcast_in_dim.12), calls=%async_computation.1 | async-start | bytes 1835008 | tf_op jit(solution)/shard_map/all_to_all | solution.py:695
  37.1 7.8 %collective-permute-done = bf16[128,896]{1,0:T(8,128)(2,1)S(1)} collective-permute-done((bf16[128,896]{1,0:T(8,128)(2,1)S(1)}, bf16[128,896]{1,0:T(8,128)(2,1)S(1)}, u32[]{:S(2)}, u32[]{:S(2)}) %collective-permute-start) | collective-permute-done | bytes 229408 | tf_op jit(solution)/shard_map/ppermute | solution.py:668
  47.6 6.0 %all-to-all-start.2 = ((bf16[4,128,896]{2,1,0:T(8,128)(2,1)}), bf16[4,128,896]{2,1,0:T(8,128)(2,1)S(1)}, u32[]{:S(2)}, u32[]{:S(2)}) async-start(bf16[4,128,896]{2,1,0:T(8,128)(2,1)} %broadcast_in_dim.13), calls=%async_computation.2 | async-start | bytes 1835008 | tf_op jit(solution)/shard_map/all_to_all | solution.py:695
  53.8 14.7 %collective-permute-done.2 = bf16[256,512]{1,0:T(8,128)(2,1)S(1)} collective-permute-done((bf16[256,512]{1,0:T(8,128)(2,1)S(1)}, bf16[256,512]{1,0:T(8,128)(2,1)S(1)}, u32[]{:S(2)}, u32[]{:S(2)}) %collective-permute-start.2) | collective-permute-done | bytes 262176 | tf_op jit(solution)/shard_map/ppermute | solution.py:668
  72.4 5.6 %all-to-all-start.3 = ((bf16[4,512,512]{2,1,0:T(8,128)(2,1)}), bf16[4,512,512]{2,1,0:T(8,128)(2,1)S(1)}, u32[]{:S(2)}, u32[]{:S(2)}) async-start(bf16[4,512,512]{2,1,0:T(8,128)(2,1)} %broadcast_in_dim.14), calls=%async_computation.3 | async-start | bytes 4194304 | tf_op jit(solution)/shard_map/all_to_all | solution.py:695
  78.0 22.2 %forward_mixer.1 = (bf16[2,1024,1024]{2,1,0:T(8,128)(2,1)}, f32[2,1024,896]{2,1,0:T(8,128)}, f32[2,1024,512]{2,1,0:T(8,128)}, bf16[2,8,128,512]{3,2,1,0:T(8,128)(2,1)}, bf16[1024,896]{1,0:T(8,128)(2,1)}) custom-call(s32[1]{0:T(128)} %bitcast.6.order_ref, bf16[2,1024,1024]{2,1,0:T(8,128)(2,1)} %all-gather.6.cloned.1.call-done.tokens_ref, f32[1,1024]{1,0:T(1,128)} %bitcast.84, ...), custom_call_target="tpu_custom_call" | custom-call | flops 1100000000 | bytes 2000000 | tf_op jit(solution)/shard_map/forward_mixer/pallas_call | solution.py:493
  103.6 11.6 %gate_stats.1 = (bf16[512,1024]{1,0:T(8,128)(2,1)}, bf16[1024,512]{1,0:T(8,128)(2,1)}, f32[2,1024,512]{2,1,0:T(8,128)}, bf16[2,1024,512]{2,1,0:T(8,128)(2,1)}, f32[2,2,1024]{2,1,0:T(2,128)}) custom-call(s32[1]{0:T(128)} %bitcast.6.order_ref, bf16[2,1024,1024]{2,1,0:T(8,128)(2,1)} %all-gather.4.cloned.1.call-done.up_ref, ...), custom_call_target="tpu_custom_call" | custom-call | flops 1100000000 | bytes 2000000 | tf_op jit(solution)/shard_map/gate_stats/pallas_call | solution.py:526
  115.2 7.0 %all-gather = f32[8,2,1024]{2,1,0:T(2,128)} all-gather(f32[2,2,1024]{2,1,0:T(2,128)} %get-tuple-element.79), channel_id=2, replica_groups=mesh['high'=2,'low'=2,'side'=2,'ctx'=4] {'ctx'}, dimensions={0}, use_global_device_ids=true | all-gather | bytes 81920 | tf_op jit(solution)/shard_map/all_gather | solution.py:814
  122.2 18.1 %gate_back.1 = (bf16[1,1024,1024]{2,1,0:T(8,128)(2,1)}, bf16[1,1024,1024]{2,1,0:T(8,128)(2,1)}, bf16[512,1024]{1,0:T(8,128)(2,1)}, bf16[1024,512]{1,0:T(8,128)(2...) custom-call(bf16[2,1024,1024]{2,1,0:T(8,128)(2,1)} %all-gather.4.cloned.1.call-done.up_ref, ...), custom_call_target="tpu_custom_call" | custom-call | flops 1100000000 | bytes 2000000 | tf_op jit(solution)/shard_map/gate_back/pallas_call | solution.py:563
  140.9 3.8 %all-to-all-start.4 = ((bf16[8,64,1024]{2,1,0:T(8,128)(2,1)}), bf16[8,64,1024]{2,1,0:T(8,128)(2,1)S(1)}, u32[]{:S(2)}, u32[]{:S(2)}) async-start(bf16[8,64,1024]{2,1,0:T(8,128)(2,1)} %bitcast.11), calls=%async_computation.5 | async-start | bytes 2097152 | tf_op jit(solution)/shard_map/all_to_all | solution.py:695
  144.7 28.6 %mixer_back.2 = (bf16[2,1024,1024]{2,1,0:T(8,128)(2,1)}, f32[1,1024]{1,0:T(1,128)}, f32[1024,896]{1,0:T(8,128)}, f32[8,768]{1,0:T(8,128)}, f32[8,128]{1,0:T(8,128)}, /*index=5*/f32[1,512]{1,0:T(1,128)}) custom-call(f32[2,1024,896]{2,1,0:T(8,128)} %get-tuple-element.82.rest_ref.rim_ref, f32[2,1024,896]{2,1,0:T(8,128)} %get-tuple-element.82.rest_ref.rim_ref, ...), custom_call_target="tpu_custom_call" | custom-call | flops 1100000000 | bytes 2000000 | tf_op jit(solution)/shard_map/mixer_back/pallas_call | solution.py:611
  173.3 5.7 %all-to-all-start.5 = ((bf16[32,32,512]{2,1,0:T(8,128)(2,1)}), bf16[32,32,512]{2,1,0:T(8,128)(2,1)S(1)}, u32[]{:S(2)}, u32[]{:S(2)}) async-start(bf16[32,32,512]{2,1,0:T(8,128)(2,1)} %bitcast.14), calls=%async_computation.8 | async-start | bytes 2097152 | tf_op jit(solution)/shard_map/all_to_all | solution.py:695
  179.3 29.9 %mixer_back.3 = (bf16[2,1024,1024]{2,1,0:T(8,128)(2,1)}, f32[1,1024]{1,0:T(1,128)}, bf16[1024,896]{1,0:T(8,128)(2,1)}, f32[8,768]{1,0:T(8,128)}, f32[8,128]{1,0:T(8,128)}, /*index=5*/f32[1,512]{1,0:T(1,128)}) custom-call(f32[2,1024,896]{2,1,0:T(8,128)} %get-tuple-element.82.rest_ref.rim_ref, ...), custom_call_target="tpu_custom_call", output_to_operand_aliasing={{0}: (15, {})} | custom-call | flops 1100000000 | bytes 2000000 | tf_op jit(solution)/shard_map/mixer_back/pallas_call | solution.py:611
  216.8 2.6 collective-permute-done.5
  220.7 4.3 %collective-permute-start.8 = (f32[48,128]{1,0:T(8,128)S(1)}, f32[48,128]{1,0:T(8,128)S(1)}, u32[]{:S(2)}, u32[]{:S(2)}) collective-permute-start(f32[48,128]{1,0:T(8,128)S(1)} %add.127), channel_id=1, source_target_pairs={{0,1},{1,0},{2,3},{3,2},{4,5},{5,4},{6,7},{7,6},{8,9},{9,8},{10,11... | collective-permute-start | bytes 73736 | tf_op jit(solution)/shard_map/ppermute | solution.py:668
  225.0 2.4 collective-permute-start.7
  228.3 5.8 %all-to-all-start.6 = ((bf16[32,32,896]{2,1,0:T(8,128)(2,1)}), bf16[32,32,896]{2,1,0:T(8,128)(2,1)S(1)}, u32[]{:S(2)}, u32[]{:S(2)}) async-start(bf16[32,32,896]{2,1,0:T(8,128)(2,1)} %bitcast.75), calls=%async_computation.9 | async-start | bytes 3670016 | tf_op jit(solution)/shard_map/all_to_all | solution.py:695
  234.3 3.2 %collective-permute-start.9 = (f32[64,1024]{1,0:T(8,128)S(1)}, f32[64,1024]{1,0:T(8,128)S(1)}, u32[]{:S(2)}, u32[]{:S(2)}) collective-permute-start(f32[64,1024]{1,0:T(8,128)S(1)} %convert_reduce_fusion.2), channel_id=1, source_target_pairs={{0,0},{4,1},{8,2},{12,3},{16,4},{20,5},{24,6},{28,7},{1,8},{5,9},{... | collective-permute-start | bytes 786440 | tf_op jit(solution)/shard_map/ppermute | solution.py:860
  237.6 50.5 %collective-permute-done.9 = f32[64,1024]{1,0:T(8,128)S(1)} collective-permute-done((f32[64,1024]{1,0:T(8,128)S(1)}, f32[64,1024]{1,0:T(8,128)S(1)}, u32[]{:S(2)}, u32[]{:S(2)}) %collective-permute-start.9) | collective-permute-done | bytes 262176 | tf_op jit(solution)/shard_map/ppermute | solution.py:860
  293.7 2.9 multiply_subtract_fusion
  298.6 2.3 fusion.7
  (178 shorter events, 37.6 us)
Async XLA Ops:
  7.2 70.8 %all-gather.6.cloned.1.call-start = ((), (), s32[]{:S(2)}) async-start(), calls=%async_computation.11 | async-start | bytes 5242880 | tf_op jit(solution)/shard_map/all_gather | solution.py:766
  7.9 94.3 %all-gather.4.cloned.1.call-start = ((), (), s32[]{:S(2)}) async-start(), calls=%async_computation.10 | async-start | bytes 5242880 | tf_op jit(solution)/shard_map/all_gather | solution.py:767
  9.6 10.3 %all-to-all-start = ((bf16[4,32,1408]{2,1,0:T(8,128)(2,1)}), bf16[4,32,1408]{2,1,0:T(8,128)(2,1)S(1)}, u32[]{:S(2)}, u32[]{:S(2)}) async-start(bf16[4,32,1408]{2,1,0:T(8,128)(2,1)} %bitcast), calls=%async_computation | async-start | bytes 720896 | tf_op jit(solution)/shard_map/all_to_all | solution.py:695
  13.8 12.9 %collective-permute-start.1 = (bf16[64,1024]{1,0:T(8,128)(2,1)S(1)}, bf16[64,1024]{1,0:T(8,128)(2,1)S(1)}, u32[]{:S(2)}, u32[]{:S(2)}) collective-permute-start(bf16[64,1024]{1,0:T(8,128)(2,1)S(1)} %convert_element_type.49), channel_id=1, source_target_pairs={{0,0},{1,4},{2,8},{3,12},{4,16},{5,20},{6,24},{7,28},{8,1},{9,5},{... | collective-permute-start | bytes 393224 | tf_op jit(solution)/shard_map/ppermute | solution.py:745
  27.7 18.8 %all-to-all-start.1 = ((bf16[4,128,896]{2,1,0:T(8,128)(2,1)}), bf16[4,128,896]{2,1,0:T(8,128)(2,1)S(1)}, u32[]{:S(2)}, u32[]{:S(2)}) async-start(bf16[4,128,896]{2,1,0:T(8,128)(2,1)} %broadcast_in_dim.12), calls=%async_computation.1 | async-start | bytes 1835008 | tf_op jit(solution)/shard_map/all_to_all | solution.py:695
  33.7 11.2 %collective-permute-start = (bf16[128,896]{1,0:T(8,128)(2,1)S(1)}, bf16[128,896]{1,0:T(8,128)(2,1)S(1)}, u32[]{:S(2)}, u32[]{:S(2)}) collective-permute-start(bf16[128,896]{1,0:T(8,128)(2,1)S(1)} %slice.213), channel_id=1, source_target_pairs={{0,16},{16,0},{1,17},{17,1},{2,18},{18,2},{3,19},{19,3},{4,20},{20... | collective-permute-start | bytes 688136 | tf_op jit(solution)/shard_map/ppermute | solution.py:668
  47.6 23.1 %all-to-all-start.2 = ((bf16[4,128,896]{2,1,0:T(8,128)(2,1)}), bf16[4,128,896]{2,1,0:T(8,128)(2,1)S(1)}, u32[]{:S(2)}, u32[]{:S(2)}) async-start(bf16[4,128,896]{2,1,0:T(8,128)(2,1)} %broadcast_in_dim.13), calls=%async_computation.2 | async-start | bytes 1835008 | tf_op jit(solution)/shard_map/all_to_all | solution.py:695
  53.7 14.8 %collective-permute-start.2 = (bf16[256,512]{1,0:T(8,128)(2,1)S(1)}, bf16[256,512]{1,0:T(8,128)(2,1)S(1)}, u32[]{:S(2)}, u32[]{:S(2)}) collective-permute-start(bf16[256,512]{1,0:T(8,128)(2,1)S(1)} %pad_maximum_fusion.1), channel_id=1, source_target_pairs={{0,16},{16,0},{1,17},{17,1},{2,18},{18,2},{3,19},{19,3},{4,20},{20... | collective-permute-start | bytes 786440 | tf_op jit(solution)/shard_map/ppermute | solution.py:668
  72.4 29.9 %all-to-all-start.3 = ((bf16[4,512,512]{2,1,0:T(8,128)(2,1)}), bf16[4,512,512]{2,1,0:T(8,128)(2,1)S(1)}, u32[]{:S(2)}, u32[]{:S(2)}) async-start(bf16[4,512,512]{2,1,0:T(8,128)(2,1)} %broadcast_in_dim.14), calls=%async_computation.3 | async-start | bytes 4194304 | tf_op jit(solution)/shard_map/all_to_all | solution.py:695
  78.0 95.3 %reduce-scatter.4.cloned.1.call-start = ((), (), s32[]{:S(2)}) async-start(), calls=%async_computation.12 | async-start | bytes 2621440 | tf_op jit(solution)/shard_map/reduce_scatter | solution.py:672
  140.3 69.7 %reduce-scatter.6.cloned.1.call-start = ((), (), s32[]{:S(2)}) async-start(), calls=%async_computation.13 | async-start | bytes 2621440 | tf_op jit(solution)/shard_map/reduce_scatter | solution.py:672
  140.9 32.4 %all-to-all-start.4 = ((bf16[8,64,1024]{2,1,0:T(8,128)(2,1)}), bf16[8,64,1024]{2,1,0:T(8,128)(2,1)S(1)}, u32[]{:S(2)}, u32[]{:S(2)}) async-start(bf16[8,64,1024]{2,1,0:T(8,128)(2,1)} %bitcast.11), calls=%async_computation.5 | async-start | bytes 2097152 | tf_op jit(solution)/shard_map/all_to_all | solution.py:695
  173.3 37.0 %all-to-all-start.5 = ((bf16[32,32,512]{2,1,0:T(8,128)(2,1)}), bf16[32,32,512]{2,1,0:T(8,128)(2,1)S(1)}, u32[]{:S(2)}, u32[]{:S(2)}) async-start(bf16[32,32,512]{2,1,0:T(8,128)(2,1)} %bitcast.14), calls=%async_computation.8 | async-start | bytes 2097152 | tf_op jit(solution)/shard_map/all_to_all | solution.py:695
  179.0 117.5 %reduce-scatter.8.cloned.1.call-start = ((), (), s32[]{:S(2)}) async-start(), calls=%async_computation.14 | async-start | bytes 5242880 | tf_op jit(solution)/shard_map/reduce_scatter | solution.py:672
  210.5 3.6 %collective-permute-start.3 = (f32[48,128]{1,0:T(8,128)S(1)}, f32[48,128]{1,0:T(8,128)S(1)}, u32[]{:S(2)}, u32[]{:S(2)}) collective-permute-start(f32[48,128]{1,0:T(8,128)S(1)} %pad_bitcast_fusion), channel_id=1, source_target_pairs={{0,16},{16,0},{1,17},{17,1},{2,18},{18,2},{3,19},{19,3},{4,20},{20... | collective-permute-start | bytes 73736 | tf_op jit(solution)/shard_map/ppermute | solution.py:668
  214.1 2.7 collective-permute-start.4
  216.8 2.7 collective-permute-start.5
  219.5 5.5 %collective-permute-start.6 = (f32[48,128]{1,0:T(8,128)S(1)}, f32[48,128]{1,0:T(8,128)S(1)}, u32[]{:S(2)}, u32[]{:S(2)}) collective-permute-start(f32[48,128]{1,0:T(8,128)S(1)} %add.127), channel_id=1, source_target_pairs={{0,2},{1,3},{2,0},{3,1},{4,6},{5,7},{6,4},{7,5},{8,10},{9,11},{10,... | collective-permute-start | bytes 73736 | tf_op jit(solution)/shard_map/ppermute | solution.py:668
  220.7 6.7 %collective-permute-start.8 = (f32[48,128]{1,0:T(8,128)S(1)}, f32[48,128]{1,0:T(8,128)S(1)}, u32[]{:S(2)}, u32[]{:S(2)}) collective-permute-start(f32[48,128]{1,0:T(8,128)S(1)} %add.127), channel_id=1, source_target_pairs={{0,1},{1,0},{2,3},{3,2},{4,5},{5,4},{6,7},{7,6},{8,9},{9,8},{10,11... | collective-permute-start | bytes 73736 | tf_op jit(solution)/shard_map/ppermute | solution.py:668
  225.0 3.2 %collective-permute-start.7 = (f32[48,128]{1,0:T(8,128)S(1)}, f32[48,128]{1,0:T(8,128)S(1)}, u32[]{:S(2)}, u32[]{:S(2)}) collective-permute-start(f32[48,128]{1,0:T(8,128)S(1)} %collective-permute-done.6), channel_id=1, source_target_pairs={{0,1},{1,0},{2,3},{3,2},{4,5},{5,4},{6,7},{7,6},{8,9},{9,8},{10,11... | collective-permute-start | bytes 73736 | tf_op jit(solution)/shard_map/ppermute | solution.py:668
  228.3 59.8 %copy-start.18 = (f32[64,1024]{1,0:T(8,128)S(1)}, f32[64,1024]{1,0:T(8,128)}, u32[]{:S(2)}) copy-start(f32[64,1024]{1,0:T(8,128)} %param.17) | copy-start | bytes 786436
  228.3 63.9 %all-to-all-start.6 = ((bf16[32,32,896]{2,1,0:T(8,128)(2,1)}), bf16[32,32,896]{2,1,0:T(8,128)(2,1)S(1)}, u32[]{:S(2)}, u32[]{:S(2)}) async-start(bf16[32,32,896]{2,1,0:T(8,128)(2,1)} %bitcast.75), calls=%async_computation.9 | async-start | bytes 3670016 | tf_op jit(solution)/shard_map/all_to_all | solution.py:695
  234.3 57.2 %copy-start.20 = (f32[14688]{0:T(1024)S(1)}, f32[14688]{0:T(1024)}, u32[]{:S(2)}) copy-start(f32[14688]{0:T(1024)} %param.19) | copy-start | bytes 176260
  234.3 53.8 %collective-permute-start.9 = (f32[64,1024]{1,0:T(8,128)S(1)}, f32[64,1024]{1,0:T(8,128)S(1)}, u32[]{:S(2)}, u32[]{:S(2)}) collective-permute-start(f32[64,1024]{1,0:T(8,128)S(1)} %convert_reduce_fusion.2), channel_id=1, source_target_pairs={{0,0},{4,1},{8,2},{12,3},{16,4},{20,5},{24,6},{28,7},{1,8},{5,9},{... | collective-permute-start | bytes 786440 | tf_op jit(solution)/shard_map/ppermute | solution.py:860
  (35 other events, 363.7 us)
Sparse Core Ops, SparseCore 0:
  9.6 36.0 all-gather.5
  47.3 39.2 all-gather.3
  140.5 28.8 reduce-scatter.3
  171.9 35.0 reduce-scatter.5
  209.5 65.0 reduce-scatter.7
